TPU v7x, 128 devices: a whole 4x4x4 slice. The times are simulated.
128 devices in a mesh: grp: 4 (over y), tile: 32 (over x, z, core).
Axes of the slice: x: 4, y: 4, z: 4, core: 2. Of those that a mesh axis runs over, the one named last changes fastest.
Arguments:
- flow_fields: float32 [5, 1024, 16, 128], P(None, 'tile', 'grp'), may hold values from -6 to 6
- turbulent_diffusivity: float32 [1024, 16, 128], P('tile', 'grp'), may hold values from 0.05 to 0.3
- holder_unit: int32 [4, 1024, 1], P('grp', 'tile'), may hold values from 0 to 31, as said below
- spray_volume_position: int32 [32, 1024, 128], P('tile'), may hold values from 0 to 511
- patch_pick_unreduced: int32 [32, 1024], P('tile'), may hold values from 0 to 1048575
- droplet_motion: float32 [32, 1024, 3, 128], P('tile'), may hold values from -6 to 6
- droplet_warmth: float32 [32, 1024, 128], P('tile'), may hold values from -6 to 6
- droplet_weightiness: float32 [32, 1024, 128], P('tile'), may hold values from 0.25 to 2
- droplet_multiplicity: float32 [32, 1024, 128], P('tile'), may hold values from 0.5 to 2
- living_spray_batches: int32 [32], P('tile'), may hold values from 1 to 1024, 16384 in all
Outputs:
- gas_next: float32 [5, 1024, 16, 128], P(None, 'tile', 'grp')
Inputs may be any that keep to these rules, and one draw needn't show every extreme that they name: `holder_unit`: among the 32 tiles of one gas device (aligned blocks of 32 rows of owner, in order of its first two dimensions) no parcel device owns more than 2, and in every such block one parcel device owns exactly 2. Two parcel devices own no tile at all. Rows with g = 3 are not used. `living_spray_batches`: live blocks of a device are its first ones; the busiest parcel device has exactly 1024, and they sum to 16384.
All inputs are finite; a program needn't handle non-finite values.
Results may differ from a plain program's by a relative error of at most 0.0045.
Values may be sent and summed in bfloat16 or wider, within the bound.
No kernel may reach another device: no remote copies, remote signals or barrier semaphores. Data moves between devices by JAX's collectives and lax.ppermute only.
A program may use at most 64 MiB of HBM per device.

v0:
```python
import jax
import jax.numpy as jnp
from jax import lax
from jax.sharding import PartitionSpec as P

BLOCK_GROUP = 64


def with_halo(shard, sides, width):
    edges = {}
    for axis, dim in sides:
        count, length = (lax.axis_size(axis), shard.shape[dim])
        up = [(i, (i + 1) % count) for i in range(count - 1)]
        last = lax.slice_in_dim(shard, length - width, length, axis=dim)
        first = lax.slice_in_dim(shard, 0, width, axis=dim)
        edges[dim] = (
            lax.ppermute(last, axis, up),
            lax.ppermute(first, axis, [(b, a) for a, b in up]),
        )
    done = []
    for _, dim in sides:
        low, high = edges[dim]
        around = [(width, width) if d in done else (0, 0) for d in range(shard.ndim)]
        shard = jnp.concatenate([jnp.pad(low, around), shard, jnp.pad(high, around)], axis=dim)
        done.append(dim)
    return shard


def sent_to_all(shard, axis):
    count = lax.axis_size(axis)
    return lax.all_to_all(
        jnp.broadcast_to(shard[None], (count, *shard.shape)), axis, 0, 0, tiled=True
    )


def joined_along(blocks, dim):
    lengths = list(blocks.shape[1:])
    lengths[dim] *= blocks.shape[0]
    return jnp.moveaxis(blocks, 0, dim).reshape(lengths)


def gathered_copies(shard, axis, dim):
    blocks = sent_to_all(shard, axis)
    return joined_along(blocks, dim)


def in_blocks(shard, dim, count):
    lengths = shard.shape
    blocks = shard.reshape(*lengths[:dim], count, lengths[dim] // count, *lengths[dim + 1 :])
    return jnp.moveaxis(blocks, dim, 0)


def summed_on_arrival(shard, axis, dim):
    count = lax.axis_size(axis)
    blocks = lax.all_to_all(in_blocks(shard, dim, count), axis, 0, 0, tiled=True)
    return jnp.sum(blocks, axis=0)


def droplet_coupling_feeds(
    reached_markers, droplet_motion, droplet_warmth, droplet_weightiness, droplet_multiplicity
):
    gas_velocity = reached_markers[..., 0:3, :]
    fluid_warming_share = reached_markers[..., 3, :]
    gas_fuel = reached_markers[..., 4, :]
    relative = gas_velocity - droplet_motion
    speed_sq = jnp.sum(relative * relative, axis=-2)
    surface = droplet_weightiness ** (2.0 / 3.0)
    inverse_tau = 0.8 * (1.0 + 0.15 * (1.0 + speed_sq) ** 0.3435) / surface
    relaxation = 1.0 - jnp.exp(-0.5 * inverse_tau)
    new_velocity = droplet_motion + relaxation[..., None, :] * relative
    heating = 1.0 / (1.0 + jnp.exp(-(fluid_warming_share - gas_fuel)))
    leftover_liquid_load = jnp.exp(-0.3 * heating / surface)
    updated_droplet_load = droplet_weightiness * leftover_liquid_load
    warming_speed = 1.0 - jnp.exp(-0.25 * inverse_tau)
    updated_droplet_warmth = (
        droplet_warmth
        + warming_speed * (fluid_warming_share - droplet_warmth)
        - 0.5 * (1.0 - leftover_liquid_load)
    )
    momentum = (
        droplet_weightiness[..., None, :] * droplet_motion
        - updated_droplet_load[..., None, :] * new_velocity
    )
    enthalpy_content = (
        droplet_weightiness * droplet_warmth - updated_droplet_load * updated_droplet_warmth
    )
    stacked = jnp.concatenate(
        [
            momentum,
            enthalpy_content[..., None, :],
            (droplet_weightiness - updated_droplet_load)[..., None, :],
        ],
        axis=-2,
    )
    return droplet_multiplicity[..., None, :] * stacked


def local(
    flow_fields,
    turbulent_diffusivity,
    holder_unit,
    spray_volume_position,
    patch_pick_unreduced,
    droplet_motion,
    droplet_warmth,
    droplet_weightiness,
    droplet_multiplicity,
    living_spray_batches,
):
    group_count = lax.axis_size("grp")
    owners = lax.axis_size("tile")
    group_index = lax.axis_index("grp")
    gas_side = (group_index < group_count - 1).astype(jnp.float32)
    gas_field = flow_fields * gas_side
    nfield, planes, rows_y, z_cells = gas_field.shape
    tile_cells = rows_y * z_cells
    slot_depth = max(2, 2 * planes // owners)
    padded = with_halo(gas_field.astype(jnp.bfloat16), (("grp", 2), ("tile", 1)), 1).astype(
        gas_field.dtype
    )
    z_padded = jnp.pad(gas_field, ((0, 0), (0, 0), (0, 0), (1, 1)))
    beside = padded[:, 2:, 1:-1, :] + padded[:, :-2, 1:-1, :]
    beside = beside + padded[:, 1:-1, 2:, :] + padded[:, 1:-1, :-2, :]
    beside = beside + z_padded[:, :, :, 2:] + z_padded[:, :, :, :-2]
    laplace = beside - 6.0 * gas_field
    plane_owner = holder_unit[0, :, 0]
    positions = jnp.arange(planes, dtype=jnp.int32)
    same_owner = plane_owner[:, None] == plane_owner[None, :]
    plane_rank = jnp.sum(
        (same_owner & (positions[None, :] < positions[:, None])).astype(jnp.int32), axis=1
    )
    targets = jnp.arange(owners * slot_depth, dtype=jnp.int32)
    selector = (
        (plane_owner[None, :] == targets[:, None] // slot_depth)
        & (plane_rank[None, :] == targets[:, None] % slot_depth)
    ).astype(jnp.float32) * gas_side
    tile_rows = (
        gas_field.astype(jnp.bfloat16).transpose(1, 0, 2, 3).reshape(planes, nfield * tile_cells)
    )
    packed = jnp.dot(selector.astype(jnp.bfloat16), tile_rows, preferred_element_type=jnp.float32)
    packed = packed.astype(jnp.bfloat16).reshape(owners, slot_depth, nfield, tile_cells)
    slot_flags = jnp.sum(selector, axis=1).astype(jnp.int32).reshape(owners, slot_depth)
    lifted_tiles, lifted_flags = (
        gathered_copies(packed[None], "grp", 0),
        gathered_copies(slot_flags[None], "grp", 0),
    )
    arrived, arrived_flags = (
        lax.all_to_all(lifted_tiles, "tile", split_axis=1, concat_axis=1, tiled=True),
        lax.all_to_all(lifted_flags, "tile", split_axis=1, concat_axis=1, tiled=True),
    )
    gas_groups = group_count - 1
    slot_count = gas_groups * owners * slot_depth
    tile_table = arrived[:gas_groups].reshape(slot_count, nfield, tile_cells)
    valid = arrived_flags[:gas_groups].reshape(slot_count)
    owned_count = jnp.sum(valid)
    running = jnp.cumsum(valid)
    picked = patch_pick_unreduced[0] % jnp.maximum(owned_count, 1)
    matches = (valid[None, :] == 1) & (running[None, :] - 1 == picked[:, None])
    block_slot = jnp.sum(
        jnp.where(matches, jnp.arange(slot_count, dtype=jnp.int32)[None, :], 0), axis=1
    )
    live_count = living_spray_batches[0]
    share_size = (
        (live_count + group_count * BLOCK_GROUP - 1) // (group_count * BLOCK_GROUP) * BLOCK_GROUP
    )
    first_block = jnp.minimum(group_index * share_size, live_count)
    end_block = jnp.minimum(first_block + share_size, live_count)
    end_block = jnp.where(owned_count > 0, end_block, first_block)
    group_turns = (end_block - first_block + BLOCK_GROUP - 1) // BLOCK_GROUP
    parcel_cells = spray_volume_position[0]
    parcel_velocity = droplet_motion[0]
    droplet_warming_share = droplet_warmth[0]
    parcel_mass = droplet_weightiness[0]
    parcel_weight = droplet_multiplicity[0]
    cell_ids = jnp.arange(tile_cells, dtype=jnp.int32)

    def advance(step_index, totals):
        start = first_block + step_index * BLOCK_GROUP

        def block_slice(array):
            return lax.dynamic_slice_in_dim(array, start, BLOCK_GROUP, 0)

        block_ids = start + jnp.arange(BLOCK_GROUP, dtype=jnp.int32)
        keep_mask = (block_ids < end_block).astype(jnp.float32)
        slots_here = block_slice(block_slot)
        cells_here = block_slice(parcel_cells)
        tile_values = tile_table[slots_here]
        one_hot = (cells_here[:, :, None] == cell_ids[None, None, :]).astype(jnp.bfloat16)
        reached_markers = jnp.einsum(
            "bfc,bpc->bfp", tile_values, one_hot, preferred_element_type=jnp.float32
        )
        coupling_feeds = droplet_coupling_feeds(
            reached_markers,
            block_slice(parcel_velocity),
            block_slice(droplet_warming_share),
            block_slice(parcel_mass),
            block_slice(parcel_weight),
        )
        coupling_feeds = coupling_feeds * keep_mask[:, None, None]
        upper = coupling_feeds.astype(jnp.bfloat16)
        leftover = coupling_feeds - upper.astype(jnp.float32)
        middle = leftover.astype(jnp.bfloat16)
        lower = (leftover - middle.astype(jnp.float32)).astype(jnp.bfloat16)
        pieces = jnp.concatenate([upper, middle, lower], axis=1)
        deposited = jnp.einsum("bfp,bpc->bfc", pieces, one_hot, preferred_element_type=jnp.float32)
        per_block = (
            deposited[:, :nfield] + deposited[:, nfield : 2 * nfield] + deposited[:, 2 * nfield :]
        )
        return totals.at[slots_here].add(per_block)

    deposit = lax.fori_loop(
        0, group_turns, advance, jnp.zeros((slot_count, nfield, tile_cells), jnp.float32)
    )
    zero_block = jnp.zeros((1, owners, slot_depth, nfield, tile_cells), jnp.float32)
    outgoing = jnp.concatenate(
        [deposit.reshape(gas_groups, owners, slot_depth, nfield, tile_cells), zero_block], axis=0
    )
    spread = lax.all_to_all(outgoing, "tile", split_axis=1, concat_axis=1, tiled=True)
    landed = summed_on_arrival(spread, "grp", 0)
    incoming = landed.reshape(owners * slot_depth, nfield * tile_cells)
    placed = jnp.dot(
        selector.T, incoming, precision=lax.Precision.HIGHEST, preferred_element_type=jnp.float32
    )
    placed = placed.reshape(planes, nfield, rows_y, z_cells).transpose(1, 0, 2, 3)
    return (gas_field + 0.5 * turbulent_diffusivity * laplace + placed) * gas_side


def solution(mesh):
    in_specs = (
        P(None, "tile", "grp", None),
        P("tile", "grp", None),
        P("grp", "tile", None),
        P("tile", None, None),
        P("tile", None),
        P("tile", None, None, None),
        P("tile", None, None),
        P("tile", None, None),
        P("tile", None, None),
        P("tile"),
    )
    out_specs = P(None, "tile", "grp", None)
    return jax.shard_map(local, mesh=mesh, in_specs=in_specs, out_specs=out_specs, check_vma=False)
```

profile of v0, /device:TPU:1, one launch (start us, length us, event | category | flops | bytes accessed | tf_op | source)
XLA Modules:
  0.0 254.5 jit_solution(3277914769872222708)
XLA Ops:
  0.0 0.9 convert_reduce_fusion
  0.9 0.7 select_reduce_fusion.1
  1.9 0.6 broadcast_in_dim.67
  2.5 5.0 %all-to-all-start = ((s32[4,1,32,2]{2,3,1,0:T(2,128)}), s32[4,1,32,2]{2,3,1,0:T(2,128)S(1)}, u32[]{:S(2)}, u32[]{:S(2)}) async-start(s32[4,1,32,2]{2,3,1,0:T(2,128)} %broadcast_in_dim.67), calls=%async_computation | async-start | bytes 8192 | tf_op jit(solution)/shard_map/all_to_all | solution.py:31
  7.5 1.8 fusion.45
  9.4 2.2 all-to-all-done
  11.6 0.7 copy.87
  12.3 10.0 %all-to-all-start.1 = ((s32[4,32,2]{0,2,1:T(2,128)}), s32[4,32,2]{0,2,1:T(2,128)S(1)}, u32[]{:S(2)}, u32[]{:S(2)}) async-start(s32[4,32,2]{0,2,1:T(2,128)} %copy.87), calls=%async_computation.1 | async-start | bytes 65536 | tf_op jit(solution)/shard_map/all_to_all | solution.py:149
  22.4 1.0 convolution_convert_fusion
  23.4 0.4 broadcast_in_dim.70
  24.0 5.6 %all-to-all-done.1 = s32[4,32,2]{0,2,1:T(2,128)S(1)} async-done(((s32[4,32,2]{0,2,1:T(2,128)}), s32[4,32,2]{0,2,1:T(2,128)S(1)}, u32[]{:S(2)}, u32[]{:S(2)}) %all-to-all-start.1) | async-done | bytes 1056 | tf_op jit(solution)/shard_map/all_to_all | solution.py:149
  29.6 1.2 broadcast_in_dim.71
  30.9 3.5 %all-to-all-start.2 = ((bf16[4,1,32,2,5,512]{5,2,4,3,1,0:T(8,128)(2,1)}), bf16[4,1,32,2,5,512]{5,2,4,3,1,0:T(8,128)(2,1)S(1)}, u32[]{:S(2)}, u32[]{:S(2)}) async-start(bf16[4,1,32,2,5,512]{5,2,4,3,1,0:T(8,128)(2,1)} %broadcast_in_dim.71), calls=%async_computation.2 | async-start | bytes 2621440 | tf_op jit(solution)/shard_map/all_to_all | solution.py:31
  35.1 2.4 copy.115
  37.6 0.7 fusion.49
  39.1 12.9 %all-to-all-done.2 = bf16[4,1,32,2,5,512]{5,2,4,3,1,0:T(8,128)(2,1)S(1)} async-done(((bf16[4,1,32,2,5,512]{5,2,4,3,1,0:T(8,128)(2,1)}), bf16[4,1,32,2,5,512]{5,2,4,3,1,0:T(8,128)(2,1)S(1)}, u32[]{:S(2)}, u32[]{:S(2)}) %all-to-all-start.2) | async-done | bytes 1310752 | tf_op jit(solution)/shard_map/all_to_all | solution.py:31
  52.0 2.1 copy.92
  54.1 4.8 %all-to-all-start.3 = ((bf16[4,32,2,5,512]{4,0,3,2,1:T(4,128)(2,1)}), bf16[4,32,2,5,512]{4,0,3,2,1:T(4,128)(2,1)S(1)}, u32[]{:S(2)}, u32[]{:S(2)}) async-start(bf16[4,32,2,5,512]{4,0,3,2,1:T(4,128)(2,1)} %copy.92), calls=%async_computation.3 | async-start | bytes 2621440 | tf_op jit(solution)/shard_map/all_to_all | solution.py:148
  60.9 17.9 %all-to-all-done.3 = bf16[4,32,2,5,512]{4,0,3,2,1:T(4,128)(2,1)S(1)} async-done(((bf16[4,32,2,5,512]{4,0,3,2,1:T(4,128)(2,1)}), bf16[4,32,2,5,512]{4,0,3,2,1:T(4,128)(2,1)S(1)}, u32[]{:S(2)}, u32[]{:S(2)}) %all-to-all-start.3) | async-done | bytes 1310752 | tf_op jit(solution)/shard_map/all_to_all | solution.py:148
  78.8 0.4 copy.102
  79.2 2.1 broadcast_in_dim.66
  81.3 22.2 %while.14 = (s32[]{:T(128)}, f32[192,5,512]{2,1,0:T(8,128)}, s32[]{:T(128)}, s32[]{:T(128)}, s32[1024]{0:T(1024)S(1)}, /*index=5*/f32[1024,128]{1,0:T(8,128)}, f...) while((s32[]{:T(128)}, f32[192,5,512]{2,1,0:T(8,128)}, ...), condition=%wide.region_9.10_spmd.clone, body=%wide.region_6.9_spmd.clone.sunk | while | flops 178324864 | bytes 9770991 | solution.py:211
  81.4 0.6 gather_fusion
  82.0 0.8 constant_dynamic-slice_fusion.5
  82.8 4.3 %fusion.61 = f32[64,5,128]{2,1,0:T(8,128)S(1)} fusion(bf16[64,5,512]{2,1,0:T(8,128)(2,1)S(1)} %gather_fusion, s32[64,128]{1,0:T(8,128)S(1)} %constant_dynamic-slice_fusion.5), kind=kOutput, calls=%fused_computation.5.clone.1 | convolution fusion | flops 46137344 | bytes 524288 | tf_op jit(solution)/shard_map/while/body/bfc,bpc->bfp/dot_general | solution.py:189
  87.2 0.8 fusion.63
  88.0 1.0 multiply_reduce_fusion.2
  89.0 0.9 multiply_subtract_fusion.4
  89.9 1.0 multiply_subtract_fusion.5
  91.1 4.1 %fusion.65 = f32[64,15,512]{2,1,0:T(8,128)S(1)} fusion(s32[64,128]{1,0:T(8,128)S(1)} %constant_dynamic-slice_fusion.5, bf16[64,5,128]{2,1,0:T(8,128)(2,1)S(1)} %get-tuple-element.404, bf16[64,5,128]{2,1,0:T(8,128)(2,1)S(1)} %get-tuple-element.405, bf16[64,5,128]{2,1,0:T(8,128)(2,1)S(1)} %get-tuple-element.406), kind=kOutput, calls=%fused_computation.4.clone.1 | convolution fusion | flops 130760704 | bytes 2244608 | tf_op jit(solution)/shard_map/while/body/bfp,bpc->bfc/dot_general | solution.py:205
  95.5 8.0 %scatter_fusion = f32[192,5,512]{2,1,0:T(8,128)} fusion(f32[192,5,512]{2,1,0:T(8,128)} %get-tuple-element.424, s32[64]{0:T(128)S(1)} %compare_select_fusion.2, f32[64,5,512]{2,1,0:T(8,128)S(1)} %slice_add_fusion.7), kind=kCustom, calls=%fused_computation.1.clone.clone.1 | custom fusion | flops 163840 | bytes 1966336 | tf_op jit(solution)/shard_map/while/body/scatter-add | solution.py:209
  103.5 3.7 %copy.107 = f32[3,32,2,5,512]{4,0,3,2,1:T(4,128)S(1)} copy(f32[3,32,2,5,512]{4,3,2,1,0:T(8,128)} %bitcast.64) | data formatting | bytes 3932160
  107.2 0.5 concatenate.25.clone
  107.7 104.3 %all_to_all.30 = f32[4,32,2,5,512]{4,0,3,2,1:T(4,128)S(1)} all-to-all(f32[4,32,2,5,512]{4,0,3,2,1:T(4,128)S(1)} %concatenate.25.clone), channel_id=1, replica_groups=mesh['grp'=4,'tile'=32] {'tile'}, dimensions={1} | all-to-all | bytes 5242880 | tf_op jit(solution)/shard_map/all_to_all | solution.py:218
  212.0 3.0 %copy.97 = f32[4,1,32,2,5,512]{5,2,4,3,1,0:T(8,128)} copy(f32[4,1,32,2,5,512]{5,0,4,3,2,1:T(4,128)S(1)} %bitcast.66) | data formatting | bytes 5242880 | tf_op jit(solution)/shard_map/reshape | solution.py:49
  215.1 3.8 %all-to-all-start.5 = ((f32[4,1,32,2,5,512]{5,2,4,3,1,0:T(8,128)}), f32[4,1,32,2,5,512]{5,2,4,3,1,0:T(8,128)S(1)}, u32[]{:S(2)}, u32[]{:S(2)}) async-start(f32[4,1,32,2,5,512]{5,2,4,3,1,0:T(8,128)} %copy.97), calls=%async_computation.5 | async-start | bytes 5242880 | tf_op jit(solution)/shard_map/all_to_all | solution.py:55
  218.9 3.3 %collective-permute-start.1 = (bf16[5,32,1,128]{3,1,2,0:T(8,128)(2,1)S(1)}, bf16[5,32,1,128]{3,1,2,0:T(8,128)(2,1)S(1)}, u32[]{:S(2)}, u32[]{:S(2)}) collective-permute-start(bf16[5,32,1,128]{3,1,2,0:T(8,128)(2,1)S(1)} %get-tuple-element.303), channel_id=1, source_target_pairs={{0,32},{32,64},{64,96},{1,33},{33,65},{65,97},{2,34},{34,66},{66,9... | collective-permute-start | bytes 122888 | tf_op jit(solution)/shard_map/ppermute | solution.py:17
  222.2 1.3 collective-permute-start.2
  223.5 2.6 %collective-permute-start = (bf16[5,1,4,128]{3,1,2,0:T(2,128)(2,1)S(1)}, bf16[5,1,4,128]{3,1,2,0:T(2,128)(2,1)S(1)}, u32[]{:S(2)}, u32[]{:S(2)}) collective-permute-start(bf16[5,1,4,128]{3,1,2,0:T(2,128)(2,1)S(1)} %get-tuple-element.305), channel_id=1, source_target_pairs={{0,1},{1,2},{2,3},{3,4},{4,5},{5,6},{6,7},{7,8},{8,9},{9,10},{10,1... | collective-permute-start | bytes 15368 | tf_op jit(solution)/shard_map/ppermute | solution.py:17
  226.1 1.9 collective-permute-start.3
  228.1 3.3 %collective-permute-done.3 = bf16[5,1,4,128]{3,1,2,0:T(2,128)(2,1)S(1)} collective-permute-done((bf16[5,1,4,128]{3,1,2,0:T(2,128)(2,1)S(1)}, bf16[5,1,4,128]{3,1,2,0:T(2,128)(2,1)S(1)}, u32[]{:S(2)}, u32[]{:S(2)}) %collective-permute-start.3) | collective-permute-done | bytes 5152 | tf_op jit(solution)/shard_map/ppermute | solution.py:18
  231.4 17.1 %collective-permute-done.1 = bf16[5,32,1,128]{3,1,2,0:T(8,128)(2,1)S(1)} collective-permute-done((bf16[5,32,1,128]{3,1,2,0:T(8,128)(2,1)S(1)}, bf16[5,32,1,128]{3,1,2,0:T(8,128)(2,1)S(1)}, u32[]{:S(2)}, u32[]{:S(2)}) %collective-permute-start.1) | collective-permute-done | bytes 40992 | tf_op jit(solution)/shard_map/ppermute | solution.py:17
  248.6 1.9 collective-permute-done.2
  250.5 1.0 fusion.28
  251.8 0.4 copy.98
  252.2 0.4 copy.109
  252.9 0.6 fusion.18
  253.6 0.9 copy.100
  (46 shorter events, 3.5 us)
Async XLA Ops:
  2.5 9.2 %all-to-all-start = ((s32[4,1,32,2]{2,3,1,0:T(2,128)}), s32[4,1,32,2]{2,3,1,0:T(2,128)S(1)}, u32[]{:S(2)}, u32[]{:S(2)}) async-start(s32[4,1,32,2]{2,3,1,0:T(2,128)} %broadcast_in_dim.67), calls=%async_computation | async-start | bytes 8192 | tf_op jit(solution)/shard_map/all_to_all | solution.py:31
  12.3 17.3 %all-to-all-start.1 = ((s32[4,32,2]{0,2,1:T(2,128)}), s32[4,32,2]{0,2,1:T(2,128)S(1)}, u32[]{:S(2)}, u32[]{:S(2)}) async-start(s32[4,32,2]{0,2,1:T(2,128)} %copy.87), calls=%async_computation.1 | async-start | bytes 65536 | tf_op jit(solution)/shard_map/all_to_all | solution.py:149
  23.8 11.3 %copy-start = (f32[1,1024,3,128]{3,1,2,0:T(8,128)S(1)}, f32[1,1024,3,128]{3,1,2,0:T(8,128)}, u32[]{:S(2)}) copy-start(f32[1,1024,3,128]{3,1,2,0:T(8,128)} %param.17) | copy-start | bytes 4718596
  30.9 21.1 %all-to-all-start.2 = ((bf16[4,1,32,2,5,512]{5,2,4,3,1,0:T(8,128)(2,1)}), bf16[4,1,32,2,5,512]{5,2,4,3,1,0:T(8,128)(2,1)S(1)}, u32[]{:S(2)}, u32[]{:S(2)}) async-start(bf16[4,1,32,2,5,512]{5,2,4,3,1,0:T(8,128)(2,1)} %broadcast_in_dim.71), calls=%async_computation.2 | async-start | bytes 2621440 | tf_op jit(solution)/shard_map/all_to_all | solution.py:31
  52.0 8.3 %copy-start.4 = (s32[1,1024]{1,0:T(1,128)S(1)}, s32[1,1024]{1,0:T(1,128)}, u32[]{:S(2)}) copy-start(s32[1,1024]{1,0:T(1,128)} %param.16) | copy-start | bytes 12292
  54.1 24.7 %all-to-all-start.3 = ((bf16[4,32,2,5,512]{4,0,3,2,1:T(4,128)(2,1)}), bf16[4,32,2,5,512]{4,0,3,2,1:T(4,128)(2,1)S(1)}, u32[]{:S(2)}, u32[]{:S(2)}) async-start(bf16[4,32,2,5,512]{4,0,3,2,1:T(4,128)(2,1)} %copy.92), calls=%async_computation.3 | async-start | bytes 2621440 | tf_op jit(solution)/shard_map/all_to_all | solution.py:148
  215.1 13.0 %copy-start.3 = (f32[32,4,128]{2,1,0:T(4,128)S(1)}, f32[32,4,128]{2,1,0:T(4,128)}, u32[]{:S(2)}) copy-start(f32[32,4,128]{2,1,0:T(4,128)} %param.13) | copy-start | bytes 196612
  215.1 36.4 %all-to-all-start.5 = ((f32[4,1,32,2,5,512]{5,2,4,3,1,0:T(8,128)}), f32[4,1,32,2,5,512]{5,2,4,3,1,0:T(8,128)S(1)}, u32[]{:S(2)}, u32[]{:S(2)}) async-start(f32[4,1,32,2,5,512]{5,2,4,3,1,0:T(8,128)} %copy.97), calls=%async_computation.5 | async-start | bytes 5242880 | tf_op jit(solution)/shard_map/all_to_all | solution.py:55
  218.9 29.7 %collective-permute-start.1 = (bf16[5,32,1,128]{3,1,2,0:T(8,128)(2,1)S(1)}, bf16[5,32,1,128]{3,1,2,0:T(8,128)(2,1)S(1)}, u32[]{:S(2)}, u32[]{:S(2)}) collective-permute-start(bf16[5,32,1,128]{3,1,2,0:T(8,128)(2,1)S(1)} %get-tuple-element.303), channel_id=1, source_target_pairs={{0,32},{32,64},{64,96},{1,33},{33,65},{65,97},{2,34},{34,66},{66,9... | collective-permute-start | bytes 122888 | tf_op jit(solution)/shard_map/ppermute | solution.py:17
  222.2 28.3 %collective-permute-start.2 = (bf16[5,32,1,128]{3,1,2,0:T(8,128)(2,1)S(1)}, bf16[5,32,1,128]{3,1,2,0:T(8,128)(2,1)S(1)}, u32[]{:S(2)}, u32[]{:S(2)}) collective-permute-start(bf16[5,32,1,128]{3,1,2,0:T(8,128)(2,1)S(1)} %get-tuple-element.304), channel_id=1, source_target_pairs={{32,0},{64,32},{96,64},{33,1},{65,33},{97,65},{34,2},{66,34},{98,6... | collective-permute-start | bytes 122888 | tf_op jit(solution)/shard_map/ppermute | solution.py:18
  223.5 4.6 %collective-permute-start = (bf16[5,1,4,128]{3,1,2,0:T(2,128)(2,1)S(1)}, bf16[5,1,4,128]{3,1,2,0:T(2,128)(2,1)S(1)}, u32[]{:S(2)}, u32[]{:S(2)}) collective-permute-start(bf16[5,1,4,128]{3,1,2,0:T(2,128)(2,1)S(1)} %get-tuple-element.305), channel_id=1, source_target_pairs={{0,1},{1,2},{2,3},{3,4},{4,5},{5,6},{6,7},{7,8},{8,9},{9,10},{10,1... | collective-permute-start | bytes 15368 | tf_op jit(solution)/shard_map/ppermute | solution.py:17
  226.1 5.3 %collective-permute-start.3 = (bf16[5,1,4,128]{3,1,2,0:T(2,128)(2,1)S(1)}, bf16[5,1,4,128]{3,1,2,0:T(2,128)(2,1)S(1)}, u32[]{:S(2)}, u32[]{:S(2)}) collective-permute-start(bf16[5,1,4,128]{3,1,2,0:T(2,128)(2,1)S(1)} %get-tuple-element.306), channel_id=1, source_target_pairs={{1,0},{2,1},{3,2},{4,3},{5,4},{6,5},{7,6},{8,7},{9,8},{10,9},{11,1... | collective-permute-start | bytes 15368 | tf_op jit(solution)/shard_map/ppermute | solution.py:18
  251.8 1.1 copy-start.1
  251.8 1.1 copy-start.2
  251.8 1.1 copy-start.5
where the time goes:
time: 257 us; the launch traced here: 254 us
  blocking collectives  104 us (40%)
  waiting for transfers between devices  61 us (24%)
  starting transfers between devices  36.3 us (14%)
  local copies, waits for them, and re-layouts  21.9 us (9%)
  other arithmetic  18.7 us (7%)
  matrix products  10 us (4%)
    all_to_all x1, blocking collectives, local(): lax.all_to_all(outgoing, 'tile', split_axis=1, concat_axis=1, tiled=True)  104 us
    all_to_all x1, waiting for transfers between devices, local(): lax.all_to_all(lifted_tiles, 'tile', split_axis=1, concat_axis=1, tiled=T...  17.9 us
    ppermute x2, waiting for transfers between devices, with_halo(): lax.ppermute(last, axis, up)  17.2 us
    all_to_all x2, waiting for transfers between devices, sent_to_all(): lax.all_to_all(jnp.broadcast_to(shard[None], (count, *shard.shape)), axis...  15.1 us
    all_to_all x1, starting transfers between devices, local(): lax.all_to_all(lifted_flags, 'tile', split_axis=1, concat_axis=1, tiled=T...  10 us
    all_to_all x2, starting transfers between devices, sent_to_all(): lax.all_to_all(jnp.broadcast_to(shard[None], (count, *shard.shape)), axis...  8.55 us
    scatter-add x1, other arithmetic, advance(): return totals.at[slots_here].add(per_block)  8.03 us
    unnamed x16, local copies, waits for them, and re-layouts  7.06 us
  transfers between devices with their start and end apart: 9, of which 7 were waited for; matrix products, arithmetic and copies ran while one was open for 4% of the time, Pallas kernels for 0%

commit v1 on v0

v1 whole, which is shorter than its diff:
```python
import jax
import jax.numpy as jnp
from jax import lax
from jax.experimental import pallas as pl
from jax.experimental.pallas import tpu as pltpu
from jax.sharding import PartitionSpec as P

NF = 5
ROWS_Y = 4
LANES = 128
PAIR = 48
HALF = NF * ROWS_Y
VMEM_LIMIT = 48 * 1024 * 1024
NT = (((1,), (1,)), ((), ()))


def pack_kernel(planes, owners, holder_ref, near_refs, flow_ref, out_ref, plane_of, count):
    g = lax.axis_index("grp")
    groups = lax.axis_size("grp")

    def clear(p, carry):
        count[p] = 0
        plane_of[2 * p] = 0
        plane_of[2 * p + 1] = 0
        return carry

    lax.fori_loop(0, owners, clear, 0, unroll=True)

    def place(x, carry):
        owner = holder_ref[x]
        rank = count[owner]
        plane_of[2 * owner + jnp.minimum(rank, 1)] = x
        count[owner] = rank + 1
        return carry

    lax.fori_loop(0, planes, place, 0, unroll=True)

    owner_ids = lax.broadcasted_iota(jnp.int32, (owners, planes), 0)
    own = jnp.zeros((owners, 1), jnp.float32)
    before = jnp.zeros((owners, 1), jnp.float32)
    total = jnp.zeros((owners, 1), jnp.float32)
    for k, ref in enumerate(near_refs):
        group = (g - k + groups) % groups
        hits = jnp.where(owner_ids == ref[...], 1.0, 0.0)
        tally = jnp.sum(hits, axis=1, keepdims=True)
        tally = jnp.where(group < groups - 1, tally, 0.0)
        total = total + tally
        before = before + jnp.where(group < g, tally, 0.0)
        if k == 0:
            own = tally
    own, before, total = (jnp.broadcast_to(v, (owners, LANES)) for v in (own, before, total))
    row = lax.broadcasted_iota(jnp.int32, (8, LANES), 0)
    for p in range(owners):
        flags = jnp.where(
            row == 0,
            own[p : p + 1],
            jnp.where(row == 1, before[p : p + 1], jnp.where(row == 2, total[p : p + 1], 0.0)),
        )
        pieces = []
        for s in range(2):
            x = plane_of[2 * p + s]
            pieces += [flow_ref[f, x] for f in range(NF)]
        out_ref[p] = jnp.concatenate(pieces + [flags], axis=0).astype(jnp.bfloat16)


def slot_relayout():
    r = lax.broadcasted_iota(jnp.int32, (64, PAIR), 0)
    c = lax.broadcasted_iota(jnp.int32, (64, PAIR), 1)
    f = r & 7
    want = (r >> 5) * HALF + f * ROWS_Y + ((r >> 3) & 3)
    return jnp.where((f < NF) & (c == want), 1.0, 0.0).astype(jnp.bfloat16)


def slot_relayout_back():
    r = lax.broadcasted_iota(jnp.int32, (PAIR, 64), 0)
    c = lax.broadcasted_iota(jnp.int32, (PAIR, 64), 1)
    f = c & 7
    want = (c >> 5) * HALF + f * ROWS_Y + ((c >> 3) & 3)
    return jnp.where((f < NF) & (r == want), 1.0, 0.0).astype(jnp.bfloat16)


def coupling(gas, motion, warmth, mass, weight):
    relative = [gas[k] - motion[k] for k in range(3)]
    speed_sq = relative[0] * relative[0] + relative[1] * relative[1] + relative[2] * relative[2]
    inv_surface = jnp.exp((-2.0 / 3.0) * jnp.log(mass))
    drag = 0.8 * (1.0 + 0.15 * jnp.exp(0.3435 * jnp.log(1.0 + speed_sq)))
    inverse_tau = drag * inv_surface
    relaxation = 1.0 - jnp.exp(-0.5 * inverse_tau)
    heating = 1.0 / (1.0 + jnp.exp(gas[4] - gas[3]))
    remain = jnp.exp(-0.3 * heating * inv_surface)
    new_mass = mass * remain
    warming = 1.0 - jnp.exp(-0.25 * inverse_tau)
    new_warmth = warmth + warming * (gas[3] - warmth) - 0.5 * (1.0 - remain)
    out = []
    for k in range(3):
        new_velocity = motion[k] + relaxation * relative[k]
        out.append(weight * (mass * motion[k] - new_mass * new_velocity))
    out.append(weight * (mass * warmth - new_mass * new_warmth))
    out.append(weight * (mass - new_mass))
    return out


def couple_kernel(
    owners,
    blocks,
    live_ref,
    pick_ref,
    recv_ref,
    cell_hbm,
    motion_hbm,
    warmth_hbm,
    mass_hbm,
    weight_hbm,
    out_ref,
    cell,
    motion,
    warmth,
    mass,
    weight,
    table,
    deposit,
    code_v,
    code_s,
    work,
    seen,
    gathered,
    source,
    sems,
):
    slots = 2 * owners
    copies = [
        pltpu.make_async_copy(a, b, sems.at[i])
        for i, (a, b) in enumerate(
            (
                (cell_hbm, cell),
                (motion_hbm, motion),
                (warmth_hbm, warmth),
                (mass_hbm, mass),
                (weight_hbm, weight),
            )
        )
    ]
    for copy in copies:
        copy.start()

    before = jnp.zeros((8, LANES), jnp.float32)
    total = jnp.zeros((8, LANES), jnp.float32)
    counts = []
    for t in range(owners):
        flags = recv_ref[t, 32:48].astype(jnp.float32)
        counts.append(jnp.broadcast_to(flags[8:9], (8, LANES)))
        before = before + jnp.broadcast_to(flags[9:10], (8, LANES))
        total = total + jnp.broadcast_to(flags[10:11], (8, LANES))
    divisor = jnp.maximum(total, 1.0)
    pick = pick_ref[...].astype(jnp.float32)
    quotient = (pick / divisor).astype(jnp.int32)
    divisor_int = divisor.astype(jnp.int32)
    picked = pick_ref[...] - quotient * divisor_int
    picked = jnp.where(picked < 0, picked + divisor_int, picked)
    picked = jnp.where(picked >= divisor_int, picked - divisor_int, picked)
    place = picked.astype(jnp.float32) - before
    running = jnp.zeros((8, LANES), jnp.float32)
    passed = jnp.zeros((8, LANES), jnp.float32)
    slot = jnp.zeros((8, LANES), jnp.float32)
    for t in range(owners):
        running = running + counts[t]
        beyond = running <= place
        slot = jnp.where(beyond, slot + 2.0, slot)
        passed = jnp.where(beyond, running, passed)
    slot = (slot + (place - passed)).astype(jnp.int32)
    block = (
        lax.broadcasted_iota(jnp.int32, (8, LANES), 0) * LANES
        + lax.broadcasted_iota(jnp.int32, (8, LANES), 1)
    )
    mine = (place >= 0.0) & (place < running) & (block < live_ref[0])
    code_v[...] = jnp.where(mine, slot * blocks + block, -1)
    to_scalar = pltpu.make_async_copy(code_v, code_s, sems.at[5])
    to_scalar.start()

    spread = slot_relayout()
    for t in range(owners):
        rows = jnp.dot(spread, recv_ref[t], preferred_element_type=jnp.float32)
        table[8 * t : 8 * t + 8] = rows.reshape(8, 8, LANES)
    table[4 * slots : 4 * slots + 4] = jnp.zeros((4, 8, LANES), jnp.float32)

    def clear(t, carry):
        deposit[pl.ds(8 * t, 8)] = jnp.zeros((8, 8, LANES), jnp.float32)
        return carry

    lax.fori_loop(0, owners, clear, 0)
    deposit[4 * slots : 4 * slots + 4] = jnp.zeros((4, 8, LANES), jnp.float32)
    source[...] = jnp.zeros_like(source)
    to_scalar.wait()

    def collect(j, n):
        for i in range(8):
            code = code_s[j >> 4, (j & 15) * 8 + i]
            work[n] = code
            n = n + jnp.where(code >= 0, 1, 0)
        return n

    found = lax.fori_loop(0, (live_ref[0] + 7) // 8, collect, 0)
    for i in range(8):
        work[found + i] = slots * blocks
    for copy in copies:
        copy.wait()

    cell_row = lax.broadcasted_iota(jnp.int32, (LANES, LANES), 0)

    def advance(j, carry):
        where_to = []
        for i in range(8):
            code = work[8 * j + i]
            b = code & (blocks - 1)
            slot = code >> (blocks.bit_length() - 1)
            cells = cell[pl.ds(b, 1), :]
            where_to.append((slot, cells))
            around = jnp.broadcast_to(cells, (8, LANES))
            z, y = around & (LANES - 1), around >> 7
            rows = [
                jnp.take_along_axis(table[4 * slot + k], z, axis=1) for k in range(ROWS_Y)
            ]
            seen[8 * i : 8 * i + 8] = jnp.where(
                y == 0, rows[0], jnp.where(y == 1, rows[1], jnp.where(y == 2, rows[2], rows[3]))
            )
            moving = motion[b]
            for k in range(3):
                gathered[k, i : i + 1, :] = moving[k : k + 1]
            gathered[3, i : i + 1, :] = warmth[pl.ds(b, 1), :]
            gathered[4, i : i + 1, :] = mass[pl.ds(b, 1), :]
            gathered[5, i : i + 1, :] = weight[pl.ds(b, 1), :]
        gas = [seen[pl.ds(f, 8, stride=8), :] for f in range(NF)]
        sources = coupling(
            gas, [gathered[k] for k in range(3)], gathered[3], gathered[4], gathered[5]
        )
        for f in range(NF):
            source[pl.ds(f, 8, stride=8), :] = sources[f]
        for i in range(8):
            slot, cells = where_to[i]
            around = jnp.broadcast_to(cells, (8, LANES))
            y = around >> 7
            part = source[8 * i : 8 * i + 8]
            masked = jnp.concatenate([jnp.where(y == k, part, 0.0) for k in range(ROWS_Y)], axis=0)
            upper = masked.astype(jnp.bfloat16)
            lower = (masked - upper.astype(jnp.float32)).astype(jnp.bfloat16)
            hot = jnp.where(cell_row == (cells & (LANES - 1)), 1.0, 0.0).astype(jnp.bfloat16)
            both = lax.dot_general(
                jnp.concatenate([upper, lower], axis=0), hot, NT, preferred_element_type=jnp.float32
            )
            added = (both[:32] + both[32:]).reshape(4, 8, LANES)
            deposit[pl.ds(4 * slot, 4)] = deposit[pl.ds(4 * slot, 4)] + added
        return carry

    lax.fori_loop(0, (found + 7) // 8, advance, 0)

    back = slot_relayout_back()
    for t in range(owners):
        rows = deposit[8 * t : 8 * t + 8].reshape(64, LANES).astype(jnp.bfloat16)
        out_ref[t] = jnp.dot(back, rows, preferred_element_type=jnp.float32).astype(jnp.bfloat16)


def diffuse_kernel(planes, flow_ref, nu_ref, xlo_ref, xhi_ref, ylo_ref, yhi_ref, out_ref):
    lane = lax.broadcasted_iota(jnp.int32, (ROWS_Y, LANES), 1)
    for f in range(NF):
        for x in range(planes):
            here = flow_ref[f, x]
            left = xlo_ref[f] if x == 0 else flow_ref[f, x - 1]
            right = xhi_ref[f] if x == planes - 1 else flow_ref[f, x + 1]
            lower = jnp.concatenate([ylo_ref[f, x : x + 1], here[: ROWS_Y - 1]], axis=0)
            upper = jnp.concatenate([here[1:], yhi_ref[f, x : x + 1]], axis=0)
            back = jnp.where(lane == 0, 0.0, pltpu.roll(here, 1, 1))
            ahead = jnp.where(lane == LANES - 1, 0.0, pltpu.roll(here, LANES - 1, 1))
            laplace = right + left + upper + lower + ahead + back - 6.0 * here
            out_ref[f, x] = here + 0.5 * nu_ref[x] * laplace


def finish_kernel(planes, owners, holder_ref, adv_ref, recv_ref, out_ref, count):
    g = lax.axis_index("grp")
    keep = g < lax.axis_size("grp") - 1

    def clear(p, carry):
        count[p] = 0
        return carry

    lax.fori_loop(0, owners, clear, 0, unroll=True)
    for x in range(planes):
        owner = holder_ref[x]
        rank = count[owner]
        count[owner] = rank + 1
        pair = recv_ref[owner].astype(jnp.float32)
        landed = jnp.where(rank == 0, pair[:HALF], pair[HALF : 2 * HALF])
        for f in range(NF):
            value = adv_ref[f, x] + landed[ROWS_Y * f : ROWS_Y * f + ROWS_Y]
            out_ref[f, x] = jnp.where(keep, value, 0.0)


def local(
    flow_fields,
    turbulent_diffusivity,
    holder_unit,
    spray_volume_position,
    patch_pick_unreduced,
    droplet_motion,
    droplet_warmth,
    droplet_weightiness,
    droplet_multiplicity,
    living_spray_batches,
):
    groups = lax.axis_size("grp")
    owners = lax.axis_size("tile")
    planes = flow_fields.shape[1]
    blocks = spray_volume_position.shape[1]
    vmem = pl.BlockSpec(memory_space=pltpu.VMEM)
    smem = pl.BlockSpec(memory_space=pltpu.SMEM)
    hbm = pl.BlockSpec(memory_space=pl.ANY)
    params = pltpu.CompilerParams(vmem_limit_bytes=VMEM_LIMIT)

    holder = holder_unit.reshape(planes)
    near = [holder.reshape(1, planes)]
    for k in range(1, groups):
        near.append(lax.ppermute(near[0], "grp", [(i, (i + k) % groups) for i in range(groups)]))

    up_tile = [(i, i + 1) for i in range(owners - 1)]
    up_grp = [(i, i + 1) for i in range(groups - 2)]
    xlo = lax.ppermute(flow_fields[:, planes - 1], "tile", up_tile)
    xhi = lax.ppermute(flow_fields[:, 0], "tile", [(b, a) for a, b in up_tile])
    ylo = lax.ppermute(flow_fields[:, :, ROWS_Y - 1], "grp", up_grp)
    yhi = lax.ppermute(flow_fields[:, :, 0], "grp", [(b, a) for a, b in up_grp])

    def pack_body(holder_ref, n0, n1, n2, n3, flow_ref, out_ref, plane_of, count):
        pack_kernel(
            planes, owners, holder_ref, (n0, n1, n2, n3), flow_ref, out_ref, plane_of, count
        )

    message = jax.ShapeDtypeStruct((owners, PAIR, LANES), jnp.bfloat16)
    packed = pl.pallas_call(
        pack_body,
        out_shape=message,
        in_specs=[smem] + [vmem] * 5,
        out_specs=vmem,
        scratch_shapes=[pltpu.SMEM((2 * owners,), jnp.int32), pltpu.SMEM((owners,), jnp.int32)],
        compiler_params=params,
    )(holder, *near, flow_fields)
    arrived = lax.all_to_all(packed, "tile", 0, 0, tiled=True)

    def couple_body(*refs):
        couple_kernel(owners, blocks, *refs)

    outgoing = pl.pallas_call(
        couple_body,
        out_shape=message,
        in_specs=[smem, vmem, vmem] + [hbm] * 5,
        out_specs=vmem,
        scratch_shapes=[
            pltpu.VMEM((blocks, LANES), jnp.int32),
            pltpu.VMEM((blocks, 3, LANES), jnp.float32),
            pltpu.VMEM((blocks, LANES), jnp.float32),
            pltpu.VMEM((blocks, LANES), jnp.float32),
            pltpu.VMEM((blocks, LANES), jnp.float32),
            pltpu.VMEM((8 * owners + 4, 8, LANES), jnp.float32),
            pltpu.VMEM((8 * owners + 4, 8, LANES), jnp.float32),
            pltpu.VMEM((8, LANES), jnp.int32),
            pltpu.SMEM((8, LANES), jnp.int32),
            pltpu.SMEM((blocks + 16,), jnp.int32),
            pltpu.VMEM((64, LANES), jnp.float32),
            pltpu.VMEM((6, 8, LANES), jnp.float32),
            pltpu.VMEM((64, LANES), jnp.float32),
            pltpu.SemaphoreType.DMA((6,)),
        ],
        compiler_params=params,
    )(
        living_spray_batches,
        patch_pick_unreduced.reshape(8, LANES),
        arrived,
        spray_volume_position[0],
        droplet_motion[0],
        droplet_warmth[0],
        droplet_weightiness[0],
        droplet_multiplicity[0],
    )
    landed = lax.all_to_all(outgoing, "tile", 0, 0, tiled=True)

    def diffuse_body(*refs):
        diffuse_kernel(planes, *refs)

    diffused = pl.pallas_call(
        diffuse_body,
        out_shape=jax.ShapeDtypeStruct(flow_fields.shape, jnp.float32),
        in_specs=[vmem] * 6,
        out_specs=vmem,
        compiler_params=params,
    )(flow_fields, turbulent_diffusivity, xlo, xhi, ylo, yhi)

    def finish_body(*refs):
        finish_kernel(planes, owners, *refs)

    return pl.pallas_call(
        finish_body,
        out_shape=jax.ShapeDtypeStruct(flow_fields.shape, jnp.float32),
        in_specs=[smem, vmem, vmem],
        out_specs=vmem,
        scratch_shapes=[pltpu.SMEM((owners,), jnp.int32)],
        compiler_params=params,
    )(holder, diffused, landed)


def solution(mesh):
    in_specs = (
        P(None, "tile", "grp", None),
        P("tile", "grp", None),
        P("grp", "tile", None),
        P("tile", None, None),
        P("tile", None),
        P("tile", None, None, None),
        P("tile", None, None),
        P("tile", None, None),
        P("tile", None, None),
        P("tile"),
    )
    out_specs = P(None, "tile", "grp", None)
    return jax.shard_map(local, mesh=mesh, in_specs=in_specs, out_specs=out_specs, check_vma=False)
```

time: 257 us -> 81.8 us (0.32)
  blocking collectives: 104 us -> 0 us
  waiting for transfers between devices: 61 us -> 11.7 us
  Pallas kernels: 0 us -> 19.3 us
  other arithmetic: 18.7 us -> 0 us
  local copies, waits for them, and re-layouts: 21.9 us -> 7.39 us
  matrix products: 10 us -> 0 us
  starting transfers between devices: 36.3 us -> 41.9 us
    all_to_all x1 -> x0, blocking collectives: 104 us -> none  [local(): lax.all_to_all(outgoing, 'tile', split_axis=1, concat_axis=1, tiled=True)]
    all_to_all x5 -> x2, waiting for transfers between devices: 38.7 us -> 7.16 us  [the longest x1 7.16 us: local(): arrived = lax.all_to_all(packed, 'tile', 0, 0, tiled=True)]
    pallas_call x0 -> x4, Pallas kernels: none -> 19.3 us  [the longest x1 15.8 us: local(): pl.pallas_call(couple_body, out_shape=message, in_specs=[smem, vmem, vmem...]
    ppermute x4 -> x7, waiting for transfers between devices: 22.4 us -> 4.52 us  [the longest x1 3.05 us: local(): xhi = lax.ppermute(flow_fields[:, 0], 'tile', [(b, a) for a, b in up_tile])]
    dot_general x4 -> x0, matrix products: 10 us -> none  [the longest x1 4.34 us: advance(): jnp.einsum('bfc,bpc->bfp', tile_values, one_hot, preferred_element_type=j...]
    scatter-add x1 -> x0, other arithmetic: 8.03 us -> none  [advance(): return totals.at[slots_here].add(per_block)]
    ppermute x4 -> x7, starting transfers between devices: 9.12 us -> 15.6 us  [the longest x3 5.81 us: local(): lax.ppermute(near[0], 'grp', [(i, (i + k) % groups) for i in range(groups)])]
    reshape x5 -> x0, local copies, waits for them, and re-layouts: 5.91 us -> none  [the longest x1 3.04 us: in_blocks(): shard.reshape(*lengths[:dim], count, lengths[dim] // count, *lengths[dim...]
  transfers between devices with their start and end apart: 9 -> 9, of which waited for: 7 -> 4; matrix products, arithmetic and copies ran while one was open for 4% -> 3% of each run, Pallas kernels for 0% -> 1%
where the time goes in v1:
time: 81.8 us; the launch traced here: 81 us
  starting transfers between devices  41.9 us (51%)
  Pallas kernels  19.3 us (24%)
  waiting for transfers between devices  11.7 us (14%)
  local copies, waits for them, and re-layouts  7.39 us (9%)
    all_to_all x1, starting transfers between devices, local(): landed = lax.all_to_all(outgoing, 'tile', 0, 0, tiled=True)  15.9 us
    pallas_call x1, Pallas kernels, local(): pl.pallas_call(couple_body, out_shape=message, in_specs=[smem, vmem, vmem...  15.8 us
    all_to_all x1, starting transfers between devices, local(): arrived = lax.all_to_all(packed, 'tile', 0, 0, tiled=True)  10.4 us
    unnamed x21, local copies, waits for them, and re-layouts  7.26 us
    all_to_all x1, waiting for transfers between devices, local(): arrived = lax.all_to_all(packed, 'tile', 0, 0, tiled=True)  7.16 us
    ppermute x3, starting transfers between devices, local(): lax.ppermute(near[0], 'grp', [(i, (i + k) % groups) for i in range(groups)])  5.81 us
    ppermute x1, starting transfers between devices, local(): xlo = lax.ppermute(flow_fields[:, planes - 1], 'tile', up_tile)  3.82 us
    ppermute x1, waiting for transfers between devices, local(): xhi = lax.ppermute(flow_fields[:, 0], 'tile', [(b, a) for a, b in up_tile])  3.05 us
  transfers between devices with their start and end apart: 9, of which 4 were waited for; matrix products, arithmetic and copies ran while one was open for 3% of the time, Pallas kernels for 1%

profile of v1, /device:TPU:1, one launch (start us, length us, event | category | flops | bytes accessed | tf_op | source)
XLA Modules:
  0.0 81.0 jit_solution(14644936322590910854)
XLA Ops:
  0.0 2.1 %collective-permute-start.4 = (s32[1,32]{1,0:T(1,128)}, s32[1,32]{1,0:T(1,128)S(1)}, u32[]{:S(2)}, u32[]{:S(2)}) collective-permute-start(s32[1,32]{1,0:T(1,128)} %bitcast.29), channel_id=1, source_target_pairs={{0,32},{32,64},{64,96},{96,0},{1,33},{33,65},{65,97},{97,1},{2,34}... | collective-permute-start | bytes 392 | tf_op jit(solution)/shard_map/ppermute | solution.py:321
  2.1 2.6 %collective-permute-start.5 = (s32[1,32]{1,0:T(1,128)}, s32[1,32]{1,0:T(1,128)S(1)}, u32[]{:S(2)}, u32[]{:S(2)}) collective-permute-start(s32[1,32]{1,0:T(1,128)} %bitcast.30), channel_id=1, source_target_pairs={{0,64},{32,96},{64,0},{96,32},{1,65},{33,97},{65,1},{97,33},{2,66}... | collective-permute-start | bytes 392 | tf_op jit(solution)/shard_map/ppermute | solution.py:321
  4.7 1.1 %collective-permute-start.6 = (s32[1,32]{1,0:T(1,128)}, s32[1,32]{1,0:T(1,128)S(1)}, u32[]{:S(2)}, u32[]{:S(2)}) collective-permute-start(s32[1,32]{1,0:T(1,128)} %bitcast.31), channel_id=1, source_target_pairs={{0,96},{32,0},{64,32},{96,64},{1,97},{33,1},{65,33},{97,65},{2,98}... | collective-permute-start | bytes 392 | tf_op jit(solution)/shard_map/ppermute | solution.py:321
  5.8 0.0 collective-permute-done.4.n1
  5.8 0.3 collective-permute-done.5.n2
  6.2 1.1 %collective-permute-done.6.n3 = s32[1,32]{1,0:T(1,128)S(1)} collective-permute-done((s32[1,32]{1,0:T(1,128)}, s32[1,32]{1,0:T(1,128)S(1)}, u32[]{:S(2)}, u32[]{:S(2)}) %collective-permute-start.6) | collective-permute-done | bytes 160 | tf_op jit(solution)/shard_map/ppermute | solution.py:321
  7.3 0.0 copy-start
  7.3 1.0 %copy-done = f32[5,32,4,128]{3,2,1,0:T(4,128)S(1)} copy-done((f32[5,32,4,128]{3,2,1,0:T(4,128)S(1)}, f32[5,32,4,128]{3,2,1,0:T(4,128)}, u32[]{:S(2)}) %copy-start) | copy-done | bytes 327704
  8.2 0.0 copy-start.7
  8.2 0.7 copy-done.7
  8.9 1.7 %shard_map.101 = bf16[32,48,128]{2,1,0:T(8,128)(2,1)} custom-call(s32[32]{0:T(128)S(1)} %bitcast.32, s32[1,32]{1,0:T(1,128)S(1)} %bitcast.33, s32[1,32]{1,0:T(1,128)S(1)} %collective-permute-done.4.n1, s32[1,32]{1,0:T(1,128)S(1)} %collective-permute-done.5.n2, s32[1,32]{1,0:T(1,128)S(1)} %collective-permute-done.6.n3, f32[5,32,4,128]{3,2,1,0:T(4,128)S(1)} %copy-done), custom_call_target="tpu_custom_call" | custom-call | tf_op jit(solution)/shard_map/pallas_call | solution.py:336
  10.6 0.0 copy-start.2
  10.6 0.0 copy-start.9
  10.6 10.4 %all-to-all-start = ((bf16[32,48,128]{2,1,0:T(8,128)(2,1)}), bf16[32,48,128]{2,1,0:T(8,128)(2,1)S(1)}, u32[]{:S(2)}, u32[]{:S(2)}) async-start(bf16[32,48,128]{2,1,0:T(8,128)(2,1)} %shard_map.101), calls=%async_computation | async-start | bytes 786432 | tf_op jit(solution)/shard_map/all_to_all | solution.py:344
  21.0 2.5 %copy.21 = f32[1,1024,3,128]{3,2,1,0:T(4,128)S(1)} copy(f32[1,1024,3,128]{3,1,2,0:T(8,128)} %param.15) | data formatting | bytes 3145728 | tf_op args[5]
  24.2 7.2 %all-to-all-done.refs_2_ = bf16[32,48,128]{2,1,0:T(8,128)(2,1)S(1)} async-done(((bf16[32,48,128]{2,1,0:T(8,128)(2,1)}), bf16[32,48,128]{2,1,0:T(8,128)(2,1)S(1)}, u32[]{:S(2)}, u32[]{:S(2)}) %all-to-all-start) | async-done | bytes 393248 | tf_op jit(solution)/shard_map/all_to_all | solution.py:344
  31.3 0.0 copy-done.2
  31.3 0.0 copy-done.9
  31.3 0.0 copy-start.3
  31.3 1.0 %copy-done.3 = f32[1,1024,128]{2,1,0:T(8,128)S(1)} copy-done((f32[1,1024,128]{2,1,0:T(8,128)S(1)}, f32[1,1024,128]{2,1,0:T(8,128)}, u32[]{:S(2)}) %copy-start.3) | copy-done | bytes 524312
  32.4 0.0 copy-start.4
  32.4 1.0 %copy-done.4 = f32[1,1024,128]{2,1,0:T(8,128)S(1)} copy-done((f32[1,1024,128]{2,1,0:T(8,128)S(1)}, f32[1,1024,128]{2,1,0:T(8,128)}, u32[]{:S(2)}) %copy-start.4) | copy-done | bytes 524312
  33.4 0.0 copy-start.5
  33.4 1.0 %copy-done.5 = f32[1,1024,128]{2,1,0:T(8,128)S(1)} copy-done((f32[1,1024,128]{2,1,0:T(8,128)S(1)}, f32[1,1024,128]{2,1,0:T(8,128)}, u32[]{:S(2)}) %copy-start.5) | copy-done | bytes 524312
  34.5 0.0 copy-start.1
  34.5 0.0 copy-start.6
  34.5 0.0 copy-start.8
  34.5 15.8 %shard_map.102 = bf16[32,48,128]{2,1,0:T(8,128)(2,1)} custom-call(s32[1]{0:T(128)S(6)} %copy.22.refs_0_, s32[8,128]{1,0:T(8,128)S(1)} %bitcast.35, bf16[32,48,128]{2,1,0:T(8,128)(2,1)S(1)} %all-to-all-done.refs_2_, s32[1024,128]{1,0:T(8,128)S(1)} %bitcast.25, f32[1024,3,128]{2,1,0:T(4,128)S(1)} %bitcast.24, f32[1024,128]{1,0:T(8,128)S(1)} %bitcast.26, ...), custom_call_target="tpu_custom_call" | custom-call | tf_op jit(solution)/shard_map/pallas_call | solution.py:349
  50.2 15.9 %all-to-all-start.1 = ((bf16[32,48,128]{2,1,0:T(8,128)(2,1)}), bf16[32,48,128]{2,1,0:T(8,128)(2,1)S(1)}, u32[]{:S(2)}, u32[]{:S(2)}) async-start(bf16[32,48,128]{2,1,0:T(8,128)(2,1)} %shard_map.102), calls=%async_computation.1 | async-start | bytes 786432 | tf_op jit(solution)/shard_map/all_to_all | solution.py:381
  66.1 0.0 copy-done.1
  66.1 0.1 fusion
  66.2 2.7 %collective-permute-start.2 = (f32[5,32,128]{2,1,0:T(8,128)S(1)}, f32[5,32,128]{2,1,0:T(8,128)S(1)}, u32[]{:S(2)}, u32[]{:S(2)}) collective-permute-start(f32[5,32,128]{2,1,0:T(8,128)S(1)} %bitcast.37), channel_id=1, source_target_pairs={{0,32},{32,64},{1,33},{33,65},{2,34},{34,66},{3,35},{35,67},{4,36}... | collective-permute-start | bytes 245768 | tf_op jit(solution)/shard_map/ppermute | solution.py:327
  69.0 1.3 %collective-permute-start.3 = (f32[5,32,128]{2,1,0:T(8,128)S(1)}, f32[5,32,128]{2,1,0:T(8,128)S(1)}, u32[]{:S(2)}, u32[]{:S(2)}) collective-permute-start(f32[5,32,128]{2,1,0:T(8,128)S(1)} %bitcast.36), channel_id=1, source_target_pairs={{32,0},{64,32},{33,1},{65,33},{34,2},{66,34},{35,3},{67,35},{36,4}... | collective-permute-start | bytes 245768 | tf_op jit(solution)/shard_map/ppermute | solution.py:328
  70.3 3.8 %collective-permute-start = (f32[5,4,128]{2,1,0:T(4,128)S(1)}, f32[5,4,128]{2,1,0:T(4,128)S(1)}, u32[]{:S(2)}, u32[]{:S(2)}) collective-permute-start(f32[5,4,128]{2,1,0:T(4,128)S(1)} %get-tuple-element.8), channel_id=1, source_target_pairs={{0,1},{1,2},{2,3},{3,4},{4,5},{5,6},{6,7},{7,8},{8,9},{9,10},{10,1... | collective-permute-start | bytes 30728 | tf_op jit(solution)/shard_map/ppermute | solution.py:325
  74.1 1.9 %collective-permute-start.1 = (f32[5,4,128]{2,1,0:T(4,128)S(1)}, f32[5,4,128]{2,1,0:T(4,128)S(1)}, u32[]{:S(2)}, u32[]{:S(2)}) collective-permute-start(f32[5,4,128]{2,1,0:T(4,128)S(1)} %get-tuple-element.7), channel_id=1, source_target_pairs={{1,0},{2,1},{3,2},{4,3},{5,4},{6,5},{7,6},{8,7},{9,8},{10,9},{11,1... | collective-permute-start | bytes 30728 | tf_op jit(solution)/shard_map/ppermute | solution.py:326
  76.0 0.0 collective-permute-done.refs_2_
  76.0 3.1 %collective-permute-done.1.refs_3_ = f32[5,4,128]{2,1,0:T(4,128)S(1)} collective-permute-done((f32[5,4,128]{2,1,0:T(4,128)S(1)}, f32[5,4,128]{2,1,0:T(4,128)S(1)}, u32[]{:S(2)}, u32[]{:S(2)}) %collective-permute-start.1) | collective-permute-done | bytes 10272 | tf_op jit(solution)/shard_map/ppermute | solution.py:326
  79.1 0.0 collective-permute-done.2.refs_4_
  79.1 0.0 collective-permute-done.3.refs_5_
  79.1 0.0 copy-done.6
  79.1 0.4 shard_map.100.refs_1_
  79.6 0.0 all-to-all-done.1.refs_2_
  79.6 0.0 copy-done.8
  79.6 1.4 %shard_map.103 = f32[5,32,4,128]{3,2,1,0:T(4,128)} custom-call(s32[32]{0:T(128)S(1)} %bitcast.34, f32[5,32,4,128]{3,2,1,0:T(4,128)S(1)} %shard_map.100.refs_1_, bf16[32,48,128]{2,1,0:T(8,128)(2,1)S(1)} %all-to-all-done.1.refs_2_), custom_call_target="tpu_custom_call" | custom-call | tf_op jit(solution)/shard_map/pallas_call | solution.py:397
  (1 shorter events, 0.0 us)
Async XLA Ops:
  0.0 5.8 %collective-permute-start.4 = (s32[1,32]{1,0:T(1,128)}, s32[1,32]{1,0:T(1,128)S(1)}, u32[]{:S(2)}, u32[]{:S(2)}) collective-permute-start(s32[1,32]{1,0:T(1,128)} %bitcast.29), channel_id=1, source_target_pairs={{0,32},{32,64},{64,96},{96,0},{1,33},{33,65},{65,97},{97,1},{2,34}... | collective-permute-start | bytes 392 | tf_op jit(solution)/shard_map/ppermute | solution.py:321
  2.1 4.0 %collective-permute-start.5 = (s32[1,32]{1,0:T(1,128)}, s32[1,32]{1,0:T(1,128)S(1)}, u32[]{:S(2)}, u32[]{:S(2)}) collective-permute-start(s32[1,32]{1,0:T(1,128)} %bitcast.30), channel_id=1, source_target_pairs={{0,64},{32,96},{64,0},{96,32},{1,65},{33,97},{65,1},{97,33},{2,66}... | collective-permute-start | bytes 392 | tf_op jit(solution)/shard_map/ppermute | solution.py:321
  4.7 2.5 %collective-permute-start.6 = (s32[1,32]{1,0:T(1,128)}, s32[1,32]{1,0:T(1,128)S(1)}, u32[]{:S(2)}, u32[]{:S(2)}) collective-permute-start(s32[1,32]{1,0:T(1,128)} %bitcast.31), channel_id=1, source_target_pairs={{0,96},{32,0},{64,32},{96,64},{1,97},{33,1},{65,33},{97,65},{2,98}... | collective-permute-start | bytes 392 | tf_op jit(solution)/shard_map/ppermute | solution.py:321
  7.3 1.0 %copy-start = (f32[5,32,4,128]{3,2,1,0:T(4,128)S(1)}, f32[5,32,4,128]{3,2,1,0:T(4,128)}, u32[]{:S(2)}) copy-start(f32[5,32,4,128]{3,2,1,0:T(4,128)} %flow_ref.1) | copy-start | bytes 983044
  8.2 0.7 copy-start.7
  10.6 20.8 %copy-start.2 = (s32[1,1024,128]{2,1,0:T(8,128)S(1)}, s32[1,1024,128]{2,1,0:T(8,128)}, u32[]{:S(2)}) copy-start(s32[1,1024,128]{2,1,0:T(8,128)} %param.13) | copy-start | bytes 1572868
  10.6 20.8 %copy-start.9 = (s32[1,1024]{1,0:T(1,128)S(1)}, s32[1,1024]{1,0:T(1,128)}, u32[]{:S(2)}) copy-start(s32[1,1024]{1,0:T(1,128)} %param.14) | copy-start | bytes 12292
  10.6 20.8 %all-to-all-start = ((bf16[32,48,128]{2,1,0:T(8,128)(2,1)}), bf16[32,48,128]{2,1,0:T(8,128)(2,1)S(1)}, u32[]{:S(2)}, u32[]{:S(2)}) async-start(bf16[32,48,128]{2,1,0:T(8,128)(2,1)} %shard_map.101), calls=%async_computation | async-start | bytes 786432 | tf_op jit(solution)/shard_map/all_to_all | solution.py:344
  31.3 1.0 %copy-start.3 = (f32[1,1024,128]{2,1,0:T(8,128)S(1)}, f32[1,1024,128]{2,1,0:T(8,128)}, u32[]{:S(2)}) copy-start(f32[1,1024,128]{2,1,0:T(8,128)} %param.16) | copy-start | bytes 1572868
  32.4 1.0 %copy-start.4 = (f32[1,1024,128]{2,1,0:T(8,128)S(1)}, f32[1,1024,128]{2,1,0:T(8,128)}, u32[]{:S(2)}) copy-start(f32[1,1024,128]{2,1,0:T(8,128)} %param.17) | copy-start | bytes 1572868
  33.4 1.0 %copy-start.5 = (f32[1,1024,128]{2,1,0:T(8,128)S(1)}, f32[1,1024,128]{2,1,0:T(8,128)}, u32[]{:S(2)}) copy-start(f32[1,1024,128]{2,1,0:T(8,128)} %param.18) | copy-start | bytes 1572868
  34.5 31.6 %copy-start.1 = (f32[5,32,4,128]{3,2,1,0:T(4,128)S(1)}, f32[5,32,4,128]{3,2,1,0:T(4,128)}, u32[]{:S(2)}) copy-start(f32[5,32,4,128]{3,2,1,0:T(4,128)} %flow_ref.1) | copy-start | bytes 983044
  34.5 44.7 %copy-start.6 = (f32[32,4,128]{2,1,0:T(4,128)S(1)}, f32[32,4,128]{2,1,0:T(4,128)}, u32[]{:S(2)}) copy-start(f32[32,4,128]{2,1,0:T(4,128)} %refs_1_.1) | copy-start | bytes 196612
  34.5 45.1 %copy-start.8 = (s32[1,32,1]{1,2,0:T(1,128)S(1)}, s32[1,32,1]{1,2,0:T(1,128)}, u32[]{:S(2)}) copy-start(s32[1,32,1]{1,2,0:T(1,128)} %param.12) | copy-start | bytes 388
  50.2 29.3 %all-to-all-start.1 = ((bf16[32,48,128]{2,1,0:T(8,128)(2,1)}), bf16[32,48,128]{2,1,0:T(8,128)(2,1)S(1)}, u32[]{:S(2)}, u32[]{:S(2)}) async-start(bf16[32,48,128]{2,1,0:T(8,128)(2,1)} %shard_map.102), calls=%async_computation.1 | async-start | bytes 786432 | tf_op jit(solution)/shard_map/all_to_all | solution.py:381
  66.2 12.9 %collective-permute-start.2 = (f32[5,32,128]{2,1,0:T(8,128)S(1)}, f32[5,32,128]{2,1,0:T(8,128)S(1)}, u32[]{:S(2)}, u32[]{:S(2)}) collective-permute-start(f32[5,32,128]{2,1,0:T(8,128)S(1)} %bitcast.37), channel_id=1, source_target_pairs={{0,32},{32,64},{1,33},{33,65},{2,34},{34,66},{3,35},{35,67},{4,36}... | collective-permute-start | bytes 245768 | tf_op jit(solution)/shard_map/ppermute | solution.py:327
  69.0 10.1 %collective-permute-start.3 = (f32[5,32,128]{2,1,0:T(8,128)S(1)}, f32[5,32,128]{2,1,0:T(8,128)S(1)}, u32[]{:S(2)}, u32[]{:S(2)}) collective-permute-start(f32[5,32,128]{2,1,0:T(8,128)S(1)} %bitcast.36), channel_id=1, source_target_pairs={{32,0},{64,32},{33,1},{65,33},{34,2},{66,34},{35,3},{67,35},{36,4}... | collective-permute-start | bytes 245768 | tf_op jit(solution)/shard_map/ppermute | solution.py:328
  70.3 5.8 %collective-permute-start = (f32[5,4,128]{2,1,0:T(4,128)S(1)}, f32[5,4,128]{2,1,0:T(4,128)S(1)}, u32[]{:S(2)}, u32[]{:S(2)}) collective-permute-start(f32[5,4,128]{2,1,0:T(4,128)S(1)} %get-tuple-element.8), channel_id=1, source_target_pairs={{0,1},{1,2},{2,3},{3,4},{4,5},{5,6},{6,7},{7,8},{8,9},{9,10},{10,1... | collective-permute-start | bytes 30728 | tf_op jit(solution)/shard_map/ppermute | solution.py:325
  74.1 5.0 %collective-permute-start.1 = (f32[5,4,128]{2,1,0:T(4,128)S(1)}, f32[5,4,128]{2,1,0:T(4,128)S(1)}, u32[]{:S(2)}, u32[]{:S(2)}) collective-permute-start(f32[5,4,128]{2,1,0:T(4,128)S(1)} %get-tuple-element.7), channel_id=1, source_target_pairs={{1,0},{2,1},{3,2},{4,3},{5,4},{6,5},{7,6},{8,7},{9,8},{10,9},{11,1... | collective-permute-start | bytes 30728 | tf_op jit(solution)/shard_map/ppermute | solution.py:326

commit v2 on v1

--- a/solution.py
+++ b/solution.py
@@ -11,12 +11,13 @@
 PAIR = 48
 HALF = NF * ROWS_Y
 VMEM_LIMIT = 48 * 1024 * 1024
+COUPLE_VMEM = 62 * 1024 * 1024
 NT = (((1,), (1,)), ((), ()))
 
 
-def pack_kernel(planes, owners, holder_ref, near_refs, flow_ref, out_ref, plane_of, count):
+def pack_kernel(planes, owners, holder_ref, own_ref, up_ref, down_ref, flow_ref, out_ref, plane_of, count):
     g = lax.axis_index("grp")
-    groups = lax.axis_size("grp")
+    gas_groups = lax.axis_size("grp") - 1
 
     def clear(p, carry):
         count[p] = 0
@@ -36,19 +37,16 @@
     lax.fori_loop(0, planes, place, 0, unroll=True)
 
     owner_ids = lax.broadcasted_iota(jnp.int32, (owners, planes), 0)
-    own = jnp.zeros((owners, 1), jnp.float32)
-    before = jnp.zeros((owners, 1), jnp.float32)
-    total = jnp.zeros((owners, 1), jnp.float32)
-    for k, ref in enumerate(near_refs):
-        group = (g - k + groups) % groups
+
+    def tally(ref):
         hits = jnp.where(owner_ids == ref[...], 1.0, 0.0)
-        tally = jnp.sum(hits, axis=1, keepdims=True)
-        tally = jnp.where(group < groups - 1, tally, 0.0)
-        total = total + tally
-        before = before + jnp.where(group < g, tally, 0.0)
-        if k == 0:
-            own = tally
-    own, before, total = (jnp.broadcast_to(v, (owners, LANES)) for v in (own, before, total))
+        return jnp.broadcast_to(jnp.sum(hits, axis=1, keepdims=True), (owners, LANES))
+
+    own = jnp.where(g < gas_groups, tally(own_ref), 0.0)
+    above = tally(up_ref)
+    below = tally(down_ref)
+    total = own + above + below
+    before = jnp.where(g >= 1, above, 0.0) + jnp.where(g == gas_groups - 1, below, 0.0)
     row = lax.broadcasted_iota(jnp.int32, (8, LANES), 0)
     for p in range(owners):
         flags = jnp.where(
@@ -98,6 +96,60 @@
     out.append(weight * (mass * warmth - new_mass * new_warmth))
     out.append(weight * (mass - new_mass))
     return out
+
+
+UA, UB, UC = 32, 32, 32
+ENTRY_BITS = 11
+ENTRY = 1 << ENTRY_BITS
+
+
+def ordered_by_slot(slot, slots):
+    lanes = slot.shape[1]
+    spare = slots * ENTRY + slot.shape[0] * lanes
+    slot_row = lax.broadcasted_iota(jnp.int32, (slots, lanes), 0)
+    hits = [slot_row == jnp.broadcast_to(slot[r : r + 1], (slots, lanes)) for r in range(8)]
+    p = lax.broadcasted_iota(jnp.int32, (lanes, 2 * lanes), 0)
+    q = lax.broadcasted_iota(jnp.int32, (lanes, 2 * lanes), 1)
+    upto = jnp.where(p <= q, 1.0, 0.0).astype(jnp.bfloat16)
+    ones = jnp.concatenate([jnp.where(h, 1.0, 0.0).astype(jnp.bfloat16) for h in hits], axis=0)
+    tally = jnp.dot(ones, upto, preferred_element_type=jnp.float32)
+    count = sum(tally[slots * r : slots * (r + 1), lanes:] for r in range(8))
+    pairs = ((count.astype(jnp.int32) + 1) >> 1)
+    p = lax.broadcasted_iota(jnp.int32, (slots, slots), 0)
+    q = lax.broadcasted_iota(jnp.int32, (slots, slots), 1)
+    before = jnp.where(q < p, 1.0, 0.0).astype(jnp.bfloat16)
+    halves = jnp.concatenate([(pairs >> 4).astype(jnp.float32), (pairs & 15).astype(jnp.float32)], axis=1)
+    ahead = jnp.dot(before, halves.astype(jnp.bfloat16), preferred_element_type=jnp.float32)
+    start = 2.0 * (16.0 * ahead[:, :lanes] + ahead[:, lanes:])
+    number = start[slots - 1 :].astype(jnp.int32) + 2 * pairs[slots - 1 :]
+    carry = start - 1.0
+    low = lax.broadcasted_iota(jnp.int32, (lanes, lanes), 0)
+    high = lax.broadcasted_iota(jnp.int32, (16, lanes), 0)
+    lane = lax.broadcasted_iota(jnp.int32, (16, lanes), 1).astype(jnp.float32)
+    values, places = [], []
+    for r in range(8):
+        here = tally[slots * r : slots * (r + 1)]
+        at = jnp.sum(jnp.where(hits[r], here[:, :lanes] + carry, 0.0), axis=0, keepdims=True)
+        carry = carry + here[:, lanes:]
+        own = slot[r : r + 1]
+        at = jnp.where(own >= 0, at.astype(jnp.int32), -1)
+        mask = high == (at >> 7)
+        for_own = jnp.broadcast_to(own.astype(jnp.float32), (16, lanes))
+        values.append(
+            jnp.concatenate(
+                [jnp.where(mask, v, 0.0) for v in (1.0, float(r), lane, for_own)], axis=0
+            ).astype(jnp.bfloat16)
+        )
+        places.append(jnp.where(low == (at & (lanes - 1)), 1.0, 0.0).astype(jnp.bfloat16))
+    found = lax.dot_general(
+        jnp.concatenate(values, axis=1),
+        jnp.concatenate(places, axis=1),
+        NT,
+        preferred_element_type=jnp.float32,
+    )
+    code = found[48:64] * float(ENTRY) + found[16:32] * float(lanes) + found[32:48]
+    code = jnp.where(found[:16] > 0.5, code.astype(jnp.int32), spare)
+    return jnp.where(high == 15, jnp.broadcast_to(number, (16, lanes)), code)
 
 
 def couple_kernel(
@@ -121,10 +173,8 @@
     deposit,
     code_v,
     code_s,
-    work,
     seen,
     gathered,
-    source,
     sems,
 ):
     slots = 2 * owners
@@ -132,11 +182,11 @@
         pltpu.make_async_copy(a, b, sems.at[i])
         for i, (a, b) in enumerate(
             (
-                (cell_hbm, cell),
-                (motion_hbm, motion),
-                (warmth_hbm, warmth),
-                (mass_hbm, mass),
-                (weight_hbm, weight),
+                (cell_hbm, cell.at[pl.ds(0, blocks)]),
+                (motion_hbm, motion.at[:, pl.ds(0, blocks)]),
+                (warmth_hbm, warmth.at[pl.ds(0, blocks)]),
+                (mass_hbm, mass.at[pl.ds(0, blocks)]),
+                (weight_hbm, weight.at[pl.ds(0, blocks)]),
             )
         )
     ]
@@ -173,9 +223,15 @@
         + lax.broadcasted_iota(jnp.int32, (8, LANES), 1)
     )
     mine = (place >= 0.0) & (place < running) & (block < live_ref[0])
-    code_v[...] = jnp.where(mine, slot * blocks + block, -1)
+    code_v[...] = ordered_by_slot(jnp.where(mine, slot, -1), slots)
     to_scalar = pltpu.make_async_copy(code_v, code_s, sems.at[5])
     to_scalar.start()
+    cell[blocks : blocks + 8] = jnp.zeros((8, LANES), jnp.int32)
+    for k in range(3):
+        motion[k, blocks : blocks + 8] = jnp.zeros((8, LANES), jnp.float32)
+    warmth[blocks : blocks + 8] = jnp.zeros((8, LANES), jnp.float32)
+    mass[blocks : blocks + 8] = jnp.ones((8, LANES), jnp.float32)
+    weight[blocks : blocks + 8] = jnp.zeros((8, LANES), jnp.float32)
 
     spread = slot_relayout()
     for t in range(owners):
@@ -189,69 +245,92 @@
 
     lax.fori_loop(0, owners, clear, 0)
     deposit[4 * slots : 4 * slots + 4] = jnp.zeros((4, 8, LANES), jnp.float32)
-    source[...] = jnp.zeros_like(source)
     to_scalar.wait()
 
-    def collect(j, n):
-        for i in range(8):
-            code = code_s[j >> 4, (j & 15) * 8 + i]
-            work[n] = code
-            n = n + jnp.where(code >= 0, 1, 0)
-        return n
-
-    found = lax.fori_loop(0, (live_ref[0] + 7) // 8, collect, 0)
-    for i in range(8):
-        work[found + i] = slots * blocks
+    found = code_s[15, 0]
     for copy in copies:
         copy.wait()
 
-    cell_row = lax.broadcasted_iota(jnp.int32, (LANES, LANES), 0)
-
-    def advance(j, carry):
-        where_to = []
-        for i in range(8):
-            code = work[8 * j + i]
-            b = code & (blocks - 1)
-            slot = code >> (blocks.bit_length() - 1)
-            cells = cell[pl.ds(b, 1), :]
-            where_to.append((slot, cells))
-            around = jnp.broadcast_to(cells, (8, LANES))
-            z, y = around & (LANES - 1), around >> 7
-            rows = [
-                jnp.take_along_axis(table[4 * slot + k], z, axis=1) for k in range(ROWS_Y)
-            ]
-            seen[8 * i : 8 * i + 8] = jnp.where(
-                y == 0, rows[0], jnp.where(y == 1, rows[1], jnp.where(y == 2, rows[2], rows[3]))
-            )
-            moving = motion[b]
+    sub = lax.broadcasted_iota(jnp.int32, (8, LANES), 0)
+
+    def entry(n0, i):
+        code = code_s[n0 >> 7, (n0 & (LANES - 1)) + i]
+        return code & (ENTRY - 1), code >> ENTRY_BITS
+
+    def look_up(j, carry):
+        n0 = UA * j
+        for i in range(0, UA, 2):
+            slot = entry(n0, i)[1]
+            tile = [table[4 * slot + k] for k in range(ROWS_Y)]
+            for h in range(2):
+                n = n0 + i + h
+                b = entry(n0, i + h)[0]
+                around = jnp.broadcast_to(cell[pl.ds(b, 1), :], (8, LANES))
+                z, y = around & (LANES - 1), around >> 7
+                rows = [jnp.take_along_axis(tile[k], z, axis=1) for k in range(ROWS_Y)]
+                seen[n] = jnp.where(
+                    y == 0, rows[0], jnp.where(y == 1, rows[1], jnp.where(y == 2, rows[2], rows[3]))
+                )
+        for i in range(UA):
+            n = n0 + i
+            b = entry(n0, i)[0]
             for k in range(3):
-                gathered[k, i : i + 1, :] = moving[k : k + 1]
-            gathered[3, i : i + 1, :] = warmth[pl.ds(b, 1), :]
-            gathered[4, i : i + 1, :] = mass[pl.ds(b, 1), :]
-            gathered[5, i : i + 1, :] = weight[pl.ds(b, 1), :]
-        gas = [seen[pl.ds(f, 8, stride=8), :] for f in range(NF)]
+                gathered[k, pl.ds(n, 1), :] = motion[k, pl.ds(b, 1), :]
+            gathered[3, pl.ds(n, 1), :] = warmth[pl.ds(b, 1), :]
+            gathered[4, pl.ds(n, 1), :] = mass[pl.ds(b, 1), :]
+            gathered[5, pl.ds(n, 1), :] = weight[pl.ds(b, 1), :]
+        return carry
+
+    lax.fori_loop(0, (found + UA - 1) // UA, look_up, 0)
+
+    def move(j, carry):
+        at = pl.multiple_of(UB * j, UB)
+        rows = pl.ds(at, UB)
+        gas = [seen[rows, f, :] for f in range(NF)]
         sources = coupling(
-            gas, [gathered[k] for k in range(3)], gathered[3], gathered[4], gathered[5]
+            gas,
+            [gathered[k, rows, :] for k in range(3)],
+            gathered[3, rows, :],
+            gathered[4, rows, :],
+            gathered[5, rows, :],
         )
         for f in range(NF):
-            source[pl.ds(f, 8, stride=8), :] = sources[f]
-        for i in range(8):
-            slot, cells = where_to[i]
-            around = jnp.broadcast_to(cells, (8, LANES))
-            y = around >> 7
-            part = source[8 * i : 8 * i + 8]
-            masked = jnp.concatenate([jnp.where(y == k, part, 0.0) for k in range(ROWS_Y)], axis=0)
-            upper = masked.astype(jnp.bfloat16)
-            lower = (masked - upper.astype(jnp.float32)).astype(jnp.bfloat16)
-            hot = jnp.where(cell_row == (cells & (LANES - 1)), 1.0, 0.0).astype(jnp.bfloat16)
-            both = lax.dot_general(
-                jnp.concatenate([upper, lower], axis=0), hot, NT, preferred_element_type=jnp.float32
-            )
-            added = (both[:32] + both[32:]).reshape(4, 8, LANES)
+            seen[rows, f, :] = sources[f]
+        return carry
+
+    lax.fori_loop(0, (found + UB - 1) // UB, move, 0)
+
+    cell_row = lax.broadcasted_iota(jnp.int32, (LANES, LANES), 0)
+
+    def scatter(j, carry):
+        n0 = UC * j
+        for i in range(0, UC, 2):
+            slot = entry(n0, i)[1]
+            parts, hots = [], []
+            for h in range(2):
+                n = n0 + i + h
+                b = entry(n0, i + h)[0]
+                cells = cell[pl.ds(b, 1), :]
+                y = jnp.broadcast_to(cells, (8, LANES)) >> 7
+                part = seen[n]
+                parts.append(
+                    jnp.concatenate(
+                        [jnp.where(y == k, part, 0.0) for k in range(ROWS_Y)], axis=0
+                    ).astype(jnp.bfloat16)
+                )
+                hots.append(
+                    jnp.where(cell_row == (cells & (LANES - 1)), 1.0, 0.0).astype(jnp.bfloat16)
+                )
+            added = lax.dot_general(
+                jnp.concatenate(parts, axis=1),
+                jnp.concatenate(hots, axis=1),
+                NT,
+                preferred_element_type=jnp.float32,
+            ).reshape(4, 8, LANES)
             deposit[pl.ds(4 * slot, 4)] = deposit[pl.ds(4 * slot, 4)] + added
         return carry
 
-    lax.fori_loop(0, (found + 7) // 8, advance, 0)
+    lax.fori_loop(0, (found + UC - 1) // UC, scatter, 0)
 
     back = slot_relayout_back()
     for t in range(owners):
@@ -266,8 +345,10 @@
             here = flow_ref[f, x]
             left = xlo_ref[f] if x == 0 else flow_ref[f, x - 1]
             right = xhi_ref[f] if x == planes - 1 else flow_ref[f, x + 1]
-            lower = jnp.concatenate([ylo_ref[f, x : x + 1], here[: ROWS_Y - 1]], axis=0)
-            upper = jnp.concatenate([here[1:], yhi_ref[f, x : x + 1]], axis=0)
+            first = ylo_ref[f, x : x + 1]
+            last = yhi_ref[f, x : x + 1]
+            lower = jnp.concatenate([first, here[: ROWS_Y - 1]], axis=0)
+            upper = jnp.concatenate([here[1:], last], axis=0)
             back = jnp.where(lane == 0, 0.0, pltpu.roll(here, 1, 1))
             ahead = jnp.where(lane == LANES - 1, 0.0, pltpu.roll(here, LANES - 1, 1))
             laplace = right + left + upper + lower + ahead + back - 6.0 * here
@@ -292,6 +373,40 @@
         for f in range(NF):
             value = adv_ref[f, x] + landed[ROWS_Y * f : ROWS_Y * f + ROWS_Y]
             out_ref[f, x] = jnp.where(keep, value, 0.0)
+
+
+def couple_call(live, pick, arrived, cell, motion, warmth, mass, weight):
+    owners, blocks = arrived.shape[0], cell.shape[0]
+    vmem = pl.BlockSpec(memory_space=pltpu.VMEM)
+    smem = pl.BlockSpec(memory_space=pltpu.SMEM)
+    hbm = pl.BlockSpec(memory_space=pl.ANY)
+    params = pltpu.CompilerParams(vmem_limit_bytes=COUPLE_VMEM)
+    message = jax.ShapeDtypeStruct((owners, PAIR, LANES), jnp.bfloat16)
+
+    def couple_body(*refs):
+        couple_kernel(owners, blocks, *refs)
+
+    return pl.pallas_call(
+        couple_body,
+        out_shape=message,
+        in_specs=[smem, vmem, vmem] + [hbm] * 5,
+        out_specs=vmem,
+        scratch_shapes=[
+            pltpu.VMEM((blocks + 8, LANES), jnp.int32),
+            pltpu.VMEM((3, blocks + 8, LANES), jnp.float32),
+            pltpu.VMEM((blocks + 8, LANES), jnp.float32),
+            pltpu.VMEM((blocks + 8, LANES), jnp.float32),
+            pltpu.VMEM((blocks + 8, LANES), jnp.float32),
+            pltpu.VMEM((8 * owners + 4, 8, LANES), jnp.float32),
+            pltpu.VMEM((8 * owners + 4, 8, LANES), jnp.float32),
+            pltpu.VMEM((16, LANES), jnp.int32),
+            pltpu.SMEM((16, LANES), jnp.int32),
+            pltpu.VMEM((blocks + 96, 8, LANES), jnp.float32),
+            pltpu.VMEM((6, blocks + 96, LANES), jnp.float32),
+            pltpu.SemaphoreType.DMA((6,)),
+        ],
+        compiler_params=params,
+    )(live, pick, arrived, cell, motion.transpose(1, 0, 2), warmth, mass, weight)
 
 
 def local(
@@ -312,63 +427,37 @@
     blocks = spray_volume_position.shape[1]
     vmem = pl.BlockSpec(memory_space=pltpu.VMEM)
     smem = pl.BlockSpec(memory_space=pltpu.SMEM)
-    hbm = pl.BlockSpec(memory_space=pl.ANY)
     params = pltpu.CompilerParams(vmem_limit_bytes=VMEM_LIMIT)
 
     holder = holder_unit.reshape(planes)
-    near = [holder.reshape(1, planes)]
-    for k in range(1, groups):
-        near.append(lax.ppermute(near[0], "grp", [(i, (i + k) % groups) for i in range(groups)]))
-
-    up_tile = [(i, i + 1) for i in range(owners - 1)]
-    up_grp = [(i, i + 1) for i in range(groups - 2)]
-    xlo = lax.ppermute(flow_fields[:, planes - 1], "tile", up_tile)
-    xhi = lax.ppermute(flow_fields[:, 0], "tile", [(b, a) for a, b in up_tile])
-    ylo = lax.ppermute(flow_fields[:, :, ROWS_Y - 1], "grp", up_grp)
-    yhi = lax.ppermute(flow_fields[:, :, 0], "grp", [(b, a) for a, b in up_grp])
-
-    def pack_body(holder_ref, n0, n1, n2, n3, flow_ref, out_ref, plane_of, count):
-        pack_kernel(
-            planes, owners, holder_ref, (n0, n1, n2, n3), flow_ref, out_ref, plane_of, count
-        )
-
-    message = jax.ShapeDtypeStruct((owners, PAIR, LANES), jnp.bfloat16)
+    own_row = holder[None]
+
+    gas = groups - 1
+    round_up = [(i, (i + 1) % gas) for i in range(gas)]
+    up = lax.ppermute(own_row, "grp", round_up)
+    down = lax.ppermute(own_row, "grp", [(b, a) for a, b in round_up])
+
+    def pack_body(*refs):
+        pack_kernel(planes, owners, *refs)
+
     packed = pl.pallas_call(
         pack_body,
-        out_shape=message,
-        in_specs=[smem] + [vmem] * 5,
+        out_shape=jax.ShapeDtypeStruct((owners, PAIR, LANES), jnp.bfloat16),
+        in_specs=[smem] + [vmem] * 4,
         out_specs=vmem,
         scratch_shapes=[pltpu.SMEM((2 * owners,), jnp.int32), pltpu.SMEM((owners,), jnp.int32)],
         compiler_params=params,
-    )(holder, *near, flow_fields)
+    )(holder, own_row, up, down, flow_fields)
+
+    packed, top, bottom = lax.optimization_barrier(
+        (packed, flow_fields[:, :, ROWS_Y - 1], flow_fields[:, :, 0])
+    )
     arrived = lax.all_to_all(packed, "tile", 0, 0, tiled=True)
-
-    def couple_body(*refs):
-        couple_kernel(owners, blocks, *refs)
-
-    outgoing = pl.pallas_call(
-        couple_body,
-        out_shape=message,
-        in_specs=[smem, vmem, vmem] + [hbm] * 5,
-        out_specs=vmem,
-        scratch_shapes=[
-            pltpu.VMEM((blocks, LANES), jnp.int32),
-            pltpu.VMEM((blocks, 3, LANES), jnp.float32),
-            pltpu.VMEM((blocks, LANES), jnp.float32),
-            pltpu.VMEM((blocks, LANES), jnp.float32),
-            pltpu.VMEM((blocks, LANES), jnp.float32),
-            pltpu.VMEM((8 * owners + 4, 8, LANES), jnp.float32),
-            pltpu.VMEM((8 * owners + 4, 8, LANES), jnp.float32),
-            pltpu.VMEM((8, LANES), jnp.int32),
-            pltpu.SMEM((8, LANES), jnp.int32),
-            pltpu.SMEM((blocks + 16,), jnp.int32),
-            pltpu.VMEM((64, LANES), jnp.float32),
-            pltpu.VMEM((6, 8, LANES), jnp.float32),
-            pltpu.VMEM((64, LANES), jnp.float32),
-            pltpu.SemaphoreType.DMA((6,)),
-        ],
-        compiler_params=params,
-    )(
+    up_grp = [(i, i + 1) for i in range(gas - 1)]
+    ylo = lax.ppermute(top, "grp", up_grp)
+    yhi = lax.ppermute(bottom, "grp", [(b, a) for a, b in up_grp])
+    arrived, ylo, yhi = lax.optimization_barrier((arrived, ylo, yhi))
+    outgoing = couple_call(
         living_spray_batches,
         patch_pick_unreduced.reshape(8, LANES),
         arrived,
@@ -378,7 +467,14 @@
         droplet_weightiness[0],
         droplet_multiplicity[0],
     )
+
+    outgoing, back_plane, front_plane = lax.optimization_barrier(
+        (outgoing, flow_fields[:, planes - 1], flow_fields[:, 0])
+    )
     landed = lax.all_to_all(outgoing, "tile", 0, 0, tiled=True)
+    up_tile = [(i, i + 1) for i in range(owners - 1)]
+    xlo = lax.ppermute(back_plane, "tile", up_tile)
+    xhi = lax.ppermute(front_plane, "tile", [(b, a) for a, b in up_tile])
 
     def diffuse_body(*refs):
         diffuse_kernel(planes, *refs)
@@ -390,7 +486,7 @@
         out_specs=vmem,
         compiler_params=params,
     )(flow_fields, turbulent_diffusivity, xlo, xhi, ylo, yhi)
-
+    landed, diffused = lax.optimization_barrier((landed, diffused))
     def finish_body(*refs):
         finish_kernel(planes, owners, *refs)
 

time: 81.8 us -> 66.8 us (0.82)
  Pallas kernels: 19.3 us -> 11.5 us
  starting transfers between devices: 41.9 us -> 36.5 us
  local copies, waits for them, and re-layouts: 7.39 us -> 3.64 us
  waiting for transfers between devices: 11.7 us -> 14.2 us
    pallas_call x2, Pallas kernels: 17.4 us -> 9.64 us  [the longest x1 7.99 us: couple_call(): pl.pallas_call(couple_body, out_shape=message, in_specs=[smem, vmem, vmem...]
    ppermute x7 -> x6, waiting for transfers between devices: 4.52 us -> 9.82 us  [the longest x1 3.72 us: local(): yhi = lax.ppermute(bottom, 'grp', [(b, a) for a, b in up_grp])]
    all_to_all x1, starting transfers between devices: 15.9 us -> 10.8 us  [local(): landed = lax.all_to_all(outgoing, 'tile', 0, 0, tiled=True)]
    unnamed x21 -> x12, local copies, waits for them, and re-layouts: 7.26 us -> 2.39 us
    all_to_all x1, waiting for transfers between devices: 7.16 us -> 3.3 us  [local(): arrived = lax.all_to_all(packed, 'tile', 0, 0, tiled=True)]
    slice x1, local copies, waits for them, and re-layouts: 0.13 us -> 1.24 us  [local(): flow_fields[:, :, 0]]
    all_to_all x1, waiting for transfers between devices: 0.01 us -> 1.04 us  [local(): landed = lax.all_to_all(outgoing, 'tile', 0, 0, tiled=True)]
    ppermute x7 -> x6, starting transfers between devices: 15.6 us -> 15.7 us  [the longest x1 5.77 us: local(): down = lax.ppermute(own_row, 'grp', [(b, a) for a, b in round_up])]
  transfers between devices with their start and end apart: 9 -> 8, of which waited for: 4 -> 5; matrix products, arithmetic and copies ran while one was open for 3% -> 2% of each run, Pallas kernels for 1% -> 1%
where the time goes in v2:
time: 66.8 us; the launch traced here: 66.6 us
  starting transfers between devices  36.5 us (55%)
  waiting for transfers between devices  14.2 us (21%)
  Pallas kernels  11.5 us (17%)
  local copies, waits for them, and re-layouts  3.64 us (5%)
  between operations  0.79 us (1%)
    all_to_all x1, starting transfers between devices, local(): landed = lax.all_to_all(outgoing, 'tile', 0, 0, tiled=True)  10.8 us
    all_to_all x1, starting transfers between devices, local(): arrived = lax.all_to_all(packed, 'tile', 0, 0, tiled=True)  10 us
    pallas_call x1, Pallas kernels, couple_call(): pl.pallas_call(couple_body, out_shape=message, in_specs=[smem, vmem, vmem...  7.99 us
    ppermute x1, starting transfers between devices, local(): down = lax.ppermute(own_row, 'grp', [(b, a) for a, b in round_up])  5.77 us
    ppermute x1, waiting for transfers between devices, local(): yhi = lax.ppermute(bottom, 'grp', [(b, a) for a, b in up_grp])  3.72 us
    ppermute x1, starting transfers between devices, local(): xlo = lax.ppermute(back_plane, 'tile', up_tile)  3.54 us
    ppermute x1, waiting for transfers between devices, local(): xhi = lax.ppermute(front_plane, 'tile', [(b, a) for a, b in up_tile])  3.35 us
    all_to_all x1, waiting for transfers between devices, local(): arrived = lax.all_to_all(packed, 'tile', 0, 0, tiled=True)  3.3 us
  transfers between devices with their start and end apart: 8, of which 5 were waited for; matrix products, arithmetic and copies ran while one was open for 2% of the time, Pallas kernels for 1%

profile of v2, /device:TPU:1, one launch (start us, length us, event | category | flops | bytes accessed | tf_op | source)
XLA Modules:
  0.0 66.6 jit_solution(5269243511302674737)
XLA Ops:
  0.0 0.0 copy-start.1
  0.0 5.8 %collective-permute-start.1 = (s32[1,32]{1,0:T(1,128)}, s32[1,32]{1,0:T(1,128)S(1)}, u32[]{:S(2)}, u32[]{:S(2)}) collective-permute-start(s32[1,32]{1,0:T(1,128)} %bitcast.24), channel_id=1, source_target_pairs={{32,0},{64,32},{0,64},{33,1},{65,33},{1,65},{34,2},{66,34},{2,66},... | collective-permute-start | bytes 392 | tf_op jit(solution)/shard_map/ppermute | solution.py:438
  5.8 1.9 %collective-permute-start = (s32[1,32]{1,0:T(1,128)}, s32[1,32]{1,0:T(1,128)S(1)}, u32[]{:S(2)}, u32[]{:S(2)}) collective-permute-start(s32[1,32]{1,0:T(1,128)} %bitcast.25), channel_id=1, source_target_pairs={{0,32},{32,64},{64,0},{1,33},{33,65},{65,1},{2,34},{34,66},{66,2},... | collective-permute-start | bytes 392 | tf_op jit(solution)/shard_map/ppermute | solution.py:437
  7.7 1.2 %fusion = (f32[5,32,1,128]{3,2,1,0:T(1,128)S(1)}, f32[5,32,1,128]{3,2,1,0:T(1,128)S(1)}) fusion(f32[5,32,4,128]{3,2,1,0:T(4,128)} %refs_0_.2), kind=kLoop, calls=%fused_computation.2 | loop fusion | bytes 327680 | tf_op jit(solution)/shard_map/slice | solution.py:453
  9.0 0.0 collective-permute-done.1.refs_3_
  9.0 2.7 %collective-permute-done.refs_2_ = s32[1,32]{1,0:T(1,128)S(1)} collective-permute-done((s32[1,32]{1,0:T(1,128)}, s32[1,32]{1,0:T(1,128)S(1)}, u32[]{:S(2)}, u32[]{:S(2)}) %collective-permute-start) | collective-permute-done | bytes 160 | tf_op jit(solution)/shard_map/ppermute | solution.py:437
  11.7 0.0 copy-start
  11.7 1.0 %copy-done = f32[5,32,4,128]{3,2,1,0:T(4,128)S(1)} copy-done((f32[5,32,4,128]{3,2,1,0:T(4,128)S(1)}, f32[5,32,4,128]{3,2,1,0:T(4,128)}, u32[]{:S(2)}) %copy-start) | copy-done | bytes 327704
  12.7 0.0 copy-start.3
  12.7 0.7 copy-done.3
  13.3 1.7 %shard_map.100 = bf16[32,48,128]{2,1,0:T(8,128)(2,1)} custom-call(s32[32]{0:T(128)S(1)} %bitcast.26, s32[1,32]{1,0:T(1,128)S(1)} %bitcast.27, s32[1,32]{1,0:T(1,128)S(1)} %collective-permute-done.refs_2_, s32[1,32]{1,0:T(1,128)S(1)} %collective-permute-done.1.refs_3_, f32[5,32,4,128]{3,2,1,0:T(4,128)S(1)} %copy-done), custom_call_target="tpu_custom_call" | custom-call | tf_op jit(solution)/shard_map/pallas_call | solution.py:443
  15.0 10.0 %all-to-all-start = ((bf16[32,48,128]{2,1,0:T(8,128)(2,1)}), bf16[32,48,128]{2,1,0:T(8,128)(2,1)S(1)}, u32[]{:S(2)}, u32[]{:S(2)}) async-start(bf16[32,48,128]{2,1,0:T(8,128)(2,1)} %shard_map.100), calls=%async_computation | async-start | bytes 786432 | tf_op jit(solution)/shard_map/all_to_all | solution.py:455
  25.0 1.3 %collective-permute-start.2 = (f32[5,32,128]{2,1,0:T(8,128)S(1)}, f32[5,32,128]{2,1,0:T(8,128)S(1)}, u32[]{:S(2)}, u32[]{:S(2)}) collective-permute-start(f32[5,32,128]{2,1,0:T(8,128)S(1)} %bitcast.35), channel_id=1, source_target_pairs={{0,32},{32,64},{1,33},{33,65},{2,34},{34,66},{3,35},{35,67},{4,36}... | collective-permute-start | bytes 245768 | tf_op jit(solution)/shard_map/ppermute | solution.py:457
  26.3 1.3 %collective-permute-start.3 = (f32[5,32,128]{2,1,0:T(8,128)S(1)}, f32[5,32,128]{2,1,0:T(8,128)S(1)}, u32[]{:S(2)}, u32[]{:S(2)}) collective-permute-start(f32[5,32,128]{2,1,0:T(8,128)S(1)} %bitcast.34), channel_id=1, source_target_pairs={{32,0},{64,32},{33,1},{65,33},{34,2},{66,34},{35,3},{67,35},{36,4}... | collective-permute-start | bytes 245768 | tf_op jit(solution)/shard_map/ppermute | solution.py:458
  27.6 0.0 copy-done.1
  28.3 0.0 collective-permute-done.2.refs_4_
  28.3 3.7 %collective-permute-done.3.refs_5_ = f32[5,32,128]{2,1,0:T(8,128)S(1)} collective-permute-done((f32[5,32,128]{2,1,0:T(8,128)S(1)}, f32[5,32,128]{2,1,0:T(8,128)S(1)}, u32[]{:S(2)}, u32[]{:S(2)}) %collective-permute-start.3) | collective-permute-done | bytes 81952 | tf_op jit(solution)/shard_map/ppermute | solution.py:458
  32.0 3.3 %all-to-all-done.refs_2_ = bf16[32,48,128]{2,1,0:T(8,128)(2,1)S(1)} async-done(((bf16[32,48,128]{2,1,0:T(8,128)(2,1)}), bf16[32,48,128]{2,1,0:T(8,128)(2,1)S(1)}, u32[]{:S(2)}, u32[]{:S(2)}) %all-to-all-start) | async-done | bytes 393248 | tf_op jit(solution)/shard_map/all_to_all | solution.py:455
  35.3 0.0 copy-start.5
  35.3 0.8 %copy-done.5 = bf16[32,48,128]{2,1,0:T(8,128)(2,1)} copy-done((bf16[32,48,128]{2,1,0:T(8,128)(2,1)}, bf16[32,48,128]{2,1,0:T(8,128)(2,1)S(1)}, u32[]{:S(2)}) %copy-start.5) | copy-done | bytes 393240
  36.1 0.0 copy-start.2
  36.1 8.0 %shard_map.101 = bf16[32,48,128]{2,1,0:T(8,128)(2,1)} custom-call(s32[1]{0:T(128)S(6)} %copy.19.refs_0_, s32[8,128]{1,0:T(8,128)} %bitcast.36, bf16[32,48,128]{2,1,0:T(8,128)(2,1)} %copy-done.5, s32[1024,128]{1,0:T(8,128)} %bitcast.30, f32[3,1024,128]{2,1,0:T(8,128)} %bitcast.29, f32[1024,128]{1,0:T(8,128)} %bitcast.31, f32[1024,128]{1,0:T(8,128)} %bitcast.32, ...), custom_call_target="tpu_custom_call" | custom-call | tf_op jit(solution)/shard_map/pallas_call | solution.py:389
  44.1 0.0 copy-start.4
  44.1 10.8 %all-to-all-start.1 = ((bf16[32,48,128]{2,1,0:T(8,128)(2,1)}), bf16[32,48,128]{2,1,0:T(8,128)(2,1)S(1)}, u32[]{:S(2)}, u32[]{:S(2)}) async-start(bf16[32,48,128]{2,1,0:T(8,128)(2,1)} %shard_map.101), calls=%async_computation.1 | async-start | bytes 786432 | tf_op jit(solution)/shard_map/all_to_all | solution.py:474
  54.9 3.5 %collective-permute-start.4 = (f32[5,4,128]{2,1,0:T(4,128)S(1)}, f32[5,4,128]{2,1,0:T(4,128)S(1)}, u32[]{:S(2)}, u32[]{:S(2)}) collective-permute-start(f32[5,4,128]{2,1,0:T(4,128)S(1)} %get-tuple-element.21), channel_id=1, source_target_pairs={{0,1},{1,2},{2,3},{3,4},{4,5},{5,6},{6,7},{7,8},{8,9},{9,10},{10,1... | collective-permute-start | bytes 30728 | tf_op jit(solution)/shard_map/ppermute | solution.py:476
  58.4 1.9 %collective-permute-start.5 = (f32[5,4,128]{2,1,0:T(4,128)S(1)}, f32[5,4,128]{2,1,0:T(4,128)S(1)}, u32[]{:S(2)}, u32[]{:S(2)}) collective-permute-start(f32[5,4,128]{2,1,0:T(4,128)S(1)} %get-tuple-element.22), channel_id=1, source_target_pairs={{1,0},{2,1},{3,2},{4,3},{5,4},{6,5},{7,6},{8,7},{9,8},{10,9},{11,1... | collective-permute-start | bytes 30728 | tf_op jit(solution)/shard_map/ppermute | solution.py:477
  60.4 0.0 collective-permute-done.4.refs_2_
  60.4 3.3 %collective-permute-done.5.refs_3_ = f32[5,4,128]{2,1,0:T(4,128)S(1)} collective-permute-done((f32[5,4,128]{2,1,0:T(4,128)S(1)}, f32[5,4,128]{2,1,0:T(4,128)S(1)}, u32[]{:S(2)}, u32[]{:S(2)}) %collective-permute-start.5) | collective-permute-done | bytes 10272 | tf_op jit(solution)/shard_map/ppermute | solution.py:477
  63.7 0.0 copy-done.2
  63.7 0.4 shard_map.102.refs_1_
  64.1 1.0 %all-to-all-done.1.refs_2_ = bf16[32,48,128]{2,1,0:T(8,128)(2,1)S(1)} async-done(((bf16[32,48,128]{2,1,0:T(8,128)(2,1)}), bf16[32,48,128]{2,1,0:T(8,128)(2,1)S(1)}, u32[]{:S(2)}, u32[]{:S(2)}) %all-to-all-start.1) | async-done | bytes 393248 | tf_op jit(solution)/shard_map/all_to_all | solution.py:474
  65.2 0.0 copy-done.4
  65.2 1.4 %shard_map.103 = f32[5,32,4,128]{3,2,1,0:T(4,128)} custom-call(s32[32]{0:T(128)S(1)} %bitcast.28, f32[5,32,4,128]{3,2,1,0:T(4,128)S(1)} %shard_map.102.refs_1_, bf16[32,48,128]{2,1,0:T(8,128)(2,1)S(1)} %all-to-all-done.1.refs_2_), custom_call_target="tpu_custom_call" | custom-call | tf_op jit(solution)/shard_map/pallas_call | solution.py:493
  (1 shorter events, 0.0 us)
Async XLA Ops:
  0.0 27.6 %copy-start.1 = (f32[5,32,4,128]{3,2,1,0:T(4,128)S(1)}, f32[5,32,4,128]{3,2,1,0:T(4,128)}, u32[]{:S(2)}) copy-start(f32[5,32,4,128]{3,2,1,0:T(4,128)} %refs_0_.2) | copy-start | bytes 983044
  0.0 9.0 %collective-permute-start.1 = (s32[1,32]{1,0:T(1,128)}, s32[1,32]{1,0:T(1,128)S(1)}, u32[]{:S(2)}, u32[]{:S(2)}) collective-permute-start(s32[1,32]{1,0:T(1,128)} %bitcast.24), channel_id=1, source_target_pairs={{32,0},{64,32},{0,64},{33,1},{65,33},{1,65},{34,2},{66,34},{2,66},... | collective-permute-start | bytes 392 | tf_op jit(solution)/shard_map/ppermute | solution.py:438
  5.8 5.9 %collective-permute-start = (s32[1,32]{1,0:T(1,128)}, s32[1,32]{1,0:T(1,128)S(1)}, u32[]{:S(2)}, u32[]{:S(2)}) collective-permute-start(s32[1,32]{1,0:T(1,128)} %bitcast.25), channel_id=1, source_target_pairs={{0,32},{32,64},{64,0},{1,33},{33,65},{65,1},{2,34},{34,66},{66,2},... | collective-permute-start | bytes 392 | tf_op jit(solution)/shard_map/ppermute | solution.py:437
  11.7 1.0 %copy-start = (f32[5,32,4,128]{3,2,1,0:T(4,128)S(1)}, f32[5,32,4,128]{3,2,1,0:T(4,128)}, u32[]{:S(2)}) copy-start(f32[5,32,4,128]{3,2,1,0:T(4,128)} %refs_0_.2) | copy-start | bytes 983044
  12.7 0.7 copy-start.3
  15.0 20.3 %all-to-all-start = ((bf16[32,48,128]{2,1,0:T(8,128)(2,1)}), bf16[32,48,128]{2,1,0:T(8,128)(2,1)S(1)}, u32[]{:S(2)}, u32[]{:S(2)}) async-start(bf16[32,48,128]{2,1,0:T(8,128)(2,1)} %shard_map.100), calls=%async_computation | async-start | bytes 786432 | tf_op jit(solution)/shard_map/all_to_all | solution.py:455
  25.0 3.3 %collective-permute-start.2 = (f32[5,32,128]{2,1,0:T(8,128)S(1)}, f32[5,32,128]{2,1,0:T(8,128)S(1)}, u32[]{:S(2)}, u32[]{:S(2)}) collective-permute-start(f32[5,32,128]{2,1,0:T(8,128)S(1)} %bitcast.35), channel_id=1, source_target_pairs={{0,32},{32,64},{1,33},{33,65},{2,34},{34,66},{3,35},{35,67},{4,36}... | collective-permute-start | bytes 245768 | tf_op jit(solution)/shard_map/ppermute | solution.py:457
  26.3 5.7 %collective-permute-start.3 = (f32[5,32,128]{2,1,0:T(8,128)S(1)}, f32[5,32,128]{2,1,0:T(8,128)S(1)}, u32[]{:S(2)}, u32[]{:S(2)}) collective-permute-start(f32[5,32,128]{2,1,0:T(8,128)S(1)} %bitcast.34), channel_id=1, source_target_pairs={{32,0},{64,32},{33,1},{65,33},{34,2},{66,34},{35,3},{67,35},{36,4}... | collective-permute-start | bytes 245768 | tf_op jit(solution)/shard_map/ppermute | solution.py:458
  35.3 0.8 %copy-start.5 = (bf16[32,48,128]{2,1,0:T(8,128)(2,1)}, bf16[32,48,128]{2,1,0:T(8,128)(2,1)S(1)}, u32[]{:S(2)}) copy-start(bf16[32,48,128]{2,1,0:T(8,128)(2,1)S(1)} %all-to-all-done.refs_2_) | copy-start | bytes 1179652
  36.1 27.6 %copy-start.2 = (f32[32,4,128]{2,1,0:T(4,128)S(1)}, f32[32,4,128]{2,1,0:T(4,128)}, u32[]{:S(2)}) copy-start(f32[32,4,128]{2,1,0:T(4,128)} %refs_1_.1) | copy-start | bytes 196612
  44.1 21.1 %copy-start.4 = (s32[1,32,1]{1,2,0:T(1,128)S(1)}, s32[1,32,1]{1,2,0:T(1,128)}, u32[]{:S(2)}) copy-start(s32[1,32,1]{1,2,0:T(1,128)} %param.12) | copy-start | bytes 388
  44.1 21.1 %all-to-all-start.1 = ((bf16[32,48,128]{2,1,0:T(8,128)(2,1)}), bf16[32,48,128]{2,1,0:T(8,128)(2,1)S(1)}, u32[]{:S(2)}, u32[]{:S(2)}) async-start(bf16[32,48,128]{2,1,0:T(8,128)(2,1)} %shard_map.101), calls=%async_computation.1 | async-start | bytes 786432 | tf_op jit(solution)/shard_map/all_to_all | solution.py:474
  54.9 5.5 %collective-permute-start.4 = (f32[5,4,128]{2,1,0:T(4,128)S(1)}, f32[5,4,128]{2,1,0:T(4,128)S(1)}, u32[]{:S(2)}, u32[]{:S(2)}) collective-permute-start(f32[5,4,128]{2,1,0:T(4,128)S(1)} %get-tuple-element.21), channel_id=1, source_target_pairs={{0,1},{1,2},{2,3},{3,4},{4,5},{5,6},{6,7},{7,8},{8,9},{9,10},{10,1... | collective-permute-start | bytes 30728 | tf_op jit(solution)/shard_map/ppermute | solution.py:476
  58.4 5.3 %collective-permute-start.5 = (f32[5,4,128]{2,1,0:T(4,128)S(1)}, f32[5,4,128]{2,1,0:T(4,128)S(1)}, u32[]{:S(2)}, u32[]{:S(2)}) collective-permute-start(f32[5,4,128]{2,1,0:T(4,128)S(1)} %get-tuple-element.22), channel_id=1, source_target_pairs={{1,0},{2,1},{3,2},{4,3},{5,4},{6,5},{7,6},{8,7},{9,8},{10,9},{11,1... | collective-permute-start | bytes 30728 | tf_op jit(solution)/shard_map/ppermute | solution.py:477

commit v3 on v2

--- a/solution.py
+++ b/solution.py
@@ -8,16 +8,28 @@
 NF = 5
 ROWS_Y = 4
 LANES = 128
+HALF = NF * ROWS_Y
 PAIR = 48
-HALF = NF * ROWS_Y
-VMEM_LIMIT = 48 * 1024 * 1024
-COUPLE_VMEM = 62 * 1024 * 1024
+FLAGS = 40
+TAIL = 32
+VMEM_LIMIT = 65400 * 1024
 NT = (((1,), (1,)), ((), ()))
 
 
-def pack_kernel(planes, owners, holder_ref, own_ref, up_ref, down_ref, flow_ref, out_ref, plane_of, count):
-    g = lax.axis_index("grp")
-    gas_groups = lax.axis_size("grp") - 1
+def pack_kernel(
+    planes,
+    owners,
+    holder_ref,
+    flow_ref,
+    out_ref,
+    top_ref,
+    bottom_ref,
+    front_ref,
+    back_ref,
+    plane_of,
+    count,
+):
+    is_gas = lax.axis_index("grp") < lax.axis_size("grp") - 1
 
     def clear(p, carry):
         count[p] = 0
@@ -36,29 +48,22 @@
 
     lax.fori_loop(0, planes, place, 0, unroll=True)
 
-    owner_ids = lax.broadcasted_iota(jnp.int32, (owners, planes), 0)
-
-    def tally(ref):
-        hits = jnp.where(owner_ids == ref[...], 1.0, 0.0)
-        return jnp.broadcast_to(jnp.sum(hits, axis=1, keepdims=True), (owners, LANES))
-
-    own = jnp.where(g < gas_groups, tally(own_ref), 0.0)
-    above = tally(up_ref)
-    below = tally(down_ref)
-    total = own + above + below
-    before = jnp.where(g >= 1, above, 0.0) + jnp.where(g == gas_groups - 1, below, 0.0)
-    row = lax.broadcasted_iota(jnp.int32, (8, LANES), 0)
     for p in range(owners):
-        flags = jnp.where(
-            row == 0,
-            own[p : p + 1],
-            jnp.where(row == 1, before[p : p + 1], jnp.where(row == 2, total[p : p + 1], 0.0)),
-        )
         pieces = []
         for s in range(2):
             x = plane_of[2 * p + s]
             pieces += [flow_ref[f, x] for f in range(NF)]
-        out_ref[p] = jnp.concatenate(pieces + [flags], axis=0).astype(jnp.bfloat16)
+        number = jnp.where(is_gas, count[p], 0).astype(jnp.float32)
+        pieces.append(jnp.full((PAIR - FLAGS, LANES), number))
+        out_ref[p] = jnp.concatenate(pieces, axis=0).astype(jnp.bfloat16)
+
+    for f in range(NF):
+        for x in range(planes):
+            r = f * planes + x
+            top_ref[r : r + 1] = flow_ref[f, x, ROWS_Y - 1 :]
+            bottom_ref[r : r + 1] = flow_ref[f, x, :1]
+        front_ref[f] = flow_ref[f, 0]
+        back_ref[f] = flow_ref[f, planes - 1]
 
 
 def slot_relayout():
@@ -158,6 +163,9 @@
     live_ref,
     pick_ref,
     recv_ref,
+    above_ref,
+    below_ref,
+    far_ref,
     cell_hbm,
     motion_hbm,
     warmth_hbm,
@@ -193,14 +201,17 @@
     for copy in copies:
         copy.start()
 
-    before = jnp.zeros((8, LANES), jnp.float32)
-    total = jnp.zeros((8, LANES), jnp.float32)
+    g = lax.axis_index("grp")
     counts = []
     for t in range(owners):
-        flags = recv_ref[t, 32:48].astype(jnp.float32)
-        counts.append(jnp.broadcast_to(flags[8:9], (8, LANES)))
-        before = before + jnp.broadcast_to(flags[9:10], (8, LANES))
-        total = total + jnp.broadcast_to(flags[10:11], (8, LANES))
+        flags = recv_ref[t, TAIL:].astype(jnp.float32)[FLAGS - TAIL :]
+        counts.append(jnp.broadcast_to(flags[0:1], (8, LANES)))
+    gas_groups = lax.axis_size("grp") - 1
+    near_above = jnp.where(g >= 1, above_ref[...], 0.0)
+    near_below = jnp.where(g < gas_groups - 1, below_ref[...], 0.0)
+    far = jnp.where((g + 2) % lax.axis_size("grp") < gas_groups, far_ref[...], 0.0)
+    total = sum(counts) + near_above + near_below + far
+    before = near_above + jnp.where(g == gas_groups - 1, far, 0.0)
     divisor = jnp.maximum(total, 1.0)
     pick = pick_ref[...].astype(jnp.float32)
     quotient = (pick / divisor).astype(jnp.int32)
@@ -338,49 +349,61 @@
         out_ref[t] = jnp.dot(back, rows, preferred_element_type=jnp.float32).astype(jnp.bfloat16)
 
 
-def diffuse_kernel(planes, flow_ref, nu_ref, xlo_ref, xhi_ref, ylo_ref, yhi_ref, out_ref):
+def finish_kernel(
+    planes,
+    owners,
+    holder_ref,
+    flow_ref,
+    nu_ref,
+    xlo_ref,
+    xhi_ref,
+    up_ref,
+    down_ref,
+    landed_ref,
+    out_ref,
+    count,
+):
+    me = lax.axis_index("tile")
+    g = lax.axis_index("grp")
+    gas_groups = lax.axis_size("grp") - 1
     lane = lax.broadcasted_iota(jnp.int32, (ROWS_Y, LANES), 1)
-    for f in range(NF):
-        for x in range(planes):
+
+    def clear(p, carry):
+        count[p] = 0
+        return carry
+
+    lax.fori_loop(0, owners, clear, 0, unroll=True)
+
+    xlo = [jnp.where(me > 0, xlo_ref[f], 0.0) for f in range(NF)]
+    xhi = [jnp.where(me < owners - 1, xhi_ref[f], 0.0) for f in range(NF)]
+    for x in range(planes):
+        owner = holder_ref[x]
+        rank = count[owner]
+        count[owner] = rank + 1
+        pair = landed_ref[owner].astype(jnp.float32)
+        landed = jnp.where(rank == 0, pair[:HALF], pair[HALF : 2 * HALF])
+        for f in range(NF):
+            r = f * planes + x
             here = flow_ref[f, x]
-            left = xlo_ref[f] if x == 0 else flow_ref[f, x - 1]
-            right = xhi_ref[f] if x == planes - 1 else flow_ref[f, x + 1]
-            first = ylo_ref[f, x : x + 1]
-            last = yhi_ref[f, x : x + 1]
+            left = xlo[f] if x == 0 else flow_ref[f, x - 1]
+            right = xhi[f] if x == planes - 1 else flow_ref[f, x + 1]
+            first = jnp.where(g >= 1, up_ref[r : r + 1], 0.0)
+            last = jnp.where(g < gas_groups - 1, down_ref[r : r + 1], 0.0)
             lower = jnp.concatenate([first, here[: ROWS_Y - 1]], axis=0)
             upper = jnp.concatenate([here[1:], last], axis=0)
             back = jnp.where(lane == 0, 0.0, pltpu.roll(here, 1, 1))
             ahead = jnp.where(lane == LANES - 1, 0.0, pltpu.roll(here, LANES - 1, 1))
             laplace = right + left + upper + lower + ahead + back - 6.0 * here
-            out_ref[f, x] = here + 0.5 * nu_ref[x] * laplace
-
-
-def finish_kernel(planes, owners, holder_ref, adv_ref, recv_ref, out_ref, count):
-    g = lax.axis_index("grp")
-    keep = g < lax.axis_size("grp") - 1
-
-    def clear(p, carry):
-        count[p] = 0
-        return carry
-
-    lax.fori_loop(0, owners, clear, 0, unroll=True)
-    for x in range(planes):
-        owner = holder_ref[x]
-        rank = count[owner]
-        count[owner] = rank + 1
-        pair = recv_ref[owner].astype(jnp.float32)
-        landed = jnp.where(rank == 0, pair[:HALF], pair[HALF : 2 * HALF])
-        for f in range(NF):
-            value = adv_ref[f, x] + landed[ROWS_Y * f : ROWS_Y * f + ROWS_Y]
-            out_ref[f, x] = jnp.where(keep, value, 0.0)
-
-
-def couple_call(live, pick, arrived, cell, motion, warmth, mass, weight):
+            value = here + 0.5 * nu_ref[x] * laplace + landed[ROWS_Y * f : ROWS_Y * f + ROWS_Y]
+            out_ref[f, x] = jnp.where(g < gas_groups, value, 0.0)
+
+
+def couple_call(live, pick, arrived, above, below, far, cell, motion, warmth, mass, weight):
     owners, blocks = arrived.shape[0], cell.shape[0]
     vmem = pl.BlockSpec(memory_space=pltpu.VMEM)
     smem = pl.BlockSpec(memory_space=pltpu.SMEM)
     hbm = pl.BlockSpec(memory_space=pl.ANY)
-    params = pltpu.CompilerParams(vmem_limit_bytes=COUPLE_VMEM)
+    params = pltpu.CompilerParams(vmem_limit_bytes=VMEM_LIMIT)
     message = jax.ShapeDtypeStruct((owners, PAIR, LANES), jnp.bfloat16)
 
     def couple_body(*refs):
@@ -389,7 +412,7 @@
     return pl.pallas_call(
         couple_body,
         out_shape=message,
-        in_specs=[smem, vmem, vmem] + [hbm] * 5,
+        in_specs=[smem] + [vmem] * 5 + [hbm] * 5,
         out_specs=vmem,
         scratch_shapes=[
             pltpu.VMEM((blocks + 8, LANES), jnp.int32),
@@ -406,7 +429,7 @@
             pltpu.SemaphoreType.DMA((6,)),
         ],
         compiler_params=params,
-    )(live, pick, arrived, cell, motion.transpose(1, 0, 2), warmth, mass, weight)
+    )(live, pick, arrived, above, below, far, cell, motion.transpose(1, 0, 2), warmth, mass, weight)
 
 
 def local(
@@ -430,37 +453,46 @@
     params = pltpu.CompilerParams(vmem_limit_bytes=VMEM_LIMIT)
 
     holder = holder_unit.reshape(planes)
-    own_row = holder[None]
-
-    gas = groups - 1
-    round_up = [(i, (i + 1) % gas) for i in range(gas)]
-    up = lax.ppermute(own_row, "grp", round_up)
-    down = lax.ppermute(own_row, "grp", [(b, a) for a, b in round_up])
 
     def pack_body(*refs):
         pack_kernel(planes, owners, *refs)
 
-    packed = pl.pallas_call(
+    edge = jax.ShapeDtypeStruct((NF * planes, LANES), jnp.float32)
+    plane = jax.ShapeDtypeStruct((NF, ROWS_Y, LANES), jnp.float32)
+    packed, top, bottom, front, behind = pl.pallas_call(
         pack_body,
-        out_shape=jax.ShapeDtypeStruct((owners, PAIR, LANES), jnp.bfloat16),
-        in_specs=[smem] + [vmem] * 4,
-        out_specs=vmem,
+        out_shape=(
+            jax.ShapeDtypeStruct((owners, PAIR, LANES), jnp.bfloat16),
+            edge,
+            edge,
+            plane,
+            plane,
+        ),
+        in_specs=[smem, vmem],
+        out_specs=(vmem,) * 5,
         scratch_shapes=[pltpu.SMEM((2 * owners,), jnp.int32), pltpu.SMEM((owners,), jnp.int32)],
         compiler_params=params,
-    )(holder, own_row, up, down, flow_fields)
-
-    packed, top, bottom = lax.optimization_barrier(
-        (packed, flow_fields[:, :, ROWS_Y - 1], flow_fields[:, :, 0])
-    )
+    )(holder, flow_fields)
+
+    def turned(array, axis, step):
+        size = lax.axis_size(axis)
+        return lax.ppermute(array, axis, [(i, (i + step) % size) for i in range(size)])
+
     arrived = lax.all_to_all(packed, "tile", 0, 0, tiled=True)
-    up_grp = [(i, i + 1) for i in range(gas - 1)]
-    ylo = lax.ppermute(top, "grp", up_grp)
-    yhi = lax.ppermute(bottom, "grp", [(b, a) for a, b in up_grp])
-    arrived, ylo, yhi = lax.optimization_barrier((arrived, ylo, yhi))
+    xlo = turned(behind, "tile", 1)
+    xhi = turned(front, "tile", owners - 1)
+    arrived, xlo, xhi = lax.optimization_barrier((arrived, xlo, xhi))
+
+    number = jnp.sum(arrived[:, FLAGS:].astype(jnp.float32), axis=0)
+    above, far, below = (turned(number, "grp", k) for k in range(1, groups))
+
     outgoing = couple_call(
         living_spray_batches,
         patch_pick_unreduced.reshape(8, LANES),
         arrived,
+        above,
+        below,
+        far,
         spray_volume_position[0],
         droplet_motion[0],
         droplet_warmth[0],
@@ -468,36 +500,22 @@
         droplet_multiplicity[0],
     )
 
-    outgoing, back_plane, front_plane = lax.optimization_barrier(
-        (outgoing, flow_fields[:, planes - 1], flow_fields[:, 0])
-    )
+    outgoing, top, bottom = lax.optimization_barrier((outgoing, top, bottom))
     landed = lax.all_to_all(outgoing, "tile", 0, 0, tiled=True)
-    up_tile = [(i, i + 1) for i in range(owners - 1)]
-    xlo = lax.ppermute(back_plane, "tile", up_tile)
-    xhi = lax.ppermute(front_plane, "tile", [(b, a) for a, b in up_tile])
-
-    def diffuse_body(*refs):
-        diffuse_kernel(planes, *refs)
-
-    diffused = pl.pallas_call(
-        diffuse_body,
-        out_shape=jax.ShapeDtypeStruct(flow_fields.shape, jnp.float32),
-        in_specs=[vmem] * 6,
-        out_specs=vmem,
-        compiler_params=params,
-    )(flow_fields, turbulent_diffusivity, xlo, xhi, ylo, yhi)
-    landed, diffused = lax.optimization_barrier((landed, diffused))
+    up = turned(top, "grp", 1)
+    down = turned(bottom, "grp", groups - 1)
+
     def finish_body(*refs):
         finish_kernel(planes, owners, *refs)
 
     return pl.pallas_call(
         finish_body,
         out_shape=jax.ShapeDtypeStruct(flow_fields.shape, jnp.float32),
-        in_specs=[smem, vmem, vmem],
+        in_specs=[smem] + [vmem] * 7,
         out_specs=vmem,
         scratch_shapes=[pltpu.SMEM((owners,), jnp.int32)],
         compiler_params=params,
-    )(holder, diffused, landed)
+    )(holder, flow_fields, turbulent_diffusivity, xlo, xhi, up, down, landed)
 
 
 def solution(mesh):

time: 66.8 us -> 64.7 us (0.969)
  starting transfers between devices: 36.5 us -> 27.8 us
  waiting for transfers between devices: 14.2 us -> 18.5 us
  Pallas kernels: 11.5 us -> 15.5 us
  local copies, waits for them, and re-layouts: 3.64 us -> 1.36 us
    ppermute x6 -> x7, starting transfers between devices: 15.7 us -> 8.9 us  [turned(): lax.ppermute(array, axis, [(i, (i + step) % size) for i in range(size)])]
    all_to_all x1, waiting for transfers between devices: 1.04 us -> 5.02 us  [local(): landed = lax.all_to_all(outgoing, 'tile', 0, 0, tiled=True)]
    pallas_call x3 -> x2, Pallas kernels: 10.1 us -> 13 us  [the longest x1 10.8 us: couple_call(): pl.pallas_call(couple_body, out_shape=message, in_specs=[smem] + [vmem] *...]
    all_to_all x1, waiting for transfers between devices: 3.3 us -> 4.99 us  [local(): arrived = lax.all_to_all(packed, 'tile', 0, 0, tiled=True)]
    ppermute x6 -> x7, waiting for transfers between devices: 9.82 us -> 8.5 us  [turned(): lax.ppermute(array, axis, [(i, (i + step) % size) for i in range(size)])]
    all_to_all x1, starting transfers between devices: 10.8 us -> 9.46 us  [local(): landed = lax.all_to_all(outgoing, 'tile', 0, 0, tiled=True)]
    slice x1 -> x0, local copies, waits for them, and re-layouts: 1.24 us -> none  [local(): flow_fields[:, :, 0]]
    pallas_call x1, Pallas kernels: 1.44 us -> 2.52 us  [local(): pl.pallas_call(finish_body, out_shape=jax.ShapeDtypeStruct(flow_fields.sh...]
  transfers between devices with their start and end apart: 8 -> 9, of which waited for: 5 -> 7; matrix products, arithmetic and copies ran while one was open for 2% -> 0% of each run, Pallas kernels for 1% -> 0%
where the time goes in v3:
time: 64.7 us; the launch traced here: 63.9 us
  starting transfers between devices  27.8 us (43%)
  waiting for transfers between devices  18.5 us (29%)
  Pallas kernels  15.5 us (24%)
  local copies, waits for them, and re-layouts  1.36 us (2%)
  between operations  0.71 us (1%)
    pallas_call x1, Pallas kernels, couple_call(): pl.pallas_call(couple_body, out_shape=message, in_specs=[smem] + [vmem] *...  10.8 us
    all_to_all x1, starting transfers between devices, local(): landed = lax.all_to_all(outgoing, 'tile', 0, 0, tiled=True)  9.46 us
    all_to_all x1, starting transfers between devices, local(): arrived = lax.all_to_all(packed, 'tile', 0, 0, tiled=True)  9.43 us
    ppermute x7, starting transfers between devices, turned(): lax.ppermute(array, axis, [(i, (i + step) % size) for i in range(size)])  8.9 us
    ppermute x7, waiting for transfers between devices, turned(): lax.ppermute(array, axis, [(i, (i + step) % size) for i in range(size)])  8.5 us
    all_to_all x1, waiting for transfers between devices, local(): landed = lax.all_to_all(outgoing, 'tile', 0, 0, tiled=True)  5.02 us
    all_to_all x1, waiting for transfers between devices, local(): arrived = lax.all_to_all(packed, 'tile', 0, 0, tiled=True)  4.99 us
    pallas_call x1, Pallas kernels, local(): pl.pallas_call(finish_body, out_shape=jax.ShapeDtypeStruct(flow_fields.sh...  2.52 us
  transfers between devices with their start and end apart: 9, of which 7 were waited for; matrix products, arithmetic and copies ran while one was open for 0% of the time, Pallas kernels for 0%

profile of v3, /device:TPU:1, one launch (start us, length us, event | category | flops | bytes accessed | tf_op | source)
XLA Modules:
  0.0 63.9 jit_solution(14501452097713303870)
XLA Ops:
  0.0 2.2 %shard_map.100 = (bf16[32,48,128]{2,1,0:T(8,128)(2,1)}, f32[160,128]{1,0:T(8,128)}, f32[160,128]{1,0:T(8,128)}, f32[5,4,128]{2,1,0:T(4,128)}, f32[5,4,128]{2,1,0:T(4,128)}) custom-call(s32[32]{0:T(128)} %bitcast.15, f32[5,32,4,128]{3,2,1,0:T(4,128)} %refs_1_.3), custom_call_target="tpu_custom_call" | custom-call | tf_op jit(solution)/shard_map/pallas_call | solution.py:462
  2.2 9.4 %all-to-all-start = ((bf16[32,48,128]{2,1,0:T(8,128)(2,1)}), bf16[32,48,128]{2,1,0:T(8,128)(2,1)S(1)}, u32[]{:S(2)}, u32[]{:S(2)}) async-start(bf16[32,48,128]{2,1,0:T(8,128)(2,1)} %get-tuple-element.16), calls=%async_computation | async-start | bytes 786432 | tf_op jit(solution)/shard_map/all_to_all | solution.py:481
  11.7 1.7 %collective-permute-start = (f32[5,4,128]{2,1,0:T(4,128)}, f32[5,4,128]{2,1,0:T(4,128)S(1)}, u32[]{:S(2)}, u32[]{:S(2)}) collective-permute-start(f32[5,4,128]{2,1,0:T(4,128)} %get-tuple-element.17), channel_id=1, source_target_pairs={{0,1},{1,2},{2,3},{3,4},{4,5},{5,6},{6,7},{7,8},{8,9},{9,10},{10,1... | collective-permute-start | bytes 30728 | tf_op jit(solution)/shard_map/ppermute | solution.py:479
  13.4 0.0 collective-permute-start.1
  13.4 1.0 %collective-permute-done.refs_3_ = f32[5,4,128]{2,1,0:T(4,128)S(1)} collective-permute-done((f32[5,4,128]{2,1,0:T(4,128)}, f32[5,4,128]{2,1,0:T(4,128)S(1)}, u32[]{:S(2)}, u32[]{:S(2)}) %collective-permute-start) | collective-permute-done | bytes 10272 | tf_op jit(solution)/shard_map/ppermute | solution.py:479
  14.4 0.0 copy-start.1
  14.4 2.6 %collective-permute-done.1.refs_4_ = f32[5,4,128]{2,1,0:T(4,128)S(1)} collective-permute-done((f32[5,4,128]{2,1,0:T(4,128)}, f32[5,4,128]{2,1,0:T(4,128)S(1)}, u32[]{:S(2)}, u32[]{:S(2)}) %collective-permute-start.1) | collective-permute-done | bytes 10272 | tf_op jit(solution)/shard_map/ppermute | solution.py:479
  17.0 0.0 copy-start.2
  17.0 5.0 %all-to-all-done.refs_2_ = bf16[32,48,128]{2,1,0:T(8,128)(2,1)S(1)} async-done(((bf16[32,48,128]{2,1,0:T(8,128)(2,1)}), bf16[32,48,128]{2,1,0:T(8,128)(2,1)S(1)}, u32[]{:S(2)}, u32[]{:S(2)}) %all-to-all-start) | async-done | bytes 393248 | tf_op jit(solution)/shard_map/all_to_all | solution.py:481
  22.0 0.0 copy-start
  22.0 0.8 %copy-done = bf16[32,48,128]{2,1,0:T(8,128)(2,1)} copy-done((bf16[32,48,128]{2,1,0:T(8,128)(2,1)}, bf16[32,48,128]{2,1,0:T(8,128)(2,1)S(1)}, u32[]{:S(2)}) %copy-start) | copy-done | bytes 393240
  22.8 3.0 %collective-permute-start.4 = (f32[8,128]{1,0:T(8,128)S(1)}, f32[8,128]{1,0:T(8,128)S(1)}, u32[]{:S(2)}, u32[]{:S(2)}) collective-permute-start(f32[8,128]{1,0:T(8,128)S(1)} %convert_reduce_fusion), channel_id=1, source_target_pairs={{0,64},{32,96},{64,0},{96,32},{1,65},{33,97},{65,1},{97,33},{2,66}... | collective-permute-start | bytes 12296 | tf_op jit(solution)/shard_map/ppermute | solution.py:479
  25.7 0.8 %collective-permute-start.3 = (f32[8,128]{1,0:T(8,128)S(1)}, f32[8,128]{1,0:T(8,128)S(1)}, u32[]{:S(2)}, u32[]{:S(2)}) collective-permute-start(f32[8,128]{1,0:T(8,128)S(1)} %convert_reduce_fusion), channel_id=1, source_target_pairs={{0,96},{32,0},{64,32},{96,64},{1,97},{33,1},{65,33},{97,65},{2,98}... | collective-permute-start | bytes 12296 | tf_op jit(solution)/shard_map/ppermute | solution.py:479
  26.5 0.7 %collective-permute-start.2 = (f32[8,128]{1,0:T(8,128)S(1)}, f32[8,128]{1,0:T(8,128)S(1)}, u32[]{:S(2)}, u32[]{:S(2)}) collective-permute-start(f32[8,128]{1,0:T(8,128)S(1)} %convert_reduce_fusion), channel_id=1, source_target_pairs={{0,32},{32,64},{64,96},{96,0},{1,33},{33,65},{65,97},{97,1},{2,34}... | collective-permute-start | bytes 12296 | tf_op jit(solution)/shard_map/ppermute | solution.py:479
  27.9 0.0 collective-permute-done.4.refs_5_
  27.9 0.0 copy-start.3
  27.9 0.3 collective-permute-done.3.refs_4_
  28.2 0.0 copy-start.4
  28.2 2.0 %collective-permute-done.2.refs_3_ = f32[8,128]{1,0:T(8,128)S(1)} collective-permute-done((f32[8,128]{1,0:T(8,128)S(1)}, f32[8,128]{1,0:T(8,128)S(1)}, u32[]{:S(2)}, u32[]{:S(2)}) %collective-permute-start.2) | collective-permute-done | bytes 4128 | tf_op jit(solution)/shard_map/ppermute | solution.py:479
  30.2 0.0 copy-start.5
  30.2 0.0 copy-done.3
  30.2 0.0 copy-done.4
  30.2 0.6 copy-done.5
  30.8 10.8 %shard_map.101 = bf16[32,48,128]{2,1,0:T(8,128)(2,1)} custom-call(s32[1]{0:T(128)S(6)} %copy.11.refs_0_, s32[8,128]{1,0:T(8,128)} %bitcast.14, bf16[32,48,128]{2,1,0:T(8,128)(2,1)} %copy-done, f32[8,128]{1,0:T(8,128)} %copy-done.5, f32[8,128]{1,0:T(8,128)} %copy-done.4, f32[8,128]{1,0:T(8,128)} %copy-done.3, s32[1024,128]{1,0:T(8,128)} %bitcast.10, ...), custom_call_target="tpu_custom_call" | custom-call | tf_op jit(solution)/shard_map/pallas_call | solution.py:412
  41.6 9.5 %all-to-all-start.1 = ((bf16[32,48,128]{2,1,0:T(8,128)(2,1)}), bf16[32,48,128]{2,1,0:T(8,128)(2,1)}, u32[]{:S(2)}, u32[]{:S(2)}) async-start(bf16[32,48,128]{2,1,0:T(8,128)(2,1)} %shard_map.101), calls=%async_computation.1 | async-start | bytes 786432 | tf_op jit(solution)/shard_map/all_to_all | solution.py:504
  51.1 0.2 collective-permute-start.5
  51.3 2.5 %collective-permute-start.6 = (f32[160,128]{1,0:T(8,128)}, f32[160,128]{1,0:T(8,128)}, u32[]{:S(2)}, u32[]{:S(2)}) collective-permute-start(f32[160,128]{1,0:T(8,128)} %get-tuple-element.25), channel_id=1, source_target_pairs={{0,96},{32,0},{64,32},{96,64},{1,97},{33,1},{65,33},{97,65},{2,98}... | collective-permute-start | bytes 245768 | tf_op jit(solution)/shard_map/ppermute | solution.py:479
  53.8 2.6 %collective-permute-done.5.refs_5_ = f32[160,128]{1,0:T(8,128)} collective-permute-done((f32[160,128]{1,0:T(8,128)}, f32[160,128]{1,0:T(8,128)}, u32[]{:S(2)}, u32[]{:S(2)}) %collective-permute-start.5) | collective-permute-done | bytes 81952 | tf_op jit(solution)/shard_map/ppermute | solution.py:479
  56.4 0.0 collective-permute-done.6.refs_6_
  56.4 5.0 %all-to-all-done.1.refs_7_ = bf16[32,48,128]{2,1,0:T(8,128)(2,1)} async-done(((bf16[32,48,128]{2,1,0:T(8,128)(2,1)}), bf16[32,48,128]{2,1,0:T(8,128)(2,1)}, u32[]{:S(2)}, u32[]{:S(2)}) %all-to-all-start.1) | async-done | bytes 393248 | tf_op jit(solution)/shard_map/all_to_all | solution.py:504
  61.4 0.0 copy-done.1
  61.4 0.0 copy-done.2
  61.4 2.5 %shard_map.102 = f32[5,32,4,128]{3,2,1,0:T(4,128)} custom-call(s32[32]{0:T(128)} %bitcast.16, f32[5,32,4,128]{3,2,1,0:T(4,128)} %refs_1_.3, f32[32,4,128]{2,1,0:T(4,128)} %refs_2_.1, f32[5,4,128]{2,1,0:T(4,128)} %copy-done.1, f32[5,4,128]{2,1,0:T(4,128)} %copy-done.2, f32[160,128]{1,0:T(8,128)} %collective-permute-done.5.refs_5_, ...), custom_call_target="tpu_custom_call" | custom-call | tf_op jit(solution)/shard_map/pallas_call | solution.py:511
  (1 shorter events, 0.0 us)
Async XLA Ops:
  2.2 19.7 %all-to-all-start = ((bf16[32,48,128]{2,1,0:T(8,128)(2,1)}), bf16[32,48,128]{2,1,0:T(8,128)(2,1)S(1)}, u32[]{:S(2)}, u32[]{:S(2)}) async-start(bf16[32,48,128]{2,1,0:T(8,128)(2,1)} %get-tuple-element.16), calls=%async_computation | async-start | bytes 786432 | tf_op jit(solution)/shard_map/all_to_all | solution.py:481
  11.7 2.7 %collective-permute-start = (f32[5,4,128]{2,1,0:T(4,128)}, f32[5,4,128]{2,1,0:T(4,128)S(1)}, u32[]{:S(2)}, u32[]{:S(2)}) collective-permute-start(f32[5,4,128]{2,1,0:T(4,128)} %get-tuple-element.17), channel_id=1, source_target_pairs={{0,1},{1,2},{2,3},{3,4},{4,5},{5,6},{6,7},{7,8},{8,9},{9,10},{10,1... | collective-permute-start | bytes 30728 | tf_op jit(solution)/shard_map/ppermute | solution.py:479
  13.4 3.6 %collective-permute-start.1 = (f32[5,4,128]{2,1,0:T(4,128)}, f32[5,4,128]{2,1,0:T(4,128)S(1)}, u32[]{:S(2)}, u32[]{:S(2)}) collective-permute-start(f32[5,4,128]{2,1,0:T(4,128)} %get-tuple-element.18), channel_id=1, source_target_pairs={{0,31},{1,0},{2,1},{3,2},{4,3},{5,4},{6,5},{7,6},{8,7},{9,8},{10,9... | collective-permute-start | bytes 30728 | tf_op jit(solution)/shard_map/ppermute | solution.py:479
  14.4 47.0 %copy-start.1 = (f32[5,4,128]{2,1,0:T(4,128)}, f32[5,4,128]{2,1,0:T(4,128)S(1)}, u32[]{:S(2)}) copy-start(f32[5,4,128]{2,1,0:T(4,128)S(1)} %collective-permute-done.refs_3_) | copy-start | bytes 30724
  17.0 44.4 %copy-start.2 = (f32[5,4,128]{2,1,0:T(4,128)}, f32[5,4,128]{2,1,0:T(4,128)S(1)}, u32[]{:S(2)}) copy-start(f32[5,4,128]{2,1,0:T(4,128)S(1)} %collective-permute-done.1.refs_4_) | copy-start | bytes 30724
  22.0 0.8 %copy-start = (bf16[32,48,128]{2,1,0:T(8,128)(2,1)}, bf16[32,48,128]{2,1,0:T(8,128)(2,1)S(1)}, u32[]{:S(2)}) copy-start(bf16[32,48,128]{2,1,0:T(8,128)(2,1)S(1)} %all-to-all-done.refs_2_) | copy-start | bytes 1179652
  22.8 5.1 %collective-permute-start.4 = (f32[8,128]{1,0:T(8,128)S(1)}, f32[8,128]{1,0:T(8,128)S(1)}, u32[]{:S(2)}, u32[]{:S(2)}) collective-permute-start(f32[8,128]{1,0:T(8,128)S(1)} %convert_reduce_fusion), channel_id=1, source_target_pairs={{0,64},{32,96},{64,0},{96,32},{1,65},{33,97},{65,1},{97,33},{2,66}... | collective-permute-start | bytes 12296 | tf_op jit(solution)/shard_map/ppermute | solution.py:479
  25.7 2.5 %collective-permute-start.3 = (f32[8,128]{1,0:T(8,128)S(1)}, f32[8,128]{1,0:T(8,128)S(1)}, u32[]{:S(2)}, u32[]{:S(2)}) collective-permute-start(f32[8,128]{1,0:T(8,128)S(1)} %convert_reduce_fusion), channel_id=1, source_target_pairs={{0,96},{32,0},{64,32},{96,64},{1,97},{33,1},{65,33},{97,65},{2,98}... | collective-permute-start | bytes 12296 | tf_op jit(solution)/shard_map/ppermute | solution.py:479
  26.5 3.7 %collective-permute-start.2 = (f32[8,128]{1,0:T(8,128)S(1)}, f32[8,128]{1,0:T(8,128)S(1)}, u32[]{:S(2)}, u32[]{:S(2)}) collective-permute-start(f32[8,128]{1,0:T(8,128)S(1)} %convert_reduce_fusion), channel_id=1, source_target_pairs={{0,32},{32,64},{64,96},{96,0},{1,33},{33,65},{65,97},{97,1},{2,34}... | collective-permute-start | bytes 12296 | tf_op jit(solution)/shard_map/ppermute | solution.py:479
  27.9 2.3 %copy-start.3 = (f32[8,128]{1,0:T(8,128)}, f32[8,128]{1,0:T(8,128)S(1)}, u32[]{:S(2)}) copy-start(f32[8,128]{1,0:T(8,128)S(1)} %collective-permute-done.4.refs_5_) | copy-start | bytes 12292
  28.2 2.0 %copy-start.4 = (f32[8,128]{1,0:T(8,128)}, f32[8,128]{1,0:T(8,128)S(1)}, u32[]{:S(2)}) copy-start(f32[8,128]{1,0:T(8,128)S(1)} %collective-permute-done.3.refs_4_) | copy-start | bytes 12292
  30.2 0.6 copy-start.5
  41.6 19.8 %all-to-all-start.1 = ((bf16[32,48,128]{2,1,0:T(8,128)(2,1)}), bf16[32,48,128]{2,1,0:T(8,128)(2,1)}, u32[]{:S(2)}, u32[]{:S(2)}) async-start(bf16[32,48,128]{2,1,0:T(8,128)(2,1)} %shard_map.101), calls=%async_computation.1 | async-start | bytes 786432 | tf_op jit(solution)/shard_map/all_to_all | solution.py:504
  51.1 5.3 %collective-permute-start.5 = (f32[160,128]{1,0:T(8,128)}, f32[160,128]{1,0:T(8,128)}, u32[]{:S(2)}, u32[]{:S(2)}) collective-permute-start(f32[160,128]{1,0:T(8,128)} %get-tuple-element.24), channel_id=1, source_target_pairs={{0,32},{32,64},{64,96},{96,0},{1,33},{33,65},{65,97},{97,1},{2,34}... | collective-permute-start | bytes 245768 | tf_op jit(solution)/shard_map/ppermute | solution.py:479
  51.3 5.1 %collective-permute-start.6 = (f32[160,128]{1,0:T(8,128)}, f32[160,128]{1,0:T(8,128)}, u32[]{:S(2)}, u32[]{:S(2)}) collective-permute-start(f32[160,128]{1,0:T(8,128)} %get-tuple-element.25), channel_id=1, source_target_pairs={{0,96},{32,0},{64,32},{96,64},{1,97},{33,1},{65,33},{97,65},{2,98}... | collective-permute-start | bytes 245768 | tf_op jit(solution)/shard_map/ppermute | solution.py:479

commit v4 on v3

--- a/solution.py
+++ b/solution.py
@@ -103,7 +103,7 @@
     return out
 
 
-UA, UB, UC = 32, 32, 32
+STEP = 32
 ENTRY_BITS = 11
 ENTRY = 1 << ENTRY_BITS
 
@@ -127,7 +127,7 @@
     ahead = jnp.dot(before, halves.astype(jnp.bfloat16), preferred_element_type=jnp.float32)
     start = 2.0 * (16.0 * ahead[:, :lanes] + ahead[:, lanes:])
     number = start[slots - 1 :].astype(jnp.int32) + 2 * pairs[slots - 1 :]
-    carry = start - 1.0
+    carry = start + (2 * STEP - 1.0)
     low = lax.broadcasted_iota(jnp.int32, (lanes, lanes), 0)
     high = lax.broadcasted_iota(jnp.int32, (16, lanes), 0)
     lane = lax.broadcasted_iota(jnp.int32, (16, lanes), 1).astype(jnp.float32)
@@ -183,6 +183,7 @@
     code_s,
     seen,
     gathered,
+    source,
     sems,
 ):
     slots = 2 * owners
@@ -256,81 +257,67 @@
 
     lax.fori_loop(0, owners, clear, 0)
     deposit[4 * slots : 4 * slots + 4] = jnp.zeros((4, 8, LANES), jnp.float32)
+    source[...] = jnp.zeros_like(source)
     to_scalar.wait()
 
     found = code_s[15, 0]
     for copy in copies:
         copy.wait()
 
-    sub = lax.broadcasted_iota(jnp.int32, (8, LANES), 0)
-
     def entry(n0, i):
         code = code_s[n0 >> 7, (n0 & (LANES - 1)) + i]
         return code & (ENTRY - 1), code >> ENTRY_BITS
 
-    def look_up(j, carry):
-        n0 = UA * j
-        for i in range(0, UA, 2):
+    cell_row = lax.broadcasted_iota(jnp.int32, (LANES, LANES), 0).astype(jnp.float32).astype(jnp.bfloat16)
+
+    def look_up(j):
+        n0 = STEP * j
+        for i in range(0, STEP, 2):
             slot = entry(n0, i)[1]
             tile = [table[4 * slot + k] for k in range(ROWS_Y)]
             for h in range(2):
-                n = n0 + i + h
                 b = entry(n0, i + h)[0]
                 around = jnp.broadcast_to(cell[pl.ds(b, 1), :], (8, LANES))
                 z, y = around & (LANES - 1), around >> 7
                 rows = [jnp.take_along_axis(tile[k], z, axis=1) for k in range(ROWS_Y)]
-                seen[n] = jnp.where(
+                seen[i + h] = jnp.where(
                     y == 0, rows[0], jnp.where(y == 1, rows[1], jnp.where(y == 2, rows[2], rows[3]))
                 )
-        for i in range(UA):
-            n = n0 + i
-            b = entry(n0, i)[0]
-            for k in range(3):
-                gathered[k, pl.ds(n, 1), :] = motion[k, pl.ds(b, 1), :]
-            gathered[3, pl.ds(n, 1), :] = warmth[pl.ds(b, 1), :]
-            gathered[4, pl.ds(n, 1), :] = mass[pl.ds(b, 1), :]
-            gathered[5, pl.ds(n, 1), :] = weight[pl.ds(b, 1), :]
-        return carry
-
-    lax.fori_loop(0, (found + UA - 1) // UA, look_up, 0)
-
-    def move(j, carry):
-        at = pl.multiple_of(UB * j, UB)
-        rows = pl.ds(at, UB)
-        gas = [seen[rows, f, :] for f in range(NF)]
+                for k in range(3):
+                    gathered[k, i + h : i + h + 1, :] = motion[k, pl.ds(b, 1), :]
+                gathered[3, i + h : i + h + 1, :] = warmth[pl.ds(b, 1), :]
+                gathered[4, i + h : i + h + 1, :] = mass[pl.ds(b, 1), :]
+                gathered[5, i + h : i + h + 1, :] = weight[pl.ds(b, 1), :]
+
+    def move():
+        gas = [seen[:, f, :] for f in range(NF)]
         sources = coupling(
             gas,
-            [gathered[k, rows, :] for k in range(3)],
-            gathered[3, rows, :],
-            gathered[4, rows, :],
-            gathered[5, rows, :],
+            [gathered[k] for k in range(3)],
+            gathered[3],
+            gathered[4],
+            gathered[5],
         )
         for f in range(NF):
-            seen[rows, f, :] = sources[f]
-        return carry
-
-    lax.fori_loop(0, (found + UB - 1) // UB, move, 0)
-
-    cell_row = lax.broadcasted_iota(jnp.int32, (LANES, LANES), 0)
-
-    def scatter(j, carry):
-        n0 = UC * j
-        for i in range(0, UC, 2):
+            source[:, f, :] = sources[f]
+
+    def scatter(j):
+        n0 = STEP * j
+        for i in range(0, STEP, 2):
             slot = entry(n0, i)[1]
             parts, hots = [], []
             for h in range(2):
-                n = n0 + i + h
                 b = entry(n0, i + h)[0]
                 cells = cell[pl.ds(b, 1), :]
                 y = jnp.broadcast_to(cells, (8, LANES)) >> 7
-                part = seen[n]
+                part = source[i + h]
                 parts.append(
                     jnp.concatenate(
                         [jnp.where(y == k, part, 0.0) for k in range(ROWS_Y)], axis=0
                     ).astype(jnp.bfloat16)
                 )
                 hots.append(
-                    jnp.where(cell_row == (cells & (LANES - 1)), 1.0, 0.0).astype(jnp.bfloat16)
+                    jnp.where(cell_row == (cells & (LANES - 1)).astype(jnp.float32).astype(jnp.bfloat16), jnp.bfloat16(1), jnp.bfloat16(0))
                 )
             added = lax.dot_general(
                 jnp.concatenate(parts, axis=1),
@@ -339,9 +326,14 @@
                 preferred_element_type=jnp.float32,
             ).reshape(4, 8, LANES)
             deposit[pl.ds(4 * slot, 4)] = deposit[pl.ds(4 * slot, 4)] + added
+
+    def advance(j, carry):
+        scatter(j)
+        move()
+        look_up(j + 2)
         return carry
 
-    lax.fori_loop(0, (found + UC - 1) // UC, scatter, 0)
+    lax.fori_loop(0, (found + STEP - 1) // STEP + 2, advance, 0)
 
     back = slot_relayout_back()
     for t in range(owners):
@@ -403,7 +395,7 @@
     vmem = pl.BlockSpec(memory_space=pltpu.VMEM)
     smem = pl.BlockSpec(memory_space=pltpu.SMEM)
     hbm = pl.BlockSpec(memory_space=pl.ANY)
-    params = pltpu.CompilerParams(vmem_limit_bytes=VMEM_LIMIT)
+    params = pltpu.CompilerParams(vmem_limit_bytes=64136 * 1024)
     message = jax.ShapeDtypeStruct((owners, PAIR, LANES), jnp.bfloat16)
 
     def couple_body(*refs):
@@ -424,8 +416,9 @@
             pltpu.VMEM((8 * owners + 4, 8, LANES), jnp.float32),
             pltpu.VMEM((16, LANES), jnp.int32),
             pltpu.SMEM((16, LANES), jnp.int32),
-            pltpu.VMEM((blocks + 96, 8, LANES), jnp.float32),
-            pltpu.VMEM((6, blocks + 96, LANES), jnp.float32),
+            pltpu.VMEM((STEP, 8, LANES), jnp.float32),
+            pltpu.VMEM((6, STEP, LANES), jnp.float32),
+            pltpu.VMEM((STEP, 8, LANES), jnp.float32),
             pltpu.SemaphoreType.DMA((6,)),
         ],
         compiler_params=params,
@@ -514,7 +507,7 @@
         in_specs=[smem] + [vmem] * 7,
         out_specs=vmem,
         scratch_shapes=[pltpu.SMEM((owners,), jnp.int32)],
-        compiler_params=params,
+        compiler_params=pltpu.CompilerParams(vmem_limit_bytes=40 * 1024 * 1024),
     )(holder, flow_fields, turbulent_diffusivity, xlo, xhi, up, down, landed)
 
 

time: 64.7 us -> 58.7 us (0.907)
  Pallas kernels: 15.5 us -> 10.8 us
  local copies, waits for them, and re-layouts: 1.36 us -> 0.61 us
    pallas_call x1, Pallas kernels: 10.8 us -> 6.77 us  [couple_call(): pl.pallas_call(couple_body, out_shape=message, in_specs=[smem] + [vmem] *...]
    unnamed x12 -> x18, local copies, waits for them, and re-layouts: 1.36 us -> 0.61 us
    pallas_call x1, Pallas kernels: 2.52 us -> 1.82 us  [local(): pl.pallas_call(finish_body, out_shape=jax.ShapeDtypeStruct(flow_fields.sh...]
where the time goes in v4:
time: 58.7 us; the launch traced here: 58 us
  starting transfers between devices  27.4 us (47%)
  waiting for transfers between devices  18.5 us (32%)
  Pallas kernels  10.8 us (18%)
  between operations  0.75 us (1%)
  local copies, waits for them, and re-layouts  0.61 us (1%)
    all_to_all x1, starting transfers between devices, local(): arrived = lax.all_to_all(packed, 'tile', 0, 0, tiled=True)  9.43 us
    all_to_all x1, starting transfers between devices, local(): landed = lax.all_to_all(outgoing, 'tile', 0, 0, tiled=True)  9.09 us
    ppermute x7, starting transfers between devices, turned(): lax.ppermute(array, axis, [(i, (i + step) % size) for i in range(size)])  8.89 us
    ppermute x7, waiting for transfers between devices, turned(): lax.ppermute(array, axis, [(i, (i + step) % size) for i in range(size)])  8.26 us
    pallas_call x1, Pallas kernels, couple_call(): pl.pallas_call(couple_body, out_shape=message, in_specs=[smem] + [vmem] *...  6.77 us
    all_to_all x1, waiting for transfers between devices, local(): landed = lax.all_to_all(outgoing, 'tile', 0, 0, tiled=True)  5.2 us
    all_to_all x1, waiting for transfers between devices, local(): arrived = lax.all_to_all(packed, 'tile', 0, 0, tiled=True)  4.99 us
    pallas_call x1, Pallas kernels, local(): pl.pallas_call(pack_body, out_shape=(jax.ShapeDtypeStruct((owners, PAIR,...  2.2 us
  transfers between devices with their start and end apart: 9, of which 7 were waited for; matrix products, arithmetic and copies ran while one was open for 0% of the time, Pallas kernels for 0%

profile of v4, /device:TPU:1, one launch (start us, length us, event | category | flops | bytes accessed | tf_op | source)
XLA Modules:
  0.0 58.0 jit_solution(17432692676309805114)
XLA Ops:
  0.0 2.2 %shard_map.100 = (bf16[32,48,128]{2,1,0:T(8,128)(2,1)}, f32[160,128]{1,0:T(8,128)}, f32[160,128]{1,0:T(8,128)}, f32[5,4,128]{2,1,0:T(4,128)}, f32[5,4,128]{2,1,0:T(4,128)}) custom-call(s32[32]{0:T(128)} %bitcast.9, f32[5,32,4,128]{3,2,1,0:T(4,128)} %refs_1_.3), custom_call_target="tpu_custom_call" | custom-call | tf_op jit(solution)/shard_map/pallas_call | solution.py:455
  2.2 9.4 %all-to-all-start = ((bf16[32,48,128]{2,1,0:T(8,128)(2,1)}), bf16[32,48,128]{2,1,0:T(8,128)(2,1)S(1)}, u32[]{:S(2)}, u32[]{:S(2)}) async-start(bf16[32,48,128]{2,1,0:T(8,128)(2,1)} %get-tuple-element.16), calls=%async_computation | async-start | bytes 786432 | tf_op jit(solution)/shard_map/all_to_all | solution.py:474
  11.6 1.7 %collective-permute-start = (f32[5,4,128]{2,1,0:T(4,128)}, f32[5,4,128]{2,1,0:T(4,128)S(1)}, u32[]{:S(2)}, u32[]{:S(2)}) collective-permute-start(f32[5,4,128]{2,1,0:T(4,128)} %get-tuple-element.17), channel_id=1, source_target_pairs={{0,1},{1,2},{2,3},{3,4},{4,5},{5,6},{6,7},{7,8},{8,9},{9,10},{10,1... | collective-permute-start | bytes 30728 | tf_op jit(solution)/shard_map/ppermute | solution.py:472
  13.3 0.0 collective-permute-start.1
  13.3 1.0 %collective-permute-done.refs_3_ = f32[5,4,128]{2,1,0:T(4,128)S(1)} collective-permute-done((f32[5,4,128]{2,1,0:T(4,128)}, f32[5,4,128]{2,1,0:T(4,128)S(1)}, u32[]{:S(2)}, u32[]{:S(2)}) %collective-permute-start) | collective-permute-done | bytes 10272 | tf_op jit(solution)/shard_map/ppermute | solution.py:472
  14.4 2.6 %collective-permute-done.1.refs_4_ = f32[5,4,128]{2,1,0:T(4,128)S(1)} collective-permute-done((f32[5,4,128]{2,1,0:T(4,128)}, f32[5,4,128]{2,1,0:T(4,128)S(1)}, u32[]{:S(2)}, u32[]{:S(2)}) %collective-permute-start.1) | collective-permute-done | bytes 10272 | tf_op jit(solution)/shard_map/ppermute | solution.py:472
  17.0 5.0 %all-to-all-done.refs_2_ = bf16[32,48,128]{2,1,0:T(8,128)(2,1)S(1)} async-done(((bf16[32,48,128]{2,1,0:T(8,128)(2,1)}), bf16[32,48,128]{2,1,0:T(8,128)(2,1)S(1)}, u32[]{:S(2)}, u32[]{:S(2)}) %all-to-all-start) | async-done | bytes 393248 | tf_op jit(solution)/shard_map/all_to_all | solution.py:474
  21.9 0.0 copy-start.3
  22.0 3.0 %collective-permute-start.4 = (f32[8,128]{1,0:T(8,128)S(1)}, f32[8,128]{1,0:T(8,128)S(1)}, u32[]{:S(2)}, u32[]{:S(2)}) collective-permute-start(f32[8,128]{1,0:T(8,128)S(1)} %convert_reduce_fusion), channel_id=1, source_target_pairs={{0,64},{32,96},{64,0},{96,32},{1,65},{33,97},{65,1},{97,33},{2,66}... | collective-permute-start | bytes 12296 | tf_op jit(solution)/shard_map/ppermute | solution.py:472
  25.0 0.8 %collective-permute-start.3 = (f32[8,128]{1,0:T(8,128)S(1)}, f32[8,128]{1,0:T(8,128)S(1)}, u32[]{:S(2)}, u32[]{:S(2)}) collective-permute-start(f32[8,128]{1,0:T(8,128)S(1)} %convert_reduce_fusion), channel_id=1, source_target_pairs={{0,96},{32,0},{64,32},{96,64},{1,97},{33,1},{65,33},{97,65},{2,98}... | collective-permute-start | bytes 12296 | tf_op jit(solution)/shard_map/ppermute | solution.py:472
  25.7 0.7 %collective-permute-start.2 = (f32[8,128]{1,0:T(8,128)S(1)}, f32[8,128]{1,0:T(8,128)S(1)}, u32[]{:S(2)}, u32[]{:S(2)}) collective-permute-start(f32[8,128]{1,0:T(8,128)S(1)} %convert_reduce_fusion), channel_id=1, source_target_pairs={{0,32},{32,64},{64,96},{96,0},{1,33},{33,65},{65,97},{97,1},{2,34}... | collective-permute-start | bytes 12296 | tf_op jit(solution)/shard_map/ppermute | solution.py:472
  27.1 0.0 collective-permute-done.4.refs_5_
  27.1 0.0 copy-start.4
  27.1 0.3 collective-permute-done.3.refs_4_
  27.4 0.0 copy-start.5
  27.4 2.0 %collective-permute-done.2.refs_3_ = f32[8,128]{1,0:T(8,128)S(1)} collective-permute-done((f32[8,128]{1,0:T(8,128)S(1)}, f32[8,128]{1,0:T(8,128)S(1)}, u32[]{:S(2)}, u32[]{:S(2)}) %collective-permute-start.2) | collective-permute-done | bytes 4128 | tf_op jit(solution)/shard_map/ppermute | solution.py:472
  29.4 0.0 copy-start.6
  29.4 0.0 copy-done.3
  29.4 0.0 copy-done.4
  29.4 0.0 copy-done.5
  29.4 0.6 copy-done.6
  30.0 0.0 copy-start.8
  30.0 0.0 copy-start.7
  30.0 0.0 copy-start
  30.0 0.0 copy-start.1
  30.0 0.0 copy-start.2
  30.0 6.8 %shard_map.101 = bf16[32,48,128]{2,1,0:T(8,128)(2,1)} custom-call(s32[1]{0:T(128)S(6)} %copy.11.refs_0_, s32[8,128]{1,0:T(8,128)} %bitcast.16, bf16[32,48,128]{2,1,0:T(8,128)(2,1)} %copy-done.3, f32[8,128]{1,0:T(8,128)} %copy-done.6, f32[8,128]{1,0:T(8,128)} %copy-done.5, f32[8,128]{1,0:T(8,128)} %copy-done.4, s32[1024,128]{1,0:T(8,128)} %bitcast.12, ...), custom_call_target="tpu_custom_call" | custom-call | tf_op jit(solution)/shard_map/pallas_call | solution.py:404
  36.8 9.1 %all-to-all-start.1 = ((bf16[32,48,128]{2,1,0:T(8,128)(2,1)}), bf16[32,48,128]{2,1,0:T(8,128)(2,1)S(1)}, u32[]{:S(2)}, u32[]{:S(2)}) async-start(bf16[32,48,128]{2,1,0:T(8,128)(2,1)} %shard_map.101), calls=%async_computation.1 | async-start | bytes 786432 | tf_op jit(solution)/shard_map/all_to_all | solution.py:497
  45.9 0.0 copy-done.8
  45.9 0.1 collective-permute-start.5
  46.0 0.0 copy-done.7
  46.0 2.7 %collective-permute-start.6 = (f32[160,128]{1,0:T(8,128)S(1)}, f32[160,128]{1,0:T(8,128)S(1)}, u32[]{:S(2)}, u32[]{:S(2)}) collective-permute-start(f32[160,128]{1,0:T(8,128)S(1)} %copy-done.7), channel_id=1, source_target_pairs={{0,96},{32,0},{64,32},{96,64},{1,97},{33,1},{65,33},{97,65},{2,98}... | collective-permute-start | bytes 245768 | tf_op jit(solution)/shard_map/ppermute | solution.py:472
  48.7 2.3 %collective-permute-done.5.refs_5_ = f32[160,128]{1,0:T(8,128)S(1)} collective-permute-done((f32[160,128]{1,0:T(8,128)S(1)}, f32[160,128]{1,0:T(8,128)S(1)}, u32[]{:S(2)}, u32[]{:S(2)}) %collective-permute-start.5) | collective-permute-done | bytes 81952 | tf_op jit(solution)/shard_map/ppermute | solution.py:472
  51.0 0.0 collective-permute-done.6.refs_6_
  51.0 5.2 %all-to-all-done.1.refs_7_ = bf16[32,48,128]{2,1,0:T(8,128)(2,1)S(1)} async-done(((bf16[32,48,128]{2,1,0:T(8,128)(2,1)}), bf16[32,48,128]{2,1,0:T(8,128)(2,1)S(1)}, u32[]{:S(2)}, u32[]{:S(2)}) %all-to-all-start.1) | async-done | bytes 393248 | tf_op jit(solution)/shard_map/all_to_all | solution.py:497
  56.2 0.0 copy-done
  56.2 0.0 copy-done.1
  56.2 0.0 copy-done.2
  56.2 1.8 %shard_map.102 = f32[5,32,4,128]{3,2,1,0:T(4,128)} custom-call(s32[32]{0:T(128)S(1)} %bitcast.10, f32[5,32,4,128]{3,2,1,0:T(4,128)S(1)} %copy-done, f32[32,4,128]{2,1,0:T(4,128)S(1)} %copy-done.1, f32[5,4,128]{2,1,0:T(4,128)S(1)} %collective-permute-done.refs_3_, f32[5,4,128]{2,1,0:T(4,128)S(1)} %collective-permute-done.1.refs_4_, ...), custom_call_target="tpu_custom_call" | custom-call | tf_op jit(solution)/shard_map/pallas_call | solution.py:504
  (1 shorter events, 0.0 us)
Async XLA Ops:
  2.2 19.7 %all-to-all-start = ((bf16[32,48,128]{2,1,0:T(8,128)(2,1)}), bf16[32,48,128]{2,1,0:T(8,128)(2,1)S(1)}, u32[]{:S(2)}, u32[]{:S(2)}) async-start(bf16[32,48,128]{2,1,0:T(8,128)(2,1)} %get-tuple-element.16), calls=%async_computation | async-start | bytes 786432 | tf_op jit(solution)/shard_map/all_to_all | solution.py:474
  11.6 2.7 %collective-permute-start = (f32[5,4,128]{2,1,0:T(4,128)}, f32[5,4,128]{2,1,0:T(4,128)S(1)}, u32[]{:S(2)}, u32[]{:S(2)}) collective-permute-start(f32[5,4,128]{2,1,0:T(4,128)} %get-tuple-element.17), channel_id=1, source_target_pairs={{0,1},{1,2},{2,3},{3,4},{4,5},{5,6},{6,7},{7,8},{8,9},{9,10},{10,1... | collective-permute-start | bytes 30728 | tf_op jit(solution)/shard_map/ppermute | solution.py:472
  13.3 3.6 %collective-permute-start.1 = (f32[5,4,128]{2,1,0:T(4,128)}, f32[5,4,128]{2,1,0:T(4,128)S(1)}, u32[]{:S(2)}, u32[]{:S(2)}) collective-permute-start(f32[5,4,128]{2,1,0:T(4,128)} %get-tuple-element.18), channel_id=1, source_target_pairs={{0,31},{1,0},{2,1},{3,2},{4,3},{5,4},{6,5},{7,6},{8,7},{9,8},{10,9... | collective-permute-start | bytes 30728 | tf_op jit(solution)/shard_map/ppermute | solution.py:472
  21.9 7.5 %copy-start.3 = (bf16[32,48,128]{2,1,0:T(8,128)(2,1)}, bf16[32,48,128]{2,1,0:T(8,128)(2,1)S(1)}, u32[]{:S(2)}) copy-start(bf16[32,48,128]{2,1,0:T(8,128)(2,1)S(1)} %all-to-all-done.refs_2_) | copy-start | bytes 1179652
  22.0 5.1 %collective-permute-start.4 = (f32[8,128]{1,0:T(8,128)S(1)}, f32[8,128]{1,0:T(8,128)S(1)}, u32[]{:S(2)}, u32[]{:S(2)}) collective-permute-start(f32[8,128]{1,0:T(8,128)S(1)} %convert_reduce_fusion), channel_id=1, source_target_pairs={{0,64},{32,96},{64,0},{96,32},{1,65},{33,97},{65,1},{97,33},{2,66}... | collective-permute-start | bytes 12296 | tf_op jit(solution)/shard_map/ppermute | solution.py:472
  25.0 2.5 %collective-permute-start.3 = (f32[8,128]{1,0:T(8,128)S(1)}, f32[8,128]{1,0:T(8,128)S(1)}, u32[]{:S(2)}, u32[]{:S(2)}) collective-permute-start(f32[8,128]{1,0:T(8,128)S(1)} %convert_reduce_fusion), channel_id=1, source_target_pairs={{0,96},{32,0},{64,32},{96,64},{1,97},{33,1},{65,33},{97,65},{2,98}... | collective-permute-start | bytes 12296 | tf_op jit(solution)/shard_map/ppermute | solution.py:472
  25.7 3.7 %collective-permute-start.2 = (f32[8,128]{1,0:T(8,128)S(1)}, f32[8,128]{1,0:T(8,128)S(1)}, u32[]{:S(2)}, u32[]{:S(2)}) collective-permute-start(f32[8,128]{1,0:T(8,128)S(1)} %convert_reduce_fusion), channel_id=1, source_target_pairs={{0,32},{32,64},{64,96},{96,0},{1,33},{33,65},{65,97},{97,1},{2,34}... | collective-permute-start | bytes 12296 | tf_op jit(solution)/shard_map/ppermute | solution.py:472
  27.1 2.3 %copy-start.4 = (f32[8,128]{1,0:T(8,128)}, f32[8,128]{1,0:T(8,128)S(1)}, u32[]{:S(2)}) copy-start(f32[8,128]{1,0:T(8,128)S(1)} %collective-permute-done.4.refs_5_) | copy-start | bytes 12292
  27.4 2.0 %copy-start.5 = (f32[8,128]{1,0:T(8,128)}, f32[8,128]{1,0:T(8,128)S(1)}, u32[]{:S(2)}) copy-start(f32[8,128]{1,0:T(8,128)S(1)} %collective-permute-done.3.refs_4_) | copy-start | bytes 12292
  29.4 0.6 %copy-start.6 = (f32[8,128]{1,0:T(8,128)}, f32[8,128]{1,0:T(8,128)S(1)}, u32[]{:S(2)}) copy-start(f32[8,128]{1,0:T(8,128)S(1)} %collective-permute-done.2.refs_3_) | copy-start | bytes 12292
  30.0 15.9 %copy-start.8 = (f32[160,128]{1,0:T(8,128)S(1)}, f32[160,128]{1,0:T(8,128)}, u32[]{:S(2)}) copy-start(f32[160,128]{1,0:T(8,128)} %get-tuple-element.24) | copy-start | bytes 245764
  30.0 16.0 %copy-start.7 = (f32[160,128]{1,0:T(8,128)S(1)}, f32[160,128]{1,0:T(8,128)}, u32[]{:S(2)}) copy-start(f32[160,128]{1,0:T(8,128)} %get-tuple-element.25) | copy-start | bytes 245764
  30.0 26.2 %copy-start = (f32[5,32,4,128]{3,2,1,0:T(4,128)S(1)}, f32[5,32,4,128]{3,2,1,0:T(4,128)}, u32[]{:S(2)}) copy-start(f32[5,32,4,128]{3,2,1,0:T(4,128)} %refs_1_.3) | copy-start | bytes 983044
  30.0 26.2 %copy-start.1 = (f32[32,4,128]{2,1,0:T(4,128)S(1)}, f32[32,4,128]{2,1,0:T(4,128)}, u32[]{:S(2)}) copy-start(f32[32,4,128]{2,1,0:T(4,128)} %refs_2_.1) | copy-start | bytes 196612
  30.0 26.2 %copy-start.2 = (s32[1,32,1]{1,2,0:T(1,128)S(1)}, s32[1,32,1]{1,2,0:T(1,128)}, u32[]{:S(2)}) copy-start(s32[1,32,1]{1,2,0:T(1,128)} %param.12) | copy-start | bytes 388
  36.8 19.4 %all-to-all-start.1 = ((bf16[32,48,128]{2,1,0:T(8,128)(2,1)}), bf16[32,48,128]{2,1,0:T(8,128)(2,1)S(1)}, u32[]{:S(2)}, u32[]{:S(2)}) async-start(bf16[32,48,128]{2,1,0:T(8,128)(2,1)} %shard_map.101), calls=%async_computation.1 | async-start | bytes 786432 | tf_op jit(solution)/shard_map/all_to_all | solution.py:497
  45.9 5.1 %collective-permute-start.5 = (f32[160,128]{1,0:T(8,128)S(1)}, f32[160,128]{1,0:T(8,128)S(1)}, u32[]{:S(2)}, u32[]{:S(2)}) collective-permute-start(f32[160,128]{1,0:T(8,128)S(1)} %copy-done.8), channel_id=1, source_target_pairs={{0,32},{32,64},{64,96},{96,0},{1,33},{33,65},{65,97},{97,1},{2,34}... | collective-permute-start | bytes 245768 | tf_op jit(solution)/shard_map/ppermute | solution.py:472
  46.0 5.0 %collective-permute-start.6 = (f32[160,128]{1,0:T(8,128)S(1)}, f32[160,128]{1,0:T(8,128)S(1)}, u32[]{:S(2)}, u32[]{:S(2)}) collective-permute-start(f32[160,128]{1,0:T(8,128)S(1)} %copy-done.7), channel_id=1, source_target_pairs={{0,96},{32,0},{64,32},{96,64},{1,97},{33,1},{65,33},{97,65},{2,98}... | collective-permute-start | bytes 245768 | tf_op jit(solution)/shard_map/ppermute | solution.py:472

commit v5 on v4

--- a/solution.py
+++ b/solution.py
@@ -9,9 +9,8 @@
 ROWS_Y = 4
 LANES = 128
 HALF = NF * ROWS_Y
-PAIR = 48
-FLAGS = 40
-TAIL = 32
+PAIR = 2 * HALF
+EMPTY = 2.0**100
 VMEM_LIMIT = 65400 * 1024
 NT = (((1,), (1,)), ((), ()))
 
@@ -28,6 +27,8 @@
     back_ref,
     plane_of,
     count,
+    rows_above,
+    rows_below,
 ):
     is_gas = lax.axis_index("grp") < lax.axis_size("grp") - 1
 
@@ -48,22 +49,25 @@
 
     lax.fori_loop(0, planes, place, 0, unroll=True)
 
+    row = lax.broadcasted_iota(jnp.int32, (PAIR, LANES), 0)
     for p in range(owners):
         pieces = []
         for s in range(2):
             x = plane_of[2 * p + s]
             pieces += [flow_ref[f, x] for f in range(NF)]
-        number = jnp.where(is_gas, count[p], 0).astype(jnp.float32)
-        pieces.append(jnp.full((PAIR - FLAGS, LANES), number))
-        out_ref[p] = jnp.concatenate(pieces, axis=0).astype(jnp.bfloat16)
+        filled = HALF * jnp.where(is_gas, count[p], 0)
+        rows = jnp.where(row < filled, jnp.concatenate(pieces, axis=0), EMPTY)
+        out_ref[p] = rows.astype(jnp.bfloat16)
 
     for f in range(NF):
         for x in range(planes):
             r = f * planes + x
-            top_ref[r : r + 1] = flow_ref[f, x, ROWS_Y - 1 :]
-            bottom_ref[r : r + 1] = flow_ref[f, x, :1]
+            rows_above[r : r + 1] = flow_ref[f, x, ROWS_Y - 1 :]
+            rows_below[r : r + 1] = flow_ref[f, x, :1]
         front_ref[f] = flow_ref[f, 0]
         back_ref[f] = flow_ref[f, planes - 1]
+    top_ref[...] = rows_above[...].astype(jnp.bfloat16)
+    bottom_ref[...] = rows_below[...].astype(jnp.bfloat16)
 
 
 def slot_relayout():
@@ -205,8 +209,10 @@
     g = lax.axis_index("grp")
     counts = []
     for t in range(owners):
-        flags = recv_ref[t, TAIL:].astype(jnp.float32)[FLAGS - TAIL :]
-        counts.append(jnp.broadcast_to(flags[0:1], (8, LANES)))
+        first = recv_ref[t, :16].astype(jnp.float32)[:1]
+        second = recv_ref[t, 16:32].astype(jnp.float32)[HALF - 16 : HALF - 15]
+        held = jnp.where(first < EMPTY, 1.0, 0.0) + jnp.where(second < EMPTY, 1.0, 0.0)
+        counts.append(jnp.broadcast_to(held, (8, LANES)))
     gas_groups = lax.axis_size("grp") - 1
     near_above = jnp.where(g >= 1, above_ref[...], 0.0)
     near_below = jnp.where(g < gas_groups - 1, below_ref[...], 0.0)
@@ -354,6 +360,8 @@
     landed_ref,
     out_ref,
     count,
+    rows_above,
+    rows_below,
 ):
     me = lax.axis_index("tile")
     g = lax.axis_index("grp")
@@ -366,6 +374,8 @@
 
     lax.fori_loop(0, owners, clear, 0, unroll=True)
 
+    rows_below[...] = up_ref[...].astype(jnp.float32)
+    rows_above[...] = down_ref[...].astype(jnp.float32)
     xlo = [jnp.where(me > 0, xlo_ref[f], 0.0) for f in range(NF)]
     xhi = [jnp.where(me < owners - 1, xhi_ref[f], 0.0) for f in range(NF)]
     for x in range(planes):
@@ -379,8 +389,8 @@
             here = flow_ref[f, x]
             left = xlo[f] if x == 0 else flow_ref[f, x - 1]
             right = xhi[f] if x == planes - 1 else flow_ref[f, x + 1]
-            first = jnp.where(g >= 1, up_ref[r : r + 1], 0.0)
-            last = jnp.where(g < gas_groups - 1, down_ref[r : r + 1], 0.0)
+            first = jnp.where(g >= 1, rows_below[r : r + 1], 0.0)
+            last = jnp.where(g < gas_groups - 1, rows_above[r : r + 1], 0.0)
             lower = jnp.concatenate([first, here[: ROWS_Y - 1]], axis=0)
             upper = jnp.concatenate([here[1:], last], axis=0)
             back = jnp.where(lane == 0, 0.0, pltpu.roll(here, 1, 1))
@@ -450,7 +460,7 @@
     def pack_body(*refs):
         pack_kernel(planes, owners, *refs)
 
-    edge = jax.ShapeDtypeStruct((NF * planes, LANES), jnp.float32)
+    edge = jax.ShapeDtypeStruct((NF * planes, LANES), jnp.bfloat16)
     plane = jax.ShapeDtypeStruct((NF, ROWS_Y, LANES), jnp.float32)
     packed, top, bottom, front, behind = pl.pallas_call(
         pack_body,
@@ -463,7 +473,12 @@
         ),
         in_specs=[smem, vmem],
         out_specs=(vmem,) * 5,
-        scratch_shapes=[pltpu.SMEM((2 * owners,), jnp.int32), pltpu.SMEM((owners,), jnp.int32)],
+        scratch_shapes=[
+            pltpu.SMEM((2 * owners,), jnp.int32),
+            pltpu.SMEM((owners,), jnp.int32),
+            pltpu.VMEM((NF * planes, LANES), jnp.float32),
+            pltpu.VMEM((NF * planes, LANES), jnp.float32),
+        ],
         compiler_params=params,
     )(holder, flow_fields)
 
@@ -476,7 +491,8 @@
     xhi = turned(front, "tile", owners - 1)
     arrived, xlo, xhi = lax.optimization_barrier((arrived, xlo, xhi))
 
-    number = jnp.sum(arrived[:, FLAGS:].astype(jnp.float32), axis=0)
+    held = (arrived[:, 0] < EMPTY).astype(jnp.float32) + (arrived[:, HALF] < EMPTY).astype(jnp.float32)
+    number = jnp.broadcast_to(jnp.sum(held, axis=0), (8, LANES))
     above, far, below = (turned(number, "grp", k) for k in range(1, groups))
 
     outgoing = couple_call(
@@ -506,7 +522,11 @@
         out_shape=jax.ShapeDtypeStruct(flow_fields.shape, jnp.float32),
         in_specs=[smem] + [vmem] * 7,
         out_specs=vmem,
-        scratch_shapes=[pltpu.SMEM((owners,), jnp.int32)],
+        scratch_shapes=[
+            pltpu.SMEM((owners,), jnp.int32),
+            pltpu.VMEM((NF * planes, LANES), jnp.float32),
+            pltpu.VMEM((NF * planes, LANES), jnp.float32),
+        ],
         compiler_params=pltpu.CompilerParams(vmem_limit_bytes=40 * 1024 * 1024),
     )(holder, flow_fields, turbulent_diffusivity, xlo, xhi, up, down, landed)
 

time: 58.7 us -> 57.7 us (0.983); the launches traced: 58 us -> 57.9 us
  Pallas kernels: 10.8 us -> 14.7 us
  starting transfers between devices: 27.4 us -> 24.6 us
  waiting for transfers between devices: 18.5 us -> 17.2 us
    pallas_call x1, Pallas kernels: 6.77 us -> 10.7 us  [couple_call(): pl.pallas_call(couple_body, out_shape=message, in_specs=[smem] + [vmem] *...]
    all_to_all x1, starting transfers between devices: 9.09 us -> 6.25 us  [local(): landed = lax.all_to_all(outgoing, 'tile', 0, 0, tiled=True)]
    all_to_all x1, waiting for transfers between devices: 4.99 us -> 3.83 us  [local(): arrived = lax.all_to_all(packed, 'tile', 0, 0, tiled=True)]
where the time goes in v5:
time: 57.7 us; the launch traced here: 57.9 us
  starting transfers between devices  24.6 us (43%)
  waiting for transfers between devices  17.2 us (30%)
  Pallas kernels  14.7 us (25%)
  between operations  0.75 us (1%)
  local copies, waits for them, and re-layouts  0.62 us (1%)
    pallas_call x1, Pallas kernels, couple_call(): pl.pallas_call(couple_body, out_shape=message, in_specs=[smem] + [vmem] *...  10.7 us
    all_to_all x1, starting transfers between devices, local(): arrived = lax.all_to_all(packed, 'tile', 0, 0, tiled=True)  9.43 us
    ppermute x7, starting transfers between devices, turned(): lax.ppermute(array, axis, [(i, (i + step) % size) for i in range(size)])  8.89 us
    ppermute x7, waiting for transfers between devices, turned(): lax.ppermute(array, axis, [(i, (i + step) % size) for i in range(size)])  8.09 us
    all_to_all x1, starting transfers between devices, local(): landed = lax.all_to_all(outgoing, 'tile', 0, 0, tiled=True)  6.25 us
    all_to_all x1, waiting for transfers between devices, local(): landed = lax.all_to_all(outgoing, 'tile', 0, 0, tiled=True)  5.32 us
    all_to_all x1, waiting for transfers between devices, local(): arrived = lax.all_to_all(packed, 'tile', 0, 0, tiled=True)  3.83 us
    pallas_call x1, Pallas kernels, local(): pl.pallas_call(pack_body, out_shape=(jax.ShapeDtypeStruct((owners, PAIR,...  2.17 us
  transfers between devices with their start and end apart: 9, of which 7 were waited for; matrix products, arithmetic and copies ran while one was open for 0% of the time, Pallas kernels for 0%

profile of v5, /device:TPU:1, one launch (start us, length us, event | category | flops | bytes accessed | tf_op | source)
XLA Modules:
  0.0 57.9 jit_solution(3240050405736499335)
XLA Ops:
  0.0 2.2 %shard_map.100 = (bf16[32,40,128]{2,1,0:T(8,128)(2,1)}, bf16[160,128]{1,0:T(8,128)(2,1)}, bf16[160,128]{1,0:T(8,128)(2,1)}, f32[5,4,128]{2,1,0:T(4,128)}, f32[5,4,128]{2,1,0:T(4,128)}) custom-call(s32[32]{0:T(128)} %bitcast.9, f32[5,32,4,128]{3,2,1,0:T(4,128)} %refs_1_.3), custom_call_target="tpu_custom_call" | custom-call | tf_op jit(solution)/shard_map/pallas_call | solution.py:465
  2.2 9.4 %all-to-all-start = ((bf16[32,40,128]{2,1,0:T(8,128)(2,1)}), bf16[32,40,128]{2,1,0:T(8,128)(2,1)S(1)}, u32[]{:S(2)}, u32[]{:S(2)}) async-start(bf16[32,40,128]{2,1,0:T(8,128)(2,1)} %get-tuple-element.16), calls=%async_computation | async-start | bytes 655360 | tf_op jit(solution)/shard_map/all_to_all | solution.py:489
  11.6 1.7 %collective-permute-start = (f32[5,4,128]{2,1,0:T(4,128)}, f32[5,4,128]{2,1,0:T(4,128)S(1)}, u32[]{:S(2)}, u32[]{:S(2)}) collective-permute-start(f32[5,4,128]{2,1,0:T(4,128)} %get-tuple-element.17), channel_id=1, source_target_pairs={{0,1},{1,2},{2,3},{3,4},{4,5},{5,6},{6,7},{7,8},{8,9},{9,10},{10,1... | collective-permute-start | bytes 30728 | tf_op jit(solution)/shard_map/ppermute | solution.py:487
  13.3 0.0 collective-permute-start.1
  13.3 1.0 %collective-permute-done.refs_3_ = f32[5,4,128]{2,1,0:T(4,128)S(1)} collective-permute-done((f32[5,4,128]{2,1,0:T(4,128)}, f32[5,4,128]{2,1,0:T(4,128)S(1)}, u32[]{:S(2)}, u32[]{:S(2)}) %collective-permute-start) | collective-permute-done | bytes 10272 | tf_op jit(solution)/shard_map/ppermute | solution.py:487
  14.3 3.1 %collective-permute-done.1.refs_4_ = f32[5,4,128]{2,1,0:T(4,128)S(1)} collective-permute-done((f32[5,4,128]{2,1,0:T(4,128)}, f32[5,4,128]{2,1,0:T(4,128)S(1)}, u32[]{:S(2)}, u32[]{:S(2)}) %collective-permute-start.1) | collective-permute-done | bytes 10272 | tf_op jit(solution)/shard_map/ppermute | solution.py:487
  17.4 3.8 %all-to-all-done.refs_2_ = bf16[32,40,128]{2,1,0:T(8,128)(2,1)S(1)} async-done(((bf16[32,40,128]{2,1,0:T(8,128)(2,1)}), bf16[32,40,128]{2,1,0:T(8,128)(2,1)S(1)}, u32[]{:S(2)}, u32[]{:S(2)}) %all-to-all-start) | async-done | bytes 327712 | tf_op jit(solution)/shard_map/all_to_all | solution.py:489
  21.3 0.0 copy-start.3
  21.3 0.1 fusion.1
  21.3 3.0 %collective-permute-start.4 = (f32[8,128]{1,0:T(8,128)S(1)}, f32[8,128]{1,0:T(8,128)S(1)}, u32[]{:S(2)}, u32[]{:S(2)}) collective-permute-start(f32[8,128]{1,0:T(8,128)S(1)} %broadcast_in_dim.3), channel_id=1, source_target_pairs={{0,64},{32,96},{64,0},{96,32},{1,65},{33,97},{65,1},{97,33},{2,66}... | collective-permute-start | bytes 12296 | tf_op jit(solution)/shard_map/ppermute | solution.py:487
  24.3 0.8 %collective-permute-start.3 = (f32[8,128]{1,0:T(8,128)S(1)}, f32[8,128]{1,0:T(8,128)S(1)}, u32[]{:S(2)}, u32[]{:S(2)}) collective-permute-start(f32[8,128]{1,0:T(8,128)S(1)} %broadcast_in_dim.3), channel_id=1, source_target_pairs={{0,96},{32,0},{64,32},{96,64},{1,97},{33,1},{65,33},{97,65},{2,98}... | collective-permute-start | bytes 12296 | tf_op jit(solution)/shard_map/ppermute | solution.py:487
  25.1 0.7 %collective-permute-start.2 = (f32[8,128]{1,0:T(8,128)S(1)}, f32[8,128]{1,0:T(8,128)S(1)}, u32[]{:S(2)}, u32[]{:S(2)}) collective-permute-start(f32[8,128]{1,0:T(8,128)S(1)} %broadcast_in_dim.3), channel_id=1, source_target_pairs={{0,32},{32,64},{64,96},{96,0},{1,33},{33,65},{65,97},{97,1},{2,34}... | collective-permute-start | bytes 12296 | tf_op jit(solution)/shard_map/ppermute | solution.py:487
  26.4 0.0 collective-permute-done.4.refs_5_
  26.5 0.0 copy-start.4
  26.5 0.3 collective-permute-done.3.refs_4_
  26.8 0.0 copy-start.5
  26.8 2.0 %collective-permute-done.2.refs_3_ = f32[8,128]{1,0:T(8,128)S(1)} collective-permute-done((f32[8,128]{1,0:T(8,128)S(1)}, f32[8,128]{1,0:T(8,128)S(1)}, u32[]{:S(2)}, u32[]{:S(2)}) %collective-permute-start.2) | collective-permute-done | bytes 4128 | tf_op jit(solution)/shard_map/ppermute | solution.py:487
  28.8 0.0 copy-start.6
  28.8 0.0 copy-done.3
  28.8 0.0 copy-done.4
  28.8 0.0 copy-done.5
  28.8 0.6 %copy-done.6 = f32[8,128]{1,0:T(8,128)} copy-done((f32[8,128]{1,0:T(8,128)}, f32[8,128]{1,0:T(8,128)S(1)}, u32[]{:S(2)}) %copy-start.6) | copy-done | bytes 4120
  29.4 0.0 copy-start.8
  29.4 0.0 copy-start.7
  29.4 0.0 copy-start
  29.4 0.0 copy-start.1
  29.4 0.0 copy-start.2
  29.4 10.7 %shard_map.101 = bf16[32,40,128]{2,1,0:T(8,128)(2,1)} custom-call(s32[1]{0:T(128)S(6)} %copy.11.refs_0_, s32[8,128]{1,0:T(8,128)} %bitcast.16, bf16[32,40,128]{2,1,0:T(8,128)(2,1)} %copy-done.3, f32[8,128]{1,0:T(8,128)} %copy-done.6, f32[8,128]{1,0:T(8,128)} %copy-done.5, f32[8,128]{1,0:T(8,128)} %copy-done.4, s32[1024,128]{1,0:T(8,128)} %bitcast.12, ...), custom_call_target="tpu_custom_call" | custom-call | tf_op jit(solution)/shard_map/pallas_call | solution.py:414
  40.1 6.2 %all-to-all-start.1 = ((bf16[32,40,128]{2,1,0:T(8,128)(2,1)}), bf16[32,40,128]{2,1,0:T(8,128)(2,1)S(1)}, u32[]{:S(2)}, u32[]{:S(2)}) async-start(bf16[32,40,128]{2,1,0:T(8,128)(2,1)} %shard_map.101), calls=%async_computation.1 | async-start | bytes 655360 | tf_op jit(solution)/shard_map/all_to_all | solution.py:513
  46.3 0.0 copy-done.8
  46.3 0.1 collective-permute-start.5
  46.4 0.0 copy-done.7
  46.4 2.7 %collective-permute-start.6 = (bf16[160,128]{1,0:T(8,128)(2,1)S(1)}, bf16[160,128]{1,0:T(8,128)(2,1)S(1)}, u32[]{:S(2)}, u32[]{:S(2)}) collective-permute-start(bf16[160,128]{1,0:T(8,128)(2,1)S(1)} %copy-done.7), channel_id=1, source_target_pairs={{0,96},{32,0},{64,32},{96,64},{1,97},{33,1},{65,33},{97,65},{2,98}... | collective-permute-start | bytes 122888 | tf_op jit(solution)/shard_map/ppermute | solution.py:487
  49.1 1.7 %collective-permute-done.5.refs_5_ = bf16[160,128]{1,0:T(8,128)(2,1)S(1)} collective-permute-done((bf16[160,128]{1,0:T(8,128)(2,1)S(1)}, bf16[160,128]{1,0:T(8,128)(2,1)S(1)}, u32[]{:S(2)}, u32[]{:S(2)}) %collective-permute-start.5) | collective-permute-done | bytes 40992 | tf_op jit(solution)/shard_map/ppermute | solution.py:487
  50.8 0.0 collective-permute-done.6.refs_6_
  50.8 5.3 %all-to-all-done.1.refs_7_ = bf16[32,40,128]{2,1,0:T(8,128)(2,1)S(1)} async-done(((bf16[32,40,128]{2,1,0:T(8,128)(2,1)}), bf16[32,40,128]{2,1,0:T(8,128)(2,1)S(1)}, u32[]{:S(2)}, u32[]{:S(2)}) %all-to-all-start.1) | async-done | bytes 327712 | tf_op jit(solution)/shard_map/all_to_all | solution.py:513
  56.1 0.0 copy-done
  56.1 0.0 copy-done.1
  56.1 0.0 copy-done.2
  56.1 1.8 %shard_map.102 = f32[5,32,4,128]{3,2,1,0:T(4,128)} custom-call(s32[32]{0:T(128)S(1)} %bitcast.10, f32[5,32,4,128]{3,2,1,0:T(4,128)S(1)} %copy-done, f32[32,4,128]{2,1,0:T(4,128)S(1)} %copy-done.1, f32[5,4,128]{2,1,0:T(4,128)S(1)} %collective-permute-done.refs_3_, f32[5,4,128]{2,1,0:T(4,128)S(1)} %collective-permute-done.1.refs_4_, ...), custom_call_target="tpu_custom_call" | custom-call | tf_op jit(solution)/shard_map/pallas_call | solution.py:520
  (1 shorter events, 0.0 us)
Async XLA Ops:
  2.2 19.1 %all-to-all-start = ((bf16[32,40,128]{2,1,0:T(8,128)(2,1)}), bf16[32,40,128]{2,1,0:T(8,128)(2,1)S(1)}, u32[]{:S(2)}, u32[]{:S(2)}) async-start(bf16[32,40,128]{2,1,0:T(8,128)(2,1)} %get-tuple-element.16), calls=%async_computation | async-start | bytes 655360 | tf_op jit(solution)/shard_map/all_to_all | solution.py:489
  11.6 2.7 %collective-permute-start = (f32[5,4,128]{2,1,0:T(4,128)}, f32[5,4,128]{2,1,0:T(4,128)S(1)}, u32[]{:S(2)}, u32[]{:S(2)}) collective-permute-start(f32[5,4,128]{2,1,0:T(4,128)} %get-tuple-element.17), channel_id=1, source_target_pairs={{0,1},{1,2},{2,3},{3,4},{4,5},{5,6},{6,7},{7,8},{8,9},{9,10},{10,1... | collective-permute-start | bytes 30728 | tf_op jit(solution)/shard_map/ppermute | solution.py:487
  13.3 4.1 %collective-permute-start.1 = (f32[5,4,128]{2,1,0:T(4,128)}, f32[5,4,128]{2,1,0:T(4,128)S(1)}, u32[]{:S(2)}, u32[]{:S(2)}) collective-permute-start(f32[5,4,128]{2,1,0:T(4,128)} %get-tuple-element.18), channel_id=1, source_target_pairs={{0,31},{1,0},{2,1},{3,2},{4,3},{5,4},{6,5},{7,6},{8,7},{9,8},{10,9... | collective-permute-start | bytes 30728 | tf_op jit(solution)/shard_map/ppermute | solution.py:487
  21.3 7.5 %copy-start.3 = (bf16[32,40,128]{2,1,0:T(8,128)(2,1)}, bf16[32,40,128]{2,1,0:T(8,128)(2,1)S(1)}, u32[]{:S(2)}) copy-start(bf16[32,40,128]{2,1,0:T(8,128)(2,1)S(1)} %all-to-all-done.refs_2_) | copy-start | bytes 983044
  21.3 5.1 %collective-permute-start.4 = (f32[8,128]{1,0:T(8,128)S(1)}, f32[8,128]{1,0:T(8,128)S(1)}, u32[]{:S(2)}, u32[]{:S(2)}) collective-permute-start(f32[8,128]{1,0:T(8,128)S(1)} %broadcast_in_dim.3), channel_id=1, source_target_pairs={{0,64},{32,96},{64,0},{96,32},{1,65},{33,97},{65,1},{97,33},{2,66}... | collective-permute-start | bytes 12296 | tf_op jit(solution)/shard_map/ppermute | solution.py:487
  24.3 2.5 %collective-permute-start.3 = (f32[8,128]{1,0:T(8,128)S(1)}, f32[8,128]{1,0:T(8,128)S(1)}, u32[]{:S(2)}, u32[]{:S(2)}) collective-permute-start(f32[8,128]{1,0:T(8,128)S(1)} %broadcast_in_dim.3), channel_id=1, source_target_pairs={{0,96},{32,0},{64,32},{96,64},{1,97},{33,1},{65,33},{97,65},{2,98}... | collective-permute-start | bytes 12296 | tf_op jit(solution)/shard_map/ppermute | solution.py:487
  25.1 3.7 %collective-permute-start.2 = (f32[8,128]{1,0:T(8,128)S(1)}, f32[8,128]{1,0:T(8,128)S(1)}, u32[]{:S(2)}, u32[]{:S(2)}) collective-permute-start(f32[8,128]{1,0:T(8,128)S(1)} %broadcast_in_dim.3), channel_id=1, source_target_pairs={{0,32},{32,64},{64,96},{96,0},{1,33},{33,65},{65,97},{97,1},{2,34}... | collective-permute-start | bytes 12296 | tf_op jit(solution)/shard_map/ppermute | solution.py:487
  26.5 2.3 %copy-start.4 = (f32[8,128]{1,0:T(8,128)}, f32[8,128]{1,0:T(8,128)S(1)}, u32[]{:S(2)}) copy-start(f32[8,128]{1,0:T(8,128)S(1)} %collective-permute-done.4.refs_5_) | copy-start | bytes 12292
  26.8 2.0 %copy-start.5 = (f32[8,128]{1,0:T(8,128)}, f32[8,128]{1,0:T(8,128)S(1)}, u32[]{:S(2)}) copy-start(f32[8,128]{1,0:T(8,128)S(1)} %collective-permute-done.3.refs_4_) | copy-start | bytes 12292
  28.8 0.6 %copy-start.6 = (f32[8,128]{1,0:T(8,128)}, f32[8,128]{1,0:T(8,128)S(1)}, u32[]{:S(2)}) copy-start(f32[8,128]{1,0:T(8,128)S(1)} %collective-permute-done.2.refs_3_) | copy-start | bytes 12292
  29.4 17.0 %copy-start.8 = (bf16[160,128]{1,0:T(8,128)(2,1)S(1)}, bf16[160,128]{1,0:T(8,128)(2,1)}, u32[]{:S(2)}) copy-start(bf16[160,128]{1,0:T(8,128)(2,1)} %get-tuple-element.24) | copy-start | bytes 122884
  29.4 17.0 %copy-start.7 = (bf16[160,128]{1,0:T(8,128)(2,1)S(1)}, bf16[160,128]{1,0:T(8,128)(2,1)}, u32[]{:S(2)}) copy-start(bf16[160,128]{1,0:T(8,128)(2,1)} %get-tuple-element.25) | copy-start | bytes 122884
  29.4 26.7 %copy-start = (f32[5,32,4,128]{3,2,1,0:T(4,128)S(1)}, f32[5,32,4,128]{3,2,1,0:T(4,128)}, u32[]{:S(2)}) copy-start(f32[5,32,4,128]{3,2,1,0:T(4,128)} %refs_1_.3) | copy-start | bytes 983044
  29.4 26.7 %copy-start.1 = (f32[32,4,128]{2,1,0:T(4,128)S(1)}, f32[32,4,128]{2,1,0:T(4,128)}, u32[]{:S(2)}) copy-start(f32[32,4,128]{2,1,0:T(4,128)} %refs_2_.1) | copy-start | bytes 196612
  29.4 26.7 %copy-start.2 = (s32[1,32,1]{1,2,0:T(1,128)S(1)}, s32[1,32,1]{1,2,0:T(1,128)}, u32[]{:S(2)}) copy-start(s32[1,32,1]{1,2,0:T(1,128)} %param.12) | copy-start | bytes 388
  40.1 16.0 %all-to-all-start.1 = ((bf16[32,40,128]{2,1,0:T(8,128)(2,1)}), bf16[32,40,128]{2,1,0:T(8,128)(2,1)S(1)}, u32[]{:S(2)}, u32[]{:S(2)}) async-start(bf16[32,40,128]{2,1,0:T(8,128)(2,1)} %shard_map.101), calls=%async_computation.1 | async-start | bytes 655360 | tf_op jit(solution)/shard_map/all_to_all | solution.py:513
  46.3 4.4 %collective-permute-start.5 = (bf16[160,128]{1,0:T(8,128)(2,1)S(1)}, bf16[160,128]{1,0:T(8,128)(2,1)S(1)}, u32[]{:S(2)}, u32[]{:S(2)}) collective-permute-start(bf16[160,128]{1,0:T(8,128)(2,1)S(1)} %copy-done.8), channel_id=1, source_target_pairs={{0,32},{32,64},{64,96},{96,0},{1,33},{33,65},{65,97},{97,1},{2,34}... | collective-permute-start | bytes 122888 | tf_op jit(solution)/shard_map/ppermute | solution.py:487
  46.4 4.3 %collective-permute-start.6 = (bf16[160,128]{1,0:T(8,128)(2,1)S(1)}, bf16[160,128]{1,0:T(8,128)(2,1)S(1)}, u32[]{:S(2)}, u32[]{:S(2)}) collective-permute-start(bf16[160,128]{1,0:T(8,128)(2,1)S(1)} %copy-done.7), channel_id=1, source_target_pairs={{0,96},{32,0},{64,32},{96,64},{1,97},{33,1},{65,33},{97,65},{2,98}... | collective-permute-start | bytes 122888 | tf_op jit(solution)/shard_map/ppermute | solution.py:487

commit v6 on v5

--- a/solution.py
+++ b/solution.py
@@ -220,10 +220,10 @@
     total = sum(counts) + near_above + near_below + far
     before = near_above + jnp.where(g == gas_groups - 1, far, 0.0)
     divisor = jnp.maximum(total, 1.0)
-    pick = pick_ref[...].astype(jnp.float32)
+    pick = pick_ref[...]
     quotient = (pick / divisor).astype(jnp.int32)
     divisor_int = divisor.astype(jnp.int32)
-    picked = pick_ref[...] - quotient * divisor_int
+    picked = pick.astype(jnp.int32) - quotient * divisor_int
     picked = jnp.where(picked < 0, picked + divisor_int, picked)
     picked = jnp.where(picked >= divisor_int, picked - divisor_int, picked)
     place = picked.astype(jnp.float32) - before
@@ -405,7 +405,7 @@
     vmem = pl.BlockSpec(memory_space=pltpu.VMEM)
     smem = pl.BlockSpec(memory_space=pltpu.SMEM)
     hbm = pl.BlockSpec(memory_space=pl.ANY)
-    params = pltpu.CompilerParams(vmem_limit_bytes=64136 * 1024)
+    params = pltpu.CompilerParams(vmem_limit_bytes=54336 * 1024)
     message = jax.ShapeDtypeStruct((owners, PAIR, LANES), jnp.bfloat16)
 
     def couple_body(*refs):
@@ -489,7 +489,8 @@
     arrived = lax.all_to_all(packed, "tile", 0, 0, tiled=True)
     xlo = turned(behind, "tile", 1)
     xhi = turned(front, "tile", owners - 1)
-    arrived, xlo, xhi = lax.optimization_barrier((arrived, xlo, xhi))
+    pick = patch_pick_unreduced.reshape(8, LANES).astype(jnp.float32)
+    arrived, xlo, xhi, pick = lax.optimization_barrier((arrived, xlo, xhi, pick))
 
     held = (arrived[:, 0] < EMPTY).astype(jnp.float32) + (arrived[:, HALF] < EMPTY).astype(jnp.float32)
     number = jnp.broadcast_to(jnp.sum(held, axis=0), (8, LANES))
@@ -497,7 +498,7 @@
 
     outgoing = couple_call(
         living_spray_batches,
-        patch_pick_unreduced.reshape(8, LANES),
+        pick,
         arrived,
         above,
         below,

time: 57.7 us -> 56.1 us (0.972); the launches traced: 57.9 us -> 55.1 us
  Pallas kernels: 14.7 us -> 10.5 us
  starting transfers between devices: 24.6 us -> 26.7 us
  other arithmetic: 0.06 us -> 0.76 us
  waiting for transfers between devices: 17.2 us -> 16.5 us
  local copies, waits for them, and re-layouts: 0.62 us -> 0.03 us
    pallas_call x1, Pallas kernels: 10.7 us -> 6.44 us  [couple_call(): pl.pallas_call(couple_body, out_shape=message, in_specs=[smem] + [vmem] *...]
    all_to_all x1, starting transfers between devices: 6.25 us -> 8.35 us  [local(): landed = lax.all_to_all(outgoing, 'tile', 0, 0, tiled=True)]
    convert_element_type x0 -> x1, other arithmetic: none -> 0.69 us  [local(): pick = patch_pick_unreduced.reshape(8, LANES).astype(jnp.float32)]
    ppermute x7, waiting for transfers between devices: 8.09 us -> 7.42 us  [turned(): lax.ppermute(array, axis, [(i, (i + step) % size) for i in range(size)])]
    unnamed x18 -> x10, local copies, waits for them, and re-layouts: 0.62 us -> 0.02 us
  transfers between devices with their start and end apart: 9 -> 9, of which waited for: 7 -> 7; matrix products, arithmetic and copies ran while one was open for 0% -> 1% of each run, Pallas kernels for 0% -> 0%
where the time goes in v6:
time: 56.1 us; the launch traced here: 55.1 us
  starting transfers between devices  26.7 us (48%)
  waiting for transfers between devices  16.5 us (29%)
  Pallas kernels  10.5 us (19%)
  other arithmetic  0.76 us (1%)
  between operations  0.72 us (1%)
    all_to_all x1, starting transfers between devices, local(): arrived = lax.all_to_all(packed, 'tile', 0, 0, tiled=True)  9.43 us
    ppermute x7, starting transfers between devices, turned(): lax.ppermute(array, axis, [(i, (i + step) % size) for i in range(size)])  8.91 us
    all_to_all x1, starting transfers between devices, local(): landed = lax.all_to_all(outgoing, 'tile', 0, 0, tiled=True)  8.35 us
    ppermute x7, waiting for transfers between devices, turned(): lax.ppermute(array, axis, [(i, (i + step) % size) for i in range(size)])  7.42 us
    pallas_call x1, Pallas kernels, couple_call(): pl.pallas_call(couple_body, out_shape=message, in_specs=[smem] + [vmem] *...  6.44 us
    all_to_all x1, waiting for transfers between devices, local(): landed = lax.all_to_all(outgoing, 'tile', 0, 0, tiled=True)  5.21 us
    all_to_all x1, waiting for transfers between devices, local(): arrived = lax.all_to_all(packed, 'tile', 0, 0, tiled=True)  3.83 us
    pallas_call x1, Pallas kernels, local(): pl.pallas_call(pack_body, out_shape=(jax.ShapeDtypeStruct((owners, PAIR,...  2.17 us
  transfers between devices with their start and end apart: 9, of which 7 were waited for; matrix products, arithmetic and copies ran while one was open for 1% of the time, Pallas kernels for 0%

profile of v6, /device:TPU:1, one launch (start us, length us, event | category | flops | bytes accessed | tf_op | source)
XLA Modules:
  0.0 55.1 jit_solution(14194331565065230155)
XLA Ops:
  0.0 2.2 %shard_map.100 = (bf16[32,40,128]{2,1,0:T(8,128)(2,1)}, bf16[160,128]{1,0:T(8,128)(2,1)}, bf16[160,128]{1,0:T(8,128)(2,1)}, f32[5,4,128]{2,1,0:T(4,128)}, f32[5,4,128]{2,1,0:T(4,128)}) custom-call(s32[32]{0:T(128)} %bitcast.10, f32[5,32,4,128]{3,2,1,0:T(4,128)} %refs_1_.3), custom_call_target="tpu_custom_call" | custom-call | tf_op jit(solution)/shard_map/pallas_call | solution.py:465
  2.2 9.4 %all-to-all-start = ((bf16[32,40,128]{2,1,0:T(8,128)(2,1)}), bf16[32,40,128]{2,1,0:T(8,128)(2,1)S(1)}, u32[]{:S(2)}, u32[]{:S(2)}) async-start(bf16[32,40,128]{2,1,0:T(8,128)(2,1)} %get-tuple-element.17), calls=%async_computation | async-start | bytes 655360 | tf_op jit(solution)/shard_map/all_to_all | solution.py:489
  11.6 1.7 %collective-permute-start = (f32[5,4,128]{2,1,0:T(4,128)}, f32[5,4,128]{2,1,0:T(4,128)S(1)}, u32[]{:S(2)}, u32[]{:S(2)}) collective-permute-start(f32[5,4,128]{2,1,0:T(4,128)} %get-tuple-element.18), channel_id=1, source_target_pairs={{0,1},{1,2},{2,3},{3,4},{4,5},{5,6},{6,7},{7,8},{8,9},{9,10},{10,1... | collective-permute-start | bytes 30728 | tf_op jit(solution)/shard_map/ppermute | solution.py:487
  13.3 0.0 collective-permute-start.1
  13.3 0.7 %convert_element_type.14 = f32[1,1024]{1,0:T(1,128)S(1)} convert(s32[1,1024]{1,0:T(1,128)} %param.14) | non-fusion elementwise | flops 1024 | bytes 8192 | tf_op jit(solution)/shard_map/convert_element_type | solution.py:492
  14.0 0.3 collective-permute-done.refs_3_
  14.3 3.1 %collective-permute-done.1.refs_4_ = f32[5,4,128]{2,1,0:T(4,128)S(1)} collective-permute-done((f32[5,4,128]{2,1,0:T(4,128)}, f32[5,4,128]{2,1,0:T(4,128)S(1)}, u32[]{:S(2)}, u32[]{:S(2)}) %collective-permute-start.1) | collective-permute-done | bytes 10272 | tf_op jit(solution)/shard_map/ppermute | solution.py:487
  17.4 3.8 %all-to-all-done.refs_2_ = bf16[32,40,128]{2,1,0:T(8,128)(2,1)S(1)} async-done(((bf16[32,40,128]{2,1,0:T(8,128)(2,1)}), bf16[32,40,128]{2,1,0:T(8,128)(2,1)S(1)}, u32[]{:S(2)}, u32[]{:S(2)}) %all-to-all-start) | async-done | bytes 327712 | tf_op jit(solution)/shard_map/all_to_all | solution.py:489
  21.3 0.1 fusion.1
  21.3 3.0 %collective-permute-start.4 = (f32[8,128]{1,0:T(8,128)S(1)}, f32[8,128]{1,0:T(8,128)S(1)}, u32[]{:S(2)}, u32[]{:S(2)}) collective-permute-start(f32[8,128]{1,0:T(8,128)S(1)} %broadcast_in_dim.3), channel_id=1, source_target_pairs={{0,64},{32,96},{64,0},{96,32},{1,65},{33,97},{65,1},{97,33},{2,66}... | collective-permute-start | bytes 12296 | tf_op jit(solution)/shard_map/ppermute | solution.py:487
  24.3 0.8 %collective-permute-start.3 = (f32[8,128]{1,0:T(8,128)S(1)}, f32[8,128]{1,0:T(8,128)S(1)}, u32[]{:S(2)}, u32[]{:S(2)}) collective-permute-start(f32[8,128]{1,0:T(8,128)S(1)} %broadcast_in_dim.3), channel_id=1, source_target_pairs={{0,96},{32,0},{64,32},{96,64},{1,97},{33,1},{65,33},{97,65},{2,98}... | collective-permute-start | bytes 12296 | tf_op jit(solution)/shard_map/ppermute | solution.py:487
  25.1 0.7 %collective-permute-start.2 = (f32[8,128]{1,0:T(8,128)S(1)}, f32[8,128]{1,0:T(8,128)S(1)}, u32[]{:S(2)}, u32[]{:S(2)}) collective-permute-start(f32[8,128]{1,0:T(8,128)S(1)} %broadcast_in_dim.3), channel_id=1, source_target_pairs={{0,32},{32,64},{64,96},{96,0},{1,33},{33,65},{65,97},{97,1},{2,34}... | collective-permute-start | bytes 12296 | tf_op jit(solution)/shard_map/ppermute | solution.py:487
  26.4 0.0 collective-permute-done.4.refs_5_
  26.5 0.3 collective-permute-done.3.refs_4_
  26.8 2.0 %collective-permute-done.2.refs_3_ = f32[8,128]{1,0:T(8,128)S(1)} collective-permute-done((f32[8,128]{1,0:T(8,128)S(1)}, f32[8,128]{1,0:T(8,128)S(1)}, u32[]{:S(2)}, u32[]{:S(2)}) %collective-permute-start.2) | collective-permute-done | bytes 4128 | tf_op jit(solution)/shard_map/ppermute | solution.py:487
  28.8 0.0 copy-start.4
  28.8 0.0 copy-start.3
  28.8 0.0 copy-start
  28.8 0.0 copy-start.1
  28.8 0.0 copy-start.2
  28.8 6.4 %shard_map.101 = bf16[32,40,128]{2,1,0:T(8,128)(2,1)} custom-call(s32[1]{0:T(128)S(6)} %copy.11.refs_0_, f32[8,128]{1,0:T(8,128)S(1)} %bitcast.9, bf16[32,40,128]{2,1,0:T(8,128)(2,1)S(1)} %all-to-all-done.refs_2_, f32[8,128]{1,0:T(8,128)S(1)} %collective-permute-done.2.refs_3_, f32[8,128]{1,0:T(8,128)S(1)} %collective-permute-done.3.refs_4_, ...), custom_call_target="tpu_custom_call" | custom-call | tf_op jit(solution)/shard_map/pallas_call | solution.py:414
  35.2 8.3 %all-to-all-start.1 = ((bf16[32,40,128]{2,1,0:T(8,128)(2,1)}), bf16[32,40,128]{2,1,0:T(8,128)(2,1)S(1)}, u32[]{:S(2)}, u32[]{:S(2)}) async-start(bf16[32,40,128]{2,1,0:T(8,128)(2,1)} %shard_map.101), calls=%async_computation.1 | async-start | bytes 655360 | tf_op jit(solution)/shard_map/all_to_all | solution.py:514
  43.6 0.0 copy-done.4
  43.6 0.3 collective-permute-start.5
  43.9 0.0 copy-done.3
  43.9 2.5 %collective-permute-start.6 = (bf16[160,128]{1,0:T(8,128)(2,1)S(1)}, bf16[160,128]{1,0:T(8,128)(2,1)S(1)}, u32[]{:S(2)}, u32[]{:S(2)}) collective-permute-start(bf16[160,128]{1,0:T(8,128)(2,1)S(1)} %copy-done.3), channel_id=1, source_target_pairs={{0,96},{32,0},{64,32},{96,64},{1,97},{33,1},{65,33},{97,65},{2,98}... | collective-permute-start | bytes 122888 | tf_op jit(solution)/shard_map/ppermute | solution.py:487
  46.4 1.7 %collective-permute-done.5.refs_5_ = bf16[160,128]{1,0:T(8,128)(2,1)S(1)} collective-permute-done((bf16[160,128]{1,0:T(8,128)(2,1)S(1)}, bf16[160,128]{1,0:T(8,128)(2,1)S(1)}, u32[]{:S(2)}, u32[]{:S(2)}) %collective-permute-start.5) | collective-permute-done | bytes 40992 | tf_op jit(solution)/shard_map/ppermute | solution.py:487
  48.0 0.0 collective-permute-done.6.refs_6_
  48.0 5.2 %all-to-all-done.1.refs_7_ = bf16[32,40,128]{2,1,0:T(8,128)(2,1)S(1)} async-done(((bf16[32,40,128]{2,1,0:T(8,128)(2,1)}), bf16[32,40,128]{2,1,0:T(8,128)(2,1)S(1)}, u32[]{:S(2)}, u32[]{:S(2)}) %all-to-all-start.1) | async-done | bytes 327712 | tf_op jit(solution)/shard_map/all_to_all | solution.py:514
  53.2 0.0 copy-done
  53.2 0.0 copy-done.1
  53.2 0.0 copy-done.2
  53.3 1.9 %shard_map.102 = f32[5,32,4,128]{3,2,1,0:T(4,128)} custom-call(s32[32]{0:T(128)S(1)} %bitcast.11, f32[5,32,4,128]{3,2,1,0:T(4,128)S(1)} %copy-done, f32[32,4,128]{2,1,0:T(4,128)S(1)} %copy-done.1, f32[5,4,128]{2,1,0:T(4,128)S(1)} %collective-permute-done.refs_3_, f32[5,4,128]{2,1,0:T(4,128)S(1)} %collective-permute-done.1.refs_4_, ...), custom_call_target="tpu_custom_call" | custom-call | tf_op jit(solution)/shard_map/pallas_call | solution.py:521
  (1 shorter events, 0.0 us)
Async XLA Ops:
  2.2 19.1 %all-to-all-start = ((bf16[32,40,128]{2,1,0:T(8,128)(2,1)}), bf16[32,40,128]{2,1,0:T(8,128)(2,1)S(1)}, u32[]{:S(2)}, u32[]{:S(2)}) async-start(bf16[32,40,128]{2,1,0:T(8,128)(2,1)} %get-tuple-element.17), calls=%async_computation | async-start | bytes 655360 | tf_op jit(solution)/shard_map/all_to_all | solution.py:489
  11.6 2.7 %collective-permute-start = (f32[5,4,128]{2,1,0:T(4,128)}, f32[5,4,128]{2,1,0:T(4,128)S(1)}, u32[]{:S(2)}, u32[]{:S(2)}) collective-permute-start(f32[5,4,128]{2,1,0:T(4,128)} %get-tuple-element.18), channel_id=1, source_target_pairs={{0,1},{1,2},{2,3},{3,4},{4,5},{5,6},{6,7},{7,8},{8,9},{9,10},{10,1... | collective-permute-start | bytes 30728 | tf_op jit(solution)/shard_map/ppermute | solution.py:487
  13.3 4.1 %collective-permute-start.1 = (f32[5,4,128]{2,1,0:T(4,128)}, f32[5,4,128]{2,1,0:T(4,128)S(1)}, u32[]{:S(2)}, u32[]{:S(2)}) collective-permute-start(f32[5,4,128]{2,1,0:T(4,128)} %get-tuple-element.19), channel_id=1, source_target_pairs={{0,31},{1,0},{2,1},{3,2},{4,3},{5,4},{6,5},{7,6},{8,7},{9,8},{10,9... | collective-permute-start | bytes 30728 | tf_op jit(solution)/shard_map/ppermute | solution.py:487
  21.3 5.1 %collective-permute-start.4 = (f32[8,128]{1,0:T(8,128)S(1)}, f32[8,128]{1,0:T(8,128)S(1)}, u32[]{:S(2)}, u32[]{:S(2)}) collective-permute-start(f32[8,128]{1,0:T(8,128)S(1)} %broadcast_in_dim.3), channel_id=1, source_target_pairs={{0,64},{32,96},{64,0},{96,32},{1,65},{33,97},{65,1},{97,33},{2,66}... | collective-permute-start | bytes 12296 | tf_op jit(solution)/shard_map/ppermute | solution.py:487
  24.3 2.5 %collective-permute-start.3 = (f32[8,128]{1,0:T(8,128)S(1)}, f32[8,128]{1,0:T(8,128)S(1)}, u32[]{:S(2)}, u32[]{:S(2)}) collective-permute-start(f32[8,128]{1,0:T(8,128)S(1)} %broadcast_in_dim.3), channel_id=1, source_target_pairs={{0,96},{32,0},{64,32},{96,64},{1,97},{33,1},{65,33},{97,65},{2,98}... | collective-permute-start | bytes 12296 | tf_op jit(solution)/shard_map/ppermute | solution.py:487
  25.1 3.7 %collective-permute-start.2 = (f32[8,128]{1,0:T(8,128)S(1)}, f32[8,128]{1,0:T(8,128)S(1)}, u32[]{:S(2)}, u32[]{:S(2)}) collective-permute-start(f32[8,128]{1,0:T(8,128)S(1)} %broadcast_in_dim.3), channel_id=1, source_target_pairs={{0,32},{32,64},{64,96},{96,0},{1,33},{33,65},{65,97},{97,1},{2,34}... | collective-permute-start | bytes 12296 | tf_op jit(solution)/shard_map/ppermute | solution.py:487
  28.8 14.8 %copy-start.4 = (bf16[160,128]{1,0:T(8,128)(2,1)S(1)}, bf16[160,128]{1,0:T(8,128)(2,1)}, u32[]{:S(2)}) copy-start(bf16[160,128]{1,0:T(8,128)(2,1)} %get-tuple-element.26) | copy-start | bytes 122884
  28.8 15.1 %copy-start.3 = (bf16[160,128]{1,0:T(8,128)(2,1)S(1)}, bf16[160,128]{1,0:T(8,128)(2,1)}, u32[]{:S(2)}) copy-start(bf16[160,128]{1,0:T(8,128)(2,1)} %get-tuple-element.27) | copy-start | bytes 122884
  28.8 24.5 %copy-start = (f32[5,32,4,128]{3,2,1,0:T(4,128)S(1)}, f32[5,32,4,128]{3,2,1,0:T(4,128)}, u32[]{:S(2)}) copy-start(f32[5,32,4,128]{3,2,1,0:T(4,128)} %refs_1_.3) | copy-start | bytes 983044
  28.8 24.5 %copy-start.1 = (f32[32,4,128]{2,1,0:T(4,128)S(1)}, f32[32,4,128]{2,1,0:T(4,128)}, u32[]{:S(2)}) copy-start(f32[32,4,128]{2,1,0:T(4,128)} %refs_2_.1) | copy-start | bytes 196612
  28.8 24.5 %copy-start.2 = (s32[1,32,1]{1,2,0:T(1,128)S(1)}, s32[1,32,1]{1,2,0:T(1,128)}, u32[]{:S(2)}) copy-start(s32[1,32,1]{1,2,0:T(1,128)} %param.12) | copy-start | bytes 388
  35.2 18.0 %all-to-all-start.1 = ((bf16[32,40,128]{2,1,0:T(8,128)(2,1)}), bf16[32,40,128]{2,1,0:T(8,128)(2,1)S(1)}, u32[]{:S(2)}, u32[]{:S(2)}) async-start(bf16[32,40,128]{2,1,0:T(8,128)(2,1)} %shard_map.101), calls=%async_computation.1 | async-start | bytes 655360 | tf_op jit(solution)/shard_map/all_to_all | solution.py:514
  43.6 4.4 %collective-permute-start.5 = (bf16[160,128]{1,0:T(8,128)(2,1)S(1)}, bf16[160,128]{1,0:T(8,128)(2,1)S(1)}, u32[]{:S(2)}, u32[]{:S(2)}) collective-permute-start(bf16[160,128]{1,0:T(8,128)(2,1)S(1)} %copy-done.4), channel_id=1, source_target_pairs={{0,32},{32,64},{64,96},{96,0},{1,33},{33,65},{65,97},{97,1},{2,34}... | collective-permute-start | bytes 122888 | tf_op jit(solution)/shard_map/ppermute | solution.py:487
  43.9 4.2 %collective-permute-start.6 = (bf16[160,128]{1,0:T(8,128)(2,1)S(1)}, bf16[160,128]{1,0:T(8,128)(2,1)S(1)}, u32[]{:S(2)}, u32[]{:S(2)}) collective-permute-start(bf16[160,128]{1,0:T(8,128)(2,1)S(1)} %copy-done.3), channel_id=1, source_target_pairs={{0,96},{32,0},{64,32},{96,64},{1,97},{33,1},{65,33},{97,65},{2,98}... | collective-permute-start | bytes 122888 | tf_op jit(solution)/shard_map/ppermute | solution.py:487

commit v7 on v6

--- a/solution.py
+++ b/solution.py
@@ -131,7 +131,7 @@
     ahead = jnp.dot(before, halves.astype(jnp.bfloat16), preferred_element_type=jnp.float32)
     start = 2.0 * (16.0 * ahead[:, :lanes] + ahead[:, lanes:])
     number = start[slots - 1 :].astype(jnp.int32) + 2 * pairs[slots - 1 :]
-    carry = start + (2 * STEP - 1.0)
+    carry = start + (STEP - 1.0)
     low = lax.broadcasted_iota(jnp.int32, (lanes, lanes), 0)
     high = lax.broadcasted_iota(jnp.int32, (16, lanes), 0)
     lane = lax.broadcasted_iota(jnp.int32, (16, lanes), 1).astype(jnp.float32)
@@ -335,11 +335,11 @@
 
     def advance(j, carry):
         scatter(j)
+        look_up(j + 1)
         move()
-        look_up(j + 2)
         return carry
 
-    lax.fori_loop(0, (found + STEP - 1) // STEP + 2, advance, 0)
+    lax.fori_loop(0, (found + STEP - 1) // STEP + 1, advance, 0)
 
     back = slot_relayout_back()
     for t in range(owners):

time: 56.1 us -> 56.1 us (level); the launches traced: 55.1 us -> 56.2 us
  Pallas kernels: 10.5 us -> 15.5 us
  starting transfers between devices: 26.7 us -> 22.8 us
    pallas_call x1, Pallas kernels: 6.44 us -> 11.4 us  [couple_call(): pl.pallas_call(couple_body, out_shape=message, in_specs=[smem] + [vmem] *...]
    all_to_all x1, starting transfers between devices: 8.35 us -> 4.45 us  [local(): landed = lax.all_to_all(outgoing, 'tile', 0, 0, tiled=True)]
where the time goes in v7:
time: 56.1 us; the launch traced here: 56.2 us
  starting transfers between devices  22.8 us (41%)
  waiting for transfers between devices  16.5 us (29%)
  Pallas kernels  15.5 us (28%)
  other arithmetic  0.76 us (1%)
  between operations  0.73 us (1%)
    pallas_call x1, Pallas kernels, couple_call(): pl.pallas_call(couple_body, out_shape=message, in_specs=[smem] + [vmem] *...  11.4 us
    all_to_all x1, starting transfers between devices, local(): arrived = lax.all_to_all(packed, 'tile', 0, 0, tiled=True)  9.43 us
    ppermute x7, starting transfers between devices, turned(): lax.ppermute(array, axis, [(i, (i + step) % size) for i in range(size)])  8.89 us
    ppermute x7, waiting for transfers between devices, turned(): lax.ppermute(array, axis, [(i, (i + step) % size) for i in range(size)])  7.42 us
    all_to_all x1, waiting for transfers between devices, local(): landed = lax.all_to_all(outgoing, 'tile', 0, 0, tiled=True)  5.21 us
    all_to_all x1, starting transfers between devices, local(): landed = lax.all_to_all(outgoing, 'tile', 0, 0, tiled=True)  4.45 us
    all_to_all x1, waiting for transfers between devices, local(): arrived = lax.all_to_all(packed, 'tile', 0, 0, tiled=True)  3.83 us
    pallas_call x1, Pallas kernels, local(): pl.pallas_call(pack_body, out_shape=(jax.ShapeDtypeStruct((owners, PAIR,...  2.17 us
  transfers between devices with their start and end apart: 9, of which 7 were waited for; matrix products, arithmetic and copies ran while one was open for 1% of the time, Pallas kernels for 0%

profile of v7, /device:TPU:1, one launch (start us, length us, event | category | flops | bytes accessed | tf_op | source)
XLA Modules:
  0.0 56.2 jit_solution(6763257654485587755)
XLA Ops:
  0.0 2.2 %shard_map.100 = (bf16[32,40,128]{2,1,0:T(8,128)(2,1)}, bf16[160,128]{1,0:T(8,128)(2,1)}, bf16[160,128]{1,0:T(8,128)(2,1)}, f32[5,4,128]{2,1,0:T(4,128)}, f32[5,4,128]{2,1,0:T(4,128)}) custom-call(s32[32]{0:T(128)} %bitcast.10, f32[5,32,4,128]{3,2,1,0:T(4,128)} %refs_1_.3), custom_call_target="tpu_custom_call" | custom-call | tf_op jit(solution)/shard_map/pallas_call | solution.py:465
  2.2 9.4 %all-to-all-start = ((bf16[32,40,128]{2,1,0:T(8,128)(2,1)}), bf16[32,40,128]{2,1,0:T(8,128)(2,1)S(1)}, u32[]{:S(2)}, u32[]{:S(2)}) async-start(bf16[32,40,128]{2,1,0:T(8,128)(2,1)} %get-tuple-element.17), calls=%async_computation | async-start | bytes 655360 | tf_op jit(solution)/shard_map/all_to_all | solution.py:489
  11.6 1.7 %collective-permute-start = (f32[5,4,128]{2,1,0:T(4,128)}, f32[5,4,128]{2,1,0:T(4,128)S(1)}, u32[]{:S(2)}, u32[]{:S(2)}) collective-permute-start(f32[5,4,128]{2,1,0:T(4,128)} %get-tuple-element.18), channel_id=1, source_target_pairs={{0,1},{1,2},{2,3},{3,4},{4,5},{5,6},{6,7},{7,8},{8,9},{9,10},{10,1... | collective-permute-start | bytes 30728 | tf_op jit(solution)/shard_map/ppermute | solution.py:487
  13.3 0.0 collective-permute-start.1
  13.3 0.7 %convert_element_type.14 = f32[1,1024]{1,0:T(1,128)S(1)} convert(s32[1,1024]{1,0:T(1,128)} %param.14) | non-fusion elementwise | flops 1024 | bytes 8192 | tf_op jit(solution)/shard_map/convert_element_type | solution.py:492
  14.0 0.3 collective-permute-done.refs_3_
  14.3 3.1 %collective-permute-done.1.refs_4_ = f32[5,4,128]{2,1,0:T(4,128)S(1)} collective-permute-done((f32[5,4,128]{2,1,0:T(4,128)}, f32[5,4,128]{2,1,0:T(4,128)S(1)}, u32[]{:S(2)}, u32[]{:S(2)}) %collective-permute-start.1) | collective-permute-done | bytes 10272 | tf_op jit(solution)/shard_map/ppermute | solution.py:487
  17.4 3.8 %all-to-all-done.refs_2_ = bf16[32,40,128]{2,1,0:T(8,128)(2,1)S(1)} async-done(((bf16[32,40,128]{2,1,0:T(8,128)(2,1)}), bf16[32,40,128]{2,1,0:T(8,128)(2,1)S(1)}, u32[]{:S(2)}, u32[]{:S(2)}) %all-to-all-start) | async-done | bytes 327712 | tf_op jit(solution)/shard_map/all_to_all | solution.py:489
  21.3 0.1 fusion.1
  21.3 3.0 %collective-permute-start.4 = (f32[8,128]{1,0:T(8,128)S(1)}, f32[8,128]{1,0:T(8,128)S(1)}, u32[]{:S(2)}, u32[]{:S(2)}) collective-permute-start(f32[8,128]{1,0:T(8,128)S(1)} %broadcast_in_dim.3), channel_id=1, source_target_pairs={{0,64},{32,96},{64,0},{96,32},{1,65},{33,97},{65,1},{97,33},{2,66}... | collective-permute-start | bytes 12296 | tf_op jit(solution)/shard_map/ppermute | solution.py:487
  24.3 0.8 %collective-permute-start.3 = (f32[8,128]{1,0:T(8,128)S(1)}, f32[8,128]{1,0:T(8,128)S(1)}, u32[]{:S(2)}, u32[]{:S(2)}) collective-permute-start(f32[8,128]{1,0:T(8,128)S(1)} %broadcast_in_dim.3), channel_id=1, source_target_pairs={{0,96},{32,0},{64,32},{96,64},{1,97},{33,1},{65,33},{97,65},{2,98}... | collective-permute-start | bytes 12296 | tf_op jit(solution)/shard_map/ppermute | solution.py:487
  25.1 0.7 %collective-permute-start.2 = (f32[8,128]{1,0:T(8,128)S(1)}, f32[8,128]{1,0:T(8,128)S(1)}, u32[]{:S(2)}, u32[]{:S(2)}) collective-permute-start(f32[8,128]{1,0:T(8,128)S(1)} %broadcast_in_dim.3), channel_id=1, source_target_pairs={{0,32},{32,64},{64,96},{96,0},{1,33},{33,65},{65,97},{97,1},{2,34}... | collective-permute-start | bytes 12296 | tf_op jit(solution)/shard_map/ppermute | solution.py:487
  26.4 0.0 collective-permute-done.4.refs_5_
  26.4 0.3 collective-permute-done.3.refs_4_
  26.8 2.0 %collective-permute-done.2.refs_3_ = f32[8,128]{1,0:T(8,128)S(1)} collective-permute-done((f32[8,128]{1,0:T(8,128)S(1)}, f32[8,128]{1,0:T(8,128)S(1)}, u32[]{:S(2)}, u32[]{:S(2)}) %collective-permute-start.2) | collective-permute-done | bytes 4128 | tf_op jit(solution)/shard_map/ppermute | solution.py:487
  28.8 0.0 copy-start.4
  28.8 0.0 copy-start.3
  28.8 0.0 copy-start
  28.8 0.0 copy-start.1
  28.8 0.0 copy-start.2
  28.8 11.4 %shard_map.101 = bf16[32,40,128]{2,1,0:T(8,128)(2,1)} custom-call(s32[1]{0:T(128)S(6)} %copy.11.refs_0_, f32[8,128]{1,0:T(8,128)S(1)} %bitcast.9, bf16[32,40,128]{2,1,0:T(8,128)(2,1)S(1)} %all-to-all-done.refs_2_, f32[8,128]{1,0:T(8,128)S(1)} %collective-permute-done.2.refs_3_, f32[8,128]{1,0:T(8,128)S(1)} %collective-permute-done.3.refs_4_, ...), custom_call_target="tpu_custom_call" | custom-call | tf_op jit(solution)/shard_map/pallas_call | solution.py:414
  40.2 4.5 %all-to-all-start.1 = ((bf16[32,40,128]{2,1,0:T(8,128)(2,1)}), bf16[32,40,128]{2,1,0:T(8,128)(2,1)S(1)}, u32[]{:S(2)}, u32[]{:S(2)}) async-start(bf16[32,40,128]{2,1,0:T(8,128)(2,1)} %shard_map.101), calls=%async_computation.1 | async-start | bytes 655360 | tf_op jit(solution)/shard_map/all_to_all | solution.py:514
  44.7 0.0 copy-done.4
  44.7 0.1 collective-permute-start.5
  44.8 0.0 copy-done.3
  44.8 2.7 %collective-permute-start.6 = (bf16[160,128]{1,0:T(8,128)(2,1)S(1)}, bf16[160,128]{1,0:T(8,128)(2,1)S(1)}, u32[]{:S(2)}, u32[]{:S(2)}) collective-permute-start(bf16[160,128]{1,0:T(8,128)(2,1)S(1)} %copy-done.3), channel_id=1, source_target_pairs={{0,96},{32,0},{64,32},{96,64},{1,97},{33,1},{65,33},{97,65},{2,98}... | collective-permute-start | bytes 122888 | tf_op jit(solution)/shard_map/ppermute | solution.py:487
  47.5 1.7 %collective-permute-done.5.refs_5_ = bf16[160,128]{1,0:T(8,128)(2,1)S(1)} collective-permute-done((bf16[160,128]{1,0:T(8,128)(2,1)S(1)}, bf16[160,128]{1,0:T(8,128)(2,1)S(1)}, u32[]{:S(2)}, u32[]{:S(2)}) %collective-permute-start.5) | collective-permute-done | bytes 40992 | tf_op jit(solution)/shard_map/ppermute | solution.py:487
  49.1 0.0 collective-permute-done.6.refs_6_
  49.1 5.2 %all-to-all-done.1.refs_7_ = bf16[32,40,128]{2,1,0:T(8,128)(2,1)S(1)} async-done(((bf16[32,40,128]{2,1,0:T(8,128)(2,1)}), bf16[32,40,128]{2,1,0:T(8,128)(2,1)S(1)}, u32[]{:S(2)}, u32[]{:S(2)}) %all-to-all-start.1) | async-done | bytes 327712 | tf_op jit(solution)/shard_map/all_to_all | solution.py:514
  54.3 0.0 copy-done
  54.3 0.0 copy-done.1
  54.4 0.0 copy-done.2
  54.4 1.8 %shard_map.102 = f32[5,32,4,128]{3,2,1,0:T(4,128)} custom-call(s32[32]{0:T(128)S(1)} %bitcast.11, f32[5,32,4,128]{3,2,1,0:T(4,128)S(1)} %copy-done, f32[32,4,128]{2,1,0:T(4,128)S(1)} %copy-done.1, f32[5,4,128]{2,1,0:T(4,128)S(1)} %collective-permute-done.refs_3_, f32[5,4,128]{2,1,0:T(4,128)S(1)} %collective-permute-done.1.refs_4_, ...), custom_call_target="tpu_custom_call" | custom-call | tf_op jit(solution)/shard_map/pallas_call | solution.py:521
  (1 shorter events, 0.0 us)
Async XLA Ops:
  2.2 19.1 %all-to-all-start = ((bf16[32,40,128]{2,1,0:T(8,128)(2,1)}), bf16[32,40,128]{2,1,0:T(8,128)(2,1)S(1)}, u32[]{:S(2)}, u32[]{:S(2)}) async-start(bf16[32,40,128]{2,1,0:T(8,128)(2,1)} %get-tuple-element.17), calls=%async_computation | async-start | bytes 655360 | tf_op jit(solution)/shard_map/all_to_all | solution.py:489
  11.6 2.7 %collective-permute-start = (f32[5,4,128]{2,1,0:T(4,128)}, f32[5,4,128]{2,1,0:T(4,128)S(1)}, u32[]{:S(2)}, u32[]{:S(2)}) collective-permute-start(f32[5,4,128]{2,1,0:T(4,128)} %get-tuple-element.18), channel_id=1, source_target_pairs={{0,1},{1,2},{2,3},{3,4},{4,5},{5,6},{6,7},{7,8},{8,9},{9,10},{10,1... | collective-permute-start | bytes 30728 | tf_op jit(solution)/shard_map/ppermute | solution.py:487
  13.3 4.1 %collective-permute-start.1 = (f32[5,4,128]{2,1,0:T(4,128)}, f32[5,4,128]{2,1,0:T(4,128)S(1)}, u32[]{:S(2)}, u32[]{:S(2)}) collective-permute-start(f32[5,4,128]{2,1,0:T(4,128)} %get-tuple-element.19), channel_id=1, source_target_pairs={{0,31},{1,0},{2,1},{3,2},{4,3},{5,4},{6,5},{7,6},{8,7},{9,8},{10,9... | collective-permute-start | bytes 30728 | tf_op jit(solution)/shard_map/ppermute | solution.py:487
  21.3 5.1 %collective-permute-start.4 = (f32[8,128]{1,0:T(8,128)S(1)}, f32[8,128]{1,0:T(8,128)S(1)}, u32[]{:S(2)}, u32[]{:S(2)}) collective-permute-start(f32[8,128]{1,0:T(8,128)S(1)} %broadcast_in_dim.3), channel_id=1, source_target_pairs={{0,64},{32,96},{64,0},{96,32},{1,65},{33,97},{65,1},{97,33},{2,66}... | collective-permute-start | bytes 12296 | tf_op jit(solution)/shard_map/ppermute | solution.py:487
  24.3 2.5 %collective-permute-start.3 = (f32[8,128]{1,0:T(8,128)S(1)}, f32[8,128]{1,0:T(8,128)S(1)}, u32[]{:S(2)}, u32[]{:S(2)}) collective-permute-start(f32[8,128]{1,0:T(8,128)S(1)} %broadcast_in_dim.3), channel_id=1, source_target_pairs={{0,96},{32,0},{64,32},{96,64},{1,97},{33,1},{65,33},{97,65},{2,98}... | collective-permute-start | bytes 12296 | tf_op jit(solution)/shard_map/ppermute | solution.py:487
  25.1 3.7 %collective-permute-start.2 = (f32[8,128]{1,0:T(8,128)S(1)}, f32[8,128]{1,0:T(8,128)S(1)}, u32[]{:S(2)}, u32[]{:S(2)}) collective-permute-start(f32[8,128]{1,0:T(8,128)S(1)} %broadcast_in_dim.3), channel_id=1, source_target_pairs={{0,32},{32,64},{64,96},{96,0},{1,33},{33,65},{65,97},{97,1},{2,34}... | collective-permute-start | bytes 12296 | tf_op jit(solution)/shard_map/ppermute | solution.py:487
  28.8 15.9 %copy-start.4 = (bf16[160,128]{1,0:T(8,128)(2,1)S(1)}, bf16[160,128]{1,0:T(8,128)(2,1)}, u32[]{:S(2)}) copy-start(bf16[160,128]{1,0:T(8,128)(2,1)} %get-tuple-element.26) | copy-start | bytes 122884
  28.8 16.0 %copy-start.3 = (bf16[160,128]{1,0:T(8,128)(2,1)S(1)}, bf16[160,128]{1,0:T(8,128)(2,1)}, u32[]{:S(2)}) copy-start(bf16[160,128]{1,0:T(8,128)(2,1)} %get-tuple-element.27) | copy-start | bytes 122884
  28.8 25.6 %copy-start = (f32[5,32,4,128]{3,2,1,0:T(4,128)S(1)}, f32[5,32,4,128]{3,2,1,0:T(4,128)}, u32[]{:S(2)}) copy-start(f32[5,32,4,128]{3,2,1,0:T(4,128)} %refs_1_.3) | copy-start | bytes 983044
  28.8 25.6 %copy-start.1 = (f32[32,4,128]{2,1,0:T(4,128)S(1)}, f32[32,4,128]{2,1,0:T(4,128)}, u32[]{:S(2)}) copy-start(f32[32,4,128]{2,1,0:T(4,128)} %refs_2_.1) | copy-start | bytes 196612
  28.8 25.6 %copy-start.2 = (s32[1,32,1]{1,2,0:T(1,128)S(1)}, s32[1,32,1]{1,2,0:T(1,128)}, u32[]{:S(2)}) copy-start(s32[1,32,1]{1,2,0:T(1,128)} %param.12) | copy-start | bytes 388
  40.2 14.1 %all-to-all-start.1 = ((bf16[32,40,128]{2,1,0:T(8,128)(2,1)}), bf16[32,40,128]{2,1,0:T(8,128)(2,1)S(1)}, u32[]{:S(2)}, u32[]{:S(2)}) async-start(bf16[32,40,128]{2,1,0:T(8,128)(2,1)} %shard_map.101), calls=%async_computation.1 | async-start | bytes 655360 | tf_op jit(solution)/shard_map/all_to_all | solution.py:514
  44.7 4.4 %collective-permute-start.5 = (bf16[160,128]{1,0:T(8,128)(2,1)S(1)}, bf16[160,128]{1,0:T(8,128)(2,1)S(1)}, u32[]{:S(2)}, u32[]{:S(2)}) collective-permute-start(bf16[160,128]{1,0:T(8,128)(2,1)S(1)} %copy-done.4), channel_id=1, source_target_pairs={{0,32},{32,64},{64,96},{96,0},{1,33},{33,65},{65,97},{97,1},{2,34}... | collective-permute-start | bytes 122888 | tf_op jit(solution)/shard_map/ppermute | solution.py:487
  44.8 4.3 %collective-permute-start.6 = (bf16[160,128]{1,0:T(8,128)(2,1)S(1)}, bf16[160,128]{1,0:T(8,128)(2,1)S(1)}, u32[]{:S(2)}, u32[]{:S(2)}) collective-permute-start(bf16[160,128]{1,0:T(8,128)(2,1)S(1)} %copy-done.3), channel_id=1, source_target_pairs={{0,96},{32,0},{64,32},{96,64},{1,97},{33,1},{65,33},{97,65},{2,98}... | collective-permute-start | bytes 122888 | tf_op jit(solution)/shard_map/ppermute | solution.py:487
